TPU v7x, 512 devices: a whole 4x8x8 slice. The times are simulated.
512 devices in a mesh: dp: 8 (over y_lo, core), expert: 64 (over y_hi, x, z).
Axes of the slice: x: 4, y: 8 (y_hi: 2, y_lo: 4; y = y_hi * 4 + y_lo), z: 8, core: 2. Of those that a mesh axis runs over, the one named last changes fastest.
Arguments:
- tokens: bfloat16 [512, 192, 1280], P(('dp', 'expert')), may hold values from -64 to 64
- grad_out: bfloat16 [512, 192, 1280], P(('dp', 'expert')), may hold values from -6 to 6
- router: bfloat16 [1280, 64], replicated, may hold values from -0.1118034 to 0.1118034
- w_in: bfloat16 [64, 2560, 1280], P('expert', 'dp'), may hold values from -0.15625 to 0.15625
- w_out: bfloat16 [64, 2560, 1280], P('expert', 'dp'), may hold values from -0.125 to 0.125
Outputs:
- d_tokens: bfloat16 [512, 192, 1280], P(('dp', 'expert'))
- d_router: bfloat16 [1280, 64], replicated
- d_w_in: bfloat16 [64, 2560, 1280], P('expert', 'dp')
- d_w_out: bfloat16 [64, 2560, 1280], P('expert', 'dp')
All inputs are finite; a program needn't handle non-finite values.
Results may differ from a plain program's by a relative error of at most 0.019.
Values may be sent and summed in bfloat16 or wider, within the bound.
No kernel may reach another device: no remote copies, remote signals or barrier semaphores. Data moves between devices by JAX's collectives and lax.ppermute only.
A program may use at most 64 MiB of HBM per device.

v0:
```python
import jax
import jax.numpy as jnp
from jax import lax
from jax.sharding import PartitionSpec as P


def gelu_back(preact, upstream):
    return jax.vjp(jax.nn.gelu, preact)[1](upstream)[0]


def local(tokens, grad_out, router, w_in, w_out):
    logits = jnp.einsum("imd,ds->ims", tokens, router, preferred_element_type=jnp.float32)
    dispatch = jax.nn.softmax(logits, axis=1)
    combine = jax.nn.softmax(logits, axis=2)
    dispatch_cast = dispatch.astype(jnp.bfloat16)
    combine_cast = combine.astype(jnp.bfloat16)
    own_in = jnp.einsum(
        "ims,imd->isd", dispatch_cast, tokens, preferred_element_type=jnp.float32
    ).astype(jnp.bfloat16)
    own_grad = jnp.einsum(
        "ims,imd->isd", combine_cast, grad_out, preferred_element_type=jnp.float32
    ).astype(jnp.bfloat16)
    moved_in, moved_grad = (
        lax.all_to_all(own_in, "expert", split_axis=1, concat_axis=0, tiled=True),
        lax.all_to_all(own_grad, "expert", split_axis=1, concat_axis=0, tiled=True),
    )
    slot_in, slot_grad = (
        lax.all_gather(moved_in, "dp", axis=0, tiled=True),
        lax.all_gather(moved_grad, "dp", axis=0, tiled=True),
    )
    preact = jnp.einsum("ied,ehd->ieh", slot_in, w_in, preferred_element_type=jnp.float32)
    hidden = jax.nn.gelu(preact).astype(jnp.bfloat16)
    hidden_grad = jnp.einsum("ied,ehd->ieh", slot_grad, w_out, preferred_element_type=jnp.float32)
    preact_grad = gelu_back(preact, hidden_grad).astype(jnp.bfloat16)
    d_w_out = jnp.einsum(
        "ieh,ied->ehd", hidden, slot_grad, preferred_element_type=jnp.float32
    ).astype(jnp.bfloat16)
    d_w_in = jnp.einsum(
        "ieh,ied->ehd", preact_grad, slot_in, preferred_element_type=jnp.float32
    ).astype(jnp.bfloat16)
    out_partial = jnp.einsum("ieh,ehd->ied", hidden, w_out, preferred_element_type=jnp.float32)
    input_partial = jnp.einsum(
        "ieh,ehd->ied", preact_grad, w_in, preferred_element_type=jnp.float32
    )
    summed_out, summed_back = (
        lax.psum_scatter(
            out_partial.astype(jnp.bfloat16), "dp", scatter_dimension=0, tiled=True
        ).astype(jnp.float32),
        lax.psum_scatter(
            input_partial.astype(jnp.bfloat16), "dp", scatter_dimension=0, tiled=True
        ).astype(jnp.float32),
    )
    slot_out, slot_in_grad = (
        lax.all_to_all(
            summed_out.astype(jnp.bfloat16), "expert", split_axis=0, concat_axis=1, tiled=True
        ),
        lax.all_to_all(
            summed_back.astype(jnp.bfloat16), "expert", split_axis=0, concat_axis=1, tiled=True
        ),
    )
    slot_stat = jnp.einsum("isd,isd->is", own_in, slot_in_grad, preferred_element_type=jnp.float32)
    combine_grad = jnp.einsum(
        "imd,isd->ims", grad_out, slot_out, preferred_element_type=jnp.float32
    )
    combine_logit = combine * (
        combine_grad - jnp.sum(combine * combine_grad, axis=2, keepdims=True)
    )
    dispatch_grad = jnp.einsum(
        "imd,isd->ims", tokens, slot_in_grad, preferred_element_type=jnp.float32
    )
    logit_grad = (dispatch * (dispatch_grad - slot_stat[:, None, :]) + combine_logit).astype(
        jnp.bfloat16
    )
    from_logits = jnp.einsum("ims,ds->imd", logit_grad, router, preferred_element_type=jnp.float32)
    from_slots = jnp.einsum(
        "ims,isd->imd", dispatch_cast, slot_in_grad, preferred_element_type=jnp.float32
    )
    d_tokens = (from_logits + from_slots).astype(jnp.bfloat16)
    router_term = jnp.einsum("imd,ims->ds", tokens, logit_grad, preferred_element_type=jnp.float32)
    d_router = lax.psum(router_term, ("dp", "expert")).astype(jnp.bfloat16)
    return (d_tokens, d_router, d_w_in, d_w_out)


def solution(mesh):
    placed = (
        P(("dp", "expert"), None, None),
        P(("dp", "expert"), None, None),
        P(),
        P("expert", "dp", None),
        P("expert", "dp", None),
    )
    return jax.shard_map(
        local,
        mesh=mesh,
        in_specs=placed,
        out_specs=(
            P(("dp", "expert"), None, None),
            P(),
            P("expert", "dp", None),
            P("expert", "dp", None),
        ),
        check_vma=False,
    )
```

profile of v0, /device:TPU:1, one launch (start us, length us, event | category | flops | bytes accessed | tf_op | source)
XLA Modules:
  0.0 345.8 jit_solution(10371675420042226882)
XLA Ops:
  7.2 1.5 fusion.69
  9.0 1.3 convolution_convert_fusion.4
  10.3 0.3 copy.43
  10.5 0.6 broadcast.68
  11.1 1.6 reduce.12
  12.8 33.2 %all_to_all.42 = bf16[64,2,640]{2,1,0:T(2,128)(2,1)S(1)} all-to-all(bf16[64,2,640]{2,1,0:T(2,128)(2,1)S(1)} %reshape.161), channel_id=1, replica_groups=mesh['dp'=8,'expert'=64] {'expert'}, dimensions={0} | all-to-all | bytes 327680 | tf_op jit(solution)/shard_map/all_to_all | solution.py:24
  46.1 0.7 copy.16
  47.4 1.6 reduce.14
  49.1 20.9 %all_to_all.43 = bf16[64,2,640]{2,1,0:T(2,128)(2,1)S(1)} all-to-all(bf16[64,2,640]{2,1,0:T(2,128)(2,1)S(1)} %reshape.165), channel_id=1, replica_groups=mesh['dp'=8,'expert'=64] {'expert'}, dimensions={0} | all-to-all | bytes 327680 | tf_op jit(solution)/shard_map/all_to_all | solution.py:25
  70.0 0.7 copy.14
  70.8 8.0 %all-gather.7.cloned.1.call-done = bf16[1,512,1280]{2,1,0:T(8,128)(2,1)} async-done(((bf16[1,64,1280]{2,1,0:T(8,128)(2,1)}), bf16[1,512,1280]{2,1,0:T(8,128)(2,1)}) %all-gather.7.cloned.1.call-update) | async-done | bytes 1310736 | tf_op jit(solution)/shard_map/all_gather | solution.py:28
  78.8 1.9 fusion.16
  80.8 2.0 fusion.1
  82.9 38.7 %all-gather.5.cloned.1.call-done = bf16[1,512,1280]{2,1,0:T(8,128)(2,1)} async-done(((bf16[1,64,1280]{2,1,0:T(8,128)(2,1)}), bf16[1,512,1280]{2,1,0:T(8,128)(2,1)}) %all-gather.5.cloned.1.call-update) | async-done | bytes 1310736 | tf_op jit(solution)/shard_map/all_gather | solution.py:29
  121.7 2.2 fusion.38
  123.9 2.0 fusion
  125.9 38.3 %reduce-scatter.5.cloned.1.call-done = bf16[64,1,1280]{2,0,1:T(8,128)(2,1)} async-done(((bf16[512,1,1280]{2,0,1:T(8,128)(2,1)}), bf16[64,1,1280]{2,0,1:T(8,128)(2,1)}) %reduce-scatter.5.cloned.1.call-update) | async-done | bytes 163856 | tf_op jit(solution)/shard_map/reduce_scatter | solution.py:46
  164.2 1.7 reduce.13
  165.9 0.7 reshape.163
  166.6 14.3 %all-to-all-start.3 = ((bf16[64,2,640]{2,1,0:T(2,128)(2,1)}), bf16[64,2,640]{2,1,0:T(2,128)(2,1)S(1)}, u32[]{:S(2)}, u32[]{:S(2)}) async-start(bf16[64,2,640]{2,1,0:T(2,128)(2,1)} %reshape.163), calls=%async_computation.5 | async-start | bytes 327680 | tf_op jit(solution)/shard_map/all_to_all | solution.py:54
  180.9 3.3 fusion.3
  184.2 24.5 %reduce-scatter.3.cloned.1.call-done = bf16[64,1,1280]{2,0,1:T(8,128)(2,1)} async-done(((bf16[512,1,1280]{2,0,1:T(8,128)(2,1)}), bf16[64,1,1280]{2,0,1:T(8,128)(2,1)}) %reduce-scatter.3.cloned.1.call-update) | async-done | bytes 163856 | tf_op jit(solution)/shard_map/reduce_scatter | solution.py:49
  208.8 1.7 reduce.15
  210.4 0.7 reshape.167
  211.1 13.0 %all-to-all-start.2 = ((bf16[64,2,640]{2,1,0:T(2,128)(2,1)}), bf16[64,2,640]{2,1,0:T(2,128)(2,1)S(1)}, u32[]{:S(2)}, u32[]{:S(2)}) async-start(bf16[64,2,640]{2,1,0:T(2,128)(2,1)} %reshape.167), calls=%async_computation.3 | async-start | bytes 327680 | tf_op jit(solution)/shard_map/all_to_all | solution.py:57
  224.1 1.5 fusion.2
  225.8 0.3 multiply_reduce_fusion
  226.1 11.5 %all-to-all-done.2 = bf16[64,2,640]{2,1,0:T(2,128)(2,1)S(1)} async-done(((bf16[64,2,640]{2,1,0:T(2,128)(2,1)}), bf16[64,2,640]{2,1,0:T(2,128)(2,1)S(1)}, u32[]{:S(2)}, u32[]{:S(2)}) %all-to-all-start.2) | async-done | bytes 163872 | tf_op jit(solution)/shard_map/all_to_all | solution.py:57
  237.9 0.3 fusion.22
  238.7 0.3 fusion.70
  239.0 99.1 %all-reduce.1 = bf16[1280,64]{0,1:T(8,128)(2,1)} all-reduce(f32[1280,64]{0,1:T(8,128)S(1)} %convolution_bitcast_fusion), channel_id=1, replica_groups=mesh['dp'=8,'expert'=64] {'dp','expert'}, use_global_device_ids=true, to_apply=%region_7.0 | all-reduce | flops 81920 | bytes 491520 | tf_op jit(solution)/shard_map/psum | solution.py:80
  338.1 1.2 fusion.5
  (34 shorter events, 2.1 us)
Async XLA Ops:
  7.2 73.6 %copy-start = (bf16[1,320,1280]{2,1,0:T(8,128)(2,1)S(1)}, bf16[1,320,1280]{2,1,0:T(8,128)(2,1)}, u32[]{:S(2)}) copy-start(bf16[1,320,1280]{2,1,0:T(8,128)(2,1)} %param.9) | copy-start | bytes 2457604
  7.2 71.7 %all-gather.7.cloned.1.call-start = ((), (), s32[]{:S(2)}) async-start(), calls=%async_computation.9 | async-start | bytes 1474560 | tf_op jit(solution)/shard_map/all_gather | solution.py:28
  10.3 36.6 %copy-start.4 = (bf16[1,192,1280]{2,1,0:T(8,128)(2,1)S(1)}, bf16[1,192,1280]{2,1,0:T(8,128)(2,1)}, u32[]{:S(2)}) copy-start(bf16[1,192,1280]{2,1,0:T(8,128)(2,1)} %param.6) | copy-start | bytes 1474564
  46.8 74.8 %all-gather.5.cloned.1.call-start = ((), (), s32[]{:S(2)}) async-start(), calls=%async_computation.8 | async-start | bytes 1474560 | tf_op jit(solution)/shard_map/all_gather | solution.py:29
  47.1 31.7 %copy-start.5 = (bf16[1,320,1280]{2,1,0:T(8,128)(2,1)S(1)}, bf16[1,320,1280]{2,1,0:T(8,128)(2,1)}, u32[]{:S(2)}) copy-start(bf16[1,320,1280]{2,1,0:T(8,128)(2,1)} %param.8) | copy-start | bytes 2457604
  70.8 93.5 %reduce-scatter.5.cloned.1.call-start = ((), (), s32[]{:S(2)}) async-start(), calls=%async_computation.7 | async-start | bytes 1474560 | tf_op jit(solution)/shard_map/reduce_scatter | solution.py:46
  80.8 40.9 %copy-start.6 = (f32[512,1,320]{0,2,1:T(8,128)}, f32[512,1,320]{0,2,1:T(8,128)S(1)}, u32[]{:S(2)}) copy-start(f32[512,1,320]{0,2,1:T(8,128)S(1)} %fusion.16) | copy-start | bytes 1966084
  82.9 125.9 %reduce-scatter.3.cloned.1.call-start = ((), (), s32[]{:S(2)}) async-start(), calls=%async_computation.6 | async-start | bytes 1474560 | tf_op jit(solution)/shard_map/reduce_scatter | solution.py:49
  166.6 44.6 %all-to-all-start.3 = ((bf16[64,2,640]{2,1,0:T(2,128)(2,1)}), bf16[64,2,640]{2,1,0:T(2,128)(2,1)S(1)}, u32[]{:S(2)}, u32[]{:S(2)}) async-start(bf16[64,2,640]{2,1,0:T(2,128)(2,1)} %reshape.163), calls=%async_computation.5 | async-start | bytes 327680 | tf_op jit(solution)/shard_map/all_to_all | solution.py:54
  180.9 43.2 %copy-start.2 = (bf16[1,512,1280]{2,1,0:T(8,128)(2,1)S(1)}, bf16[1,512,1280]{2,1,0:T(8,128)(2,1)}, u32[]{:S(2)}) copy-start(bf16[1,512,1280]{2,1,0:T(8,128)(2,1)} %all-gather.7.cloned.1.call-done) | copy-start | bytes 3932164
  211.1 26.5 %all-to-all-start.2 = ((bf16[64,2,640]{2,1,0:T(2,128)(2,1)}), bf16[64,2,640]{2,1,0:T(2,128)(2,1)S(1)}, u32[]{:S(2)}, u32[]{:S(2)}) async-start(bf16[64,2,640]{2,1,0:T(2,128)(2,1)} %reshape.167), calls=%async_computation.3 | async-start | bytes 327680 | tf_op jit(solution)/shard_map/all_to_all | solution.py:57
  225.6 12.3 %copy-start.1 = (bf16[1,192,1280]{2,1,0:T(8,128)(2,1)S(1)}, bf16[1,192,1280]{2,1,0:T(8,128)(2,1)}, u32[]{:S(2)}) copy-start(bf16[1,192,1280]{2,1,0:T(8,128)(2,1)} %param.5) | copy-start | bytes 1474564
  237.7 0.9 copy-start.3
Sparse Core Ops, SparseCore 0:
  46.9 31.8 all-gather.6
  81.5 40.1 all-gather.4
  124.5 39.6 reduce-scatter.4
  166.9 41.8 reduce-scatter.2
where the time goes:
time: 346 us
  blocking collectives  153 us (44%)
  waiting for transfers between devices  121 us (35%)
  starting transfers between devices  27.5 us (8%)
  matrix products  18.3 us (5%)
  between operations  14 us (4%)
  other arithmetic  6.91 us (2%)
  local copies, waits for them, and re-layouts  4.74 us (1%)
    psum x1, blocking collectives, local(): d_router = lax.psum(router_term, ('dp', 'expert')).astype(jnp.bfloat16)  99.1 us
    all_gather x1, waiting for transfers between devices, local(): lax.all_gather(moved_grad, 'dp', axis=0, tiled=True)  38.7 us
    reduce_scatter x1, waiting for transfers between devices, local(): lax.psum_scatter(out_partial.astype(jnp.bfloat16), 'dp', scatter_dimensio...  38.3 us
    all_to_all x1, blocking collectives, local(): lax.all_to_all(own_in, 'expert', split_axis=1, concat_axis=0, tiled=True)  33.2 us
    reduce_scatter x1, waiting for transfers between devices, local(): lax.psum_scatter(input_partial.astype(jnp.bfloat16), 'dp', scatter_dimens...  24.5 us
    all_to_all x1, blocking collectives, local(): lax.all_to_all(own_grad, 'expert', split_axis=1, concat_axis=0, tiled=True)  20.9 us
    all_to_all x1, starting transfers between devices, local(): lax.all_to_all(summed_out.astype(jnp.bfloat16), 'expert', split_axis=0, c...  14.3 us
    all_to_all x1, starting transfers between devices, local(): lax.all_to_all(summed_back.astype(jnp.bfloat16), 'expert', split_axis=0,...  13 us
  transfers between devices with their start and end apart: 6, of which 5 were waited for; matrix products, arithmetic and copies ran while one was open for 6% of the time, Pallas kernels for 0%

commit v1 on v0

v1 whole, which is shorter than its diff:
```python
import jax
import jax.numpy as jnp
from jax import lax
from jax.sharding import Mesh, PartitionSpec as P

SWAP = [(0, 1), (1, 0)]
DP = ("y_lo", "core")
EXPERT = ("y_hi", "x", "z")
PLANE = ("x", "z")
COLUMN = ("y_lo", "y_hi")
RING = ("y_lo", "x")
REST = ("core", "y_hi", "z")
BF = jnp.bfloat16
F32 = jnp.float32


def gelu_back(preact, upstream):
    return jax.vjp(jax.nn.gelu, preact)[1](upstream)[0]


def exchange(blocks, axes):
    return lax.all_to_all(blocks, axes, split_axis=0, concat_axis=0, tiled=True)


def swap(value):
    return lax.ppermute(value, "core", SWAP)


def dot(spec, left, right):
    return jnp.einsum(spec, left, right, preferred_element_type=F32)


def local(tokens, grad_out, router, w_in, w_out):
    tokens, grad_out, w_in, w_out = tokens[0], grad_out[0], w_in[0], w_out[0]
    first = lax.axis_index("core") == 0
    weight_kept = jnp.where(first, w_in, w_out)
    weight_got = swap(jnp.where(first, w_out, w_in))
    weight = jnp.concatenate(
        [jnp.where(first, weight_kept, weight_got), jnp.where(first, weight_got, weight_kept)]
    )
    router = router.reshape(1280, 2, 32).swapaxes(1, 2).reshape(1280, 64)
    logits = dot("md,ds->ms", tokens, router)
    dispatch = jax.nn.softmax(logits, axis=0)
    combine = jax.nn.softmax(logits, axis=1)
    dispatch_cast = dispatch.astype(BF)
    own_in = dot("ms,md->sd", dispatch_cast, tokens).astype(BF)
    own_grad = dot("ms,md->sd", combine.astype(BF), grad_out).astype(BF)
    got = swap(jnp.where(first, own_grad, own_in))
    pair = jnp.stack(
        [jnp.where(first, own_in, got), jnp.where(first, got, own_grad)], axis=1
    )
    blocks = pair.reshape(32, 4, 1280)
    moved = exchange(blocks, PLANE).reshape(32, 2, 2, 1280)
    moved = moved.swapaxes(0, 1).reshape(1, 2, 64, 1280)
    rows = exchange(
        jnp.broadcast_to(moved, (4, 2, 64, 1280)).reshape(8, 64, 1280), COLUMN
    ).reshape(512, 1280)
    act = dot("id,hd->ih", rows, weight)
    other = swap(jnp.where(first, jax.nn.gelu(act), act).astype(BF))
    hid = jnp.where(first, gelu_back(act, other.astype(F32)).astype(BF), other)
    partial = dot("ih,hd->id", hid, weight).astype(BF)
    d_weight = dot("ih,id->hd", hid, rows).astype(BF)
    parts = exchange(partial.reshape(8, 64, 1280), COLUMN).reshape(4, 2, 32, 2, 1280)
    summed = jnp.sum(parts.astype(F32), axis=0).astype(BF)
    back = exchange(
        summed.swapaxes(0, 1).reshape(32, 4, 1280), PLANE
    ).reshape(64, 2, 1280)
    kept = jnp.where(first, back[:, 0], back[:, 1])
    got = swap(jnp.where(first, back[:, 1], back[:, 0]))
    slot_in_grad = jnp.where(first, kept, got)
    slot_out = jnp.where(first, got, kept)
    slot_stat = jnp.sum(own_in.astype(F32) * slot_in_grad.astype(F32), axis=1)
    combine_grad = dot("md,sd->ms", grad_out, slot_out)
    combine_logit = combine * (
        combine_grad - jnp.sum(combine * combine_grad, axis=1, keepdims=True)
    )
    dispatch_grad = dot("md,sd->ms", tokens, slot_in_grad)
    logit_grad = (dispatch * (dispatch_grad - slot_stat[None]) + combine_logit).astype(BF)
    d_tokens = (
        dot("ms,ds->md", logit_grad, router) + dot("ms,sd->md", dispatch_cast, slot_in_grad)
    ).astype(BF)
    term = dot("ms,md->sd", logit_grad, tokens)
    term = jnp.sum(exchange(term.reshape(16, 4, 1280), RING), axis=0)
    term = jnp.broadcast_to(term.astype(BF)[None], (32, 4, 1280))
    term = jnp.sum(exchange(term, REST).astype(F32), axis=0).astype(BF)
    term = exchange(jnp.broadcast_to(term[None], (16, 4, 1280)), RING)
    d_router = term.reshape(32, 2, 1280).transpose(2, 1, 0).reshape(1280, 64)
    d_kept = jnp.where(first, d_weight[:320], d_weight[320:])
    d_got = swap(jnp.where(first, d_weight[320:], d_weight[:320]))
    d_w_in = jnp.where(first, d_kept, d_got)
    d_w_out = jnp.where(first, d_got, d_kept)
    return (d_tokens[None], d_router, d_w_in[None], d_w_out[None])


def solution(mesh):
    fine = Mesh(
        mesh.devices.reshape(4, 2, 2, 4, 8), ("y_lo", "core", "y_hi", "x", "z")
    )
    image = P(DP + EXPERT, None, None)
    unit = P(EXPERT, DP, None)
    return jax.shard_map(
        local,
        mesh=fine,
        in_specs=(image, image, P(), unit, unit),
        out_specs=(image, P(), unit, unit),
        check_vma=False,
    )
```

time: 346 us -> 205 us (0.59)
  blocking collectives: 153 us -> 68.8 us
  waiting for transfers between devices: 121 us -> 49.8 us
  starting transfers between devices: 27.5 us -> 57.6 us
  between operations: 14 us -> 0.96 us
  matrix products: 18.3 us -> 11.7 us
    psum x1 -> x0, blocking collectives: 99.1 us -> none  [local(): d_router = lax.psum(router_term, ('dp', 'expert')).astype(jnp.bfloat16)]
    reduce_scatter x2 -> x0, waiting for transfers between devices: 62.9 us -> none  [the longest x1 38.3 us: local(): lax.psum_scatter(out_partial.astype(jnp.bfloat16), 'dp', scatter_dimensio...]
    all_gather x2 -> x0, waiting for transfers between devices: 46.8 us -> none  [the longest x1 38.7 us: local(): lax.all_gather(moved_grad, 'dp', axis=0, tiled=True)]
    all_to_all x2 -> x4, waiting for transfers between devices: 11.5 us -> 45.1 us  [exchange(): return lax.all_to_all(blocks, axes, split_axis=0, concat_axis=0, tiled=True)]
    ppermute x0 -> x5, starting transfers between devices: none -> 29.3 us  [swap(): return lax.ppermute(value, 'core', SWAP)]
    all_to_all x2 -> x3, blocking collectives: 54 us -> 68.8 us  [exchange(): return lax.all_to_all(blocks, axes, split_axis=0, concat_axis=0, tiled=True)]
    dot_general x14 -> x11, matrix products: 18.3 us -> 11.7 us  [dot(): return jnp.einsum(spec, left, right, preferred_element_type=F32)]
    ppermute x0 -> x5, waiting for transfers between devices: none -> 4.65 us  [swap(): return lax.ppermute(value, 'core', SWAP)]
  transfers between devices with their start and end apart: 6 -> 9, of which waited for: 5 -> 7; matrix products, arithmetic and copies ran while one was open for 6% -> 6% of each run, Pallas kernels for 0% -> 0%
where the time goes in v1:
time: 205 us; the launch traced here: 204 us
  blocking collectives  68.8 us (34%)
  starting transfers between devices  57.6 us (28%)
  waiting for transfers between devices  49.8 us (24%)
  matrix products  11.7 us (6%)
  local copies, waits for them, and re-layouts  7.94 us (4%)
  other arithmetic  7.11 us (3%)
    all_to_all x3, blocking collectives, exchange(): return lax.all_to_all(blocks, axes, split_axis=0, concat_axis=0, tiled=True)  68.8 us
    all_to_all x4, waiting for transfers between devices, exchange(): return lax.all_to_all(blocks, axes, split_axis=0, concat_axis=0, tiled=True)  45.1 us
    ppermute x5, starting transfers between devices, swap(): return lax.ppermute(value, 'core', SWAP)  29.3 us
    all_to_all x4, starting transfers between devices, exchange(): return lax.all_to_all(blocks, axes, split_axis=0, concat_axis=0, tiled=True)  28.2 us
    dot_general x11, matrix products, dot(): return jnp.einsum(spec, left, right, preferred_element_type=F32)  11.7 us
    ppermute x5, waiting for transfers between devices, swap(): return lax.ppermute(value, 'core', SWAP)  4.65 us
  transfers between devices with their start and end apart: 9, of which 7 were waited for; matrix products, arithmetic and copies ran while one was open for 6% of the time, Pallas kernels for 0%

profile of v1, /device:TPU:1, one launch (start us, length us, event | category | flops | bytes accessed | tf_op | source)
XLA Modules:
  0.0 203.9 jit_solution(4501097837602607637)
XLA Ops:
  0.7 1.2 copy.73
  3.0 8.8 %collective-permute-start = (bf16[64,1280]{1,0:T(8,128)(2,1)S(1)}, bf16[64,1280]{1,0:T(8,128)(2,1)S(1)}, u32[]{:S(2)}, u32[]{:S(2)}) collective-permute-start(bf16[64,1280]{1,0:T(8,128)(2,1)S(1)} %get-tuple-element.20), channel_id=1, source_target_pairs={{0,64},{64,0},{1,65},{65,1},{2,66},{66,2},{3,67},{67,3},{4,68},{68... | collective-permute-start | bytes 491528 | tf_op jit(solution)/shard_map/ppermute | solution.py:26
  11.8 1.0 collective-permute-done
  13.4 17.8 %all_to_all.35 = bf16[32,4,1280]{2,1,0:T(4,128)(2,1)S(1)} all-to-all(bf16[32,4,1280]{2,1,0:T(4,128)(2,1)S(1)} %reshape.68), channel_id=1, replica_groups=mesh['y_lo'=4,'core'=2,'y_hi'=2,'x'=4,'z'=8] {'x','z'}, dimensions={0} | all-to-all | bytes 655360 | tf_op jit(solution)/shard_map/all_to_all | solution.py:22
  31.6 1.2 broadcast_in_dim.15
  32.8 7.0 %all-to-all-start.1 = ((bf16[8,64,1280]{2,1,0:T(8,128)(2,1)}), bf16[8,64,1280]{2,1,0:T(8,128)(2,1)}, u32[]{:S(2)}, u32[]{:S(2)}) async-start(bf16[8,64,1280]{2,1,0:T(8,128)(2,1)} %bitcast.8), calls=%async_computation.1 | async-start | bytes 2621440 | tf_op jit(solution)/shard_map/all_to_all | solution.py:22
  39.8 6.0 %collective-permute-start.1 = (bf16[320,1280]{1,0:T(8,128)(2,1)S(1)}, bf16[320,1280]{1,0:T(8,128)(2,1)S(1)}, u32[]{:S(2)}, u32[]{:S(2)}) collective-permute-start(bf16[320,1280]{1,0:T(8,128)(2,1)S(1)} %select_bitcast_fusion.2), channel_id=1, source_target_pairs={{0,64},{64,0},{1,65},{65,1},{2,66},{66,2},{3,67},{67,3},{4,68},{68... | collective-permute-start | bytes 2457608 | tf_op jit(solution)/shard_map/ppermute | solution.py:26
  45.8 1.9 collective-permute-done.1
  47.8 1.0 bitcast_select_fusion.1
  48.8 20.4 %all-to-all-done.1 = bf16[8,64,1280]{2,1,0:T(8,128)(2,1)} async-done(((bf16[8,64,1280]{2,1,0:T(8,128)(2,1)}), bf16[8,64,1280]{2,1,0:T(8,128)(2,1)}, u32[]{:S(2)}, u32[]{:S(2)}) %all-to-all-start.1) | async-done | bytes 1310752 | tf_op jit(solution)/shard_map/all_to_all | solution.py:22
  69.3 3.0 %fusion.12 = (bf16[512,640]{1,0:T(8,128)(2,1)S(1)}, f32[512,640]{1,0:T(8,128)S(1)}) fusion(pred[]{:T(512)S(6)} %eq.3, bf16[512,1280]{1,0:T(8,128)(2,1)} %bitcast.9, bf16[320,1280]{1,0:T(8,128)(2,1)} %get-tuple-element.14, bf16[320,1280]{1,0:T(8,128)(2,1)S(1)} %get-tuple-element.13), kind=kOutput, calls=%fused_computation.23 | convolution fusion | flops 845414400 | bytes 4915201 | tf_op jit(solution)/shard_map/id,hd->ih/dot_general | solution.py:30
  72.3 5.1 %collective-permute-start.2 = (bf16[512,640]{1,0:T(8,128)(2,1)S(1)}, bf16[512,640]{1,0:T(8,128)(2,1)S(1)}, u32[]{:S(2)}, u32[]{:S(2)}) collective-permute-start(bf16[512,640]{1,0:T(8,128)(2,1)S(1)} %get-tuple-element.22), channel_id=1, source_target_pairs={{0,64},{64,0},{1,65},{65,1},{2,66},{66,2},{3,67},{67,3},{4,68},{68... | collective-permute-start | bytes 1966088 | tf_op jit(solution)/shard_map/ppermute | solution.py:26
  77.4 1.7 collective-permute-done.2
  79.1 2.0 convolution_convert_fusion.1
  81.1 32.7 %all_to_all.36 = bf16[8,64,1280]{2,1,0:T(8,128)(2,1)S(1)} all-to-all(bf16[8,64,1280]{2,1,0:T(8,128)(2,1)S(1)} %bitcast.96), channel_id=1, replica_groups=mesh['y_lo'=4,'core'=2,'y_hi'=2,'x'=4,'z'=8] {'y_lo','y_hi'}, dimensions={0} | all-to-all | bytes 2621440 | tf_op jit(solution)/shard_map/all_to_all | solution.py:22
  114.3 1.8 reduce_sum.71
  116.2 1.0 copy.54
  117.2 7.5 %all-to-all-start.3 = ((bf16[32,4,1280]{2,1,0:T(4,128)(2,1)}), bf16[32,4,1280]{2,1,0:T(4,128)(2,1)S(1)}, u32[]{:S(2)}, u32[]{:S(2)}) async-start(bf16[32,4,1280]{2,1,0:T(4,128)(2,1)} %copy.54), calls=%async_computation.3 | async-start | bytes 655360 | tf_op jit(solution)/shard_map/all_to_all | solution.py:22
  124.7 3.4 %convolution_convert_fusion = bf16[640,1280]{1,0:T(8,128)(2,1)S(1)} fusion(bf16[512,1280]{1,0:T(8,128)(2,1)} %bitcast.9, bf16[512,640]{1,0:T(8,128)(2,1)S(1)} %copy-done.7, f32[512,640]{1,0:T(8,128)} %copy-done.8, pred[]{:T(512)S(6)} %eq.3), kind=kOutput, calls=%fused_computation | convolution fusion | flops 846888960 | bytes 4915201 | tf_op jit(solution)/shard_map/ih,id->hd/dot_general | solution.py:30
  128.2 6.5 %all-to-all-done.3 = bf16[32,4,1280]{2,1,0:T(4,128)(2,1)S(1)} async-done(((bf16[32,4,1280]{2,1,0:T(4,128)(2,1)}), bf16[32,4,1280]{2,1,0:T(4,128)(2,1)S(1)}, u32[]{:S(2)}, u32[]{:S(2)}) %all-to-all-start.3) | async-done | bytes 327712 | tf_op jit(solution)/shard_map/all_to_all | solution.py:22
  135.4 7.3 %collective-permute-start.3 = (bf16[64,1280]{1,0:T(8,128)(2,1)S(1)}, bf16[64,1280]{1,0:T(8,128)(2,1)S(1)}, u32[]{:S(2)}, u32[]{:S(2)}) collective-permute-start(bf16[64,1280]{1,0:T(8,128)(2,1)S(1)} %select_bitcast_fusion.3), channel_id=1, source_target_pairs={{0,64},{64,0},{1,65},{65,1},{2,66},{66,2},{3,67},{67,3},{4,68},{68... | collective-permute-start | bytes 491528 | tf_op jit(solution)/shard_map/ppermute | solution.py:26
  142.7 1.0 broadcast_select_fusion.1
  143.7 2.1 %collective-permute-start.4 = (bf16[320,1280]{1,0:T(8,128)(2,1)}, bf16[320,1280]{1,0:T(8,128)(2,1)}, u32[]{:S(2)}, u32[]{:S(2)}) collective-permute-start(bf16[320,1280]{1,0:T(8,128)(2,1)} %broadcast_select_fusion.1), channel_id=1, source_target_pairs={{0,64},{64,0},{1,65},{65,1},{2,66},{66,2},{3,67},{67,3},{4,68},{68... | collective-permute-start | bytes 2457608 | tf_op jit(solution)/shard_map/ppermute | solution.py:26
  147.1 18.3 %all_to_all.37 = f32[16,4,1280]{2,1,0:T(4,128)S(1)} all-to-all(f32[16,4,1280]{2,1,0:T(4,128)S(1)} %copy.58), channel_id=1, replica_groups=mesh['y_lo'=4,'core'=2,'y_hi'=2,'x'=4,'z'=8] {'y_lo','x'}, dimensions={0} | all-to-all | bytes 655360 | tf_op jit(solution)/shard_map/all_to_all | solution.py:22
  165.4 0.8 broadcast_in_dim.17
  166.3 7.4 %all-to-all-start.5 = ((bf16[32,4,1280]{2,1,0:T(4,128)(2,1)}), bf16[32,4,1280]{2,1,0:T(4,128)(2,1)S(1)}, u32[]{:S(2)}, u32[]{:S(2)}) async-start(bf16[32,4,1280]{2,1,0:T(4,128)(2,1)} %broadcast_in_dim.17), calls=%async_computation.5 | async-start | bytes 655360 | tf_op jit(solution)/shard_map/all_to_all | solution.py:22
  173.6 2.5 %select_bitcast_fusion = (bf16[1,320,1280]{2,1,0:T(8,128)(2,1)}, bf16[1,320,1280]{2,1,0:T(8,128)(2,1)}) fusion(bf16[320,1280]{1,0:T(8,128)(2,1)} %collective-permute-done.4, pred[]{:T(512)S(6)} %eq.3, bf16[640,1280]{1,0:T(8,128)(2,1)S(1)} %convolution_convert_fusion), kind=kLoop, calls=%fused_computation.29 | loop fusion | flops 1228800 | bytes 4096001 | tf_op jit(solution)/shard_map/broadcast_in_dim | solution.py:92
  176.1 11.7 %all-to-all-done.5 = bf16[32,4,1280]{2,1,0:T(4,128)(2,1)S(1)} async-done(((bf16[32,4,1280]{2,1,0:T(4,128)(2,1)}), bf16[32,4,1280]{2,1,0:T(4,128)(2,1)S(1)}, u32[]{:S(2)}, u32[]{:S(2)}) %all-to-all-start.5) | async-done | bytes 327712 | tf_op jit(solution)/shard_map/all_to_all | solution.py:22
  188.0 0.7 broadcast_in_dim.18
  188.7 6.4 %all-to-all-start.6 = ((bf16[16,4,1280]{2,1,0:T(4,128)(2,1)}), bf16[16,4,1280]{2,1,0:T(4,128)(2,1)S(1)}, u32[]{:S(2)}, u32[]{:S(2)}) async-start(bf16[16,4,1280]{2,1,0:T(4,128)(2,1)} %broadcast_in_dim.18), calls=%async_computation.6 | async-start | bytes 327680 | tf_op jit(solution)/shard_map/all_to_all | solution.py:22
  195.5 1.2 fusion.1
  196.7 6.4 %all-to-all-done.6 = bf16[16,4,1280]{2,1,0:T(4,128)(2,1)S(1)} async-done(((bf16[16,4,1280]{2,1,0:T(4,128)(2,1)}), bf16[16,4,1280]{2,1,0:T(4,128)(2,1)S(1)}, u32[]{:S(2)}, u32[]{:S(2)}) %all-to-all-start.6) | async-done | bytes 163872 | tf_op jit(solution)/shard_map/all_to_all | solution.py:22
  (49 shorter events, 6.0 us)
Async XLA Ops:
  0.6 1.3 copy-start
  0.6 2.1 %copy-start.4 = (bf16[1,192,1280]{2,1,0:T(8,128)(2,1)S(1)}, bf16[1,192,1280]{2,1,0:T(8,128)(2,1)}, u32[]{:S(2)}) copy-start(bf16[1,192,1280]{2,1,0:T(8,128)(2,1)} %param.6) | copy-start | bytes 1474564
  3.0 9.8 %collective-permute-start = (bf16[64,1280]{1,0:T(8,128)(2,1)S(1)}, bf16[64,1280]{1,0:T(8,128)(2,1)S(1)}, u32[]{:S(2)}, u32[]{:S(2)}) collective-permute-start(bf16[64,1280]{1,0:T(8,128)(2,1)S(1)} %get-tuple-element.20), channel_id=1, source_target_pairs={{0,64},{64,0},{1,65},{65,1},{2,66},{66,2},{3,67},{67,3},{4,68},{68... | collective-permute-start | bytes 491528 | tf_op jit(solution)/shard_map/ppermute | solution.py:26
  32.8 7.0 %copy-start.1 = (bf16[1,320,1280]{2,1,0:T(8,128)(2,1)S(1)}, bf16[1,320,1280]{2,1,0:T(8,128)(2,1)}, u32[]{:S(2)}) copy-start(bf16[1,320,1280]{2,1,0:T(8,128)(2,1)} %param.9) | copy-start | bytes 2457604
  32.8 7.0 %copy-start.2 = (bf16[1,320,1280]{2,1,0:T(8,128)(2,1)S(1)}, bf16[1,320,1280]{2,1,0:T(8,128)(2,1)}, u32[]{:S(2)}) copy-start(bf16[1,320,1280]{2,1,0:T(8,128)(2,1)} %param.8) | copy-start | bytes 2457604
  32.8 36.5 %all-to-all-start.1 = ((bf16[8,64,1280]{2,1,0:T(8,128)(2,1)}), bf16[8,64,1280]{2,1,0:T(8,128)(2,1)}, u32[]{:S(2)}, u32[]{:S(2)}) async-start(bf16[8,64,1280]{2,1,0:T(8,128)(2,1)} %bitcast.8), calls=%async_computation.1 | async-start | bytes 2621440 | tf_op jit(solution)/shard_map/all_to_all | solution.py:22
  39.8 7.9 %collective-permute-start.1 = (bf16[320,1280]{1,0:T(8,128)(2,1)S(1)}, bf16[320,1280]{1,0:T(8,128)(2,1)S(1)}, u32[]{:S(2)}, u32[]{:S(2)}) collective-permute-start(bf16[320,1280]{1,0:T(8,128)(2,1)S(1)} %select_bitcast_fusion.2), channel_id=1, source_target_pairs={{0,64},{64,0},{1,65},{65,1},{2,66},{66,2},{3,67},{67,3},{4,68},{68... | collective-permute-start | bytes 2457608 | tf_op jit(solution)/shard_map/ppermute | solution.py:26
  69.3 9.8 %copy-start.3 = (bf16[320,1280]{1,0:T(8,128)(2,1)S(1)}, bf16[320,1280]{1,0:T(8,128)(2,1)}, u32[]{:S(2)}) copy-start(bf16[320,1280]{1,0:T(8,128)(2,1)} %get-tuple-element.14) | copy-start | bytes 2457604
  72.2 8.8 %copy-start.8 = (f32[512,640]{1,0:T(8,128)}, f32[512,640]{1,0:T(8,128)S(1)}, u32[]{:S(2)}) copy-start(f32[512,640]{1,0:T(8,128)S(1)} %get-tuple-element.23) | copy-start | bytes 3932164
  72.3 6.8 %collective-permute-start.2 = (bf16[512,640]{1,0:T(8,128)(2,1)S(1)}, bf16[512,640]{1,0:T(8,128)(2,1)S(1)}, u32[]{:S(2)}, u32[]{:S(2)}) collective-permute-start(bf16[512,640]{1,0:T(8,128)(2,1)S(1)} %get-tuple-element.22), channel_id=1, source_target_pairs={{0,64},{64,0},{1,65},{65,1},{2,66},{66,2},{3,67},{67,3},{4,68},{68... | collective-permute-start | bytes 1966088 | tf_op jit(solution)/shard_map/ppermute | solution.py:26
  79.1 2.0 copy-start.6
  116.2 8.6 %copy-start.7 = (bf16[512,640]{1,0:T(8,128)(2,1)S(1)}, bf16[512,640]{1,0:T(8,128)(2,1)}, u32[]{:S(2)}) copy-start(bf16[512,640]{1,0:T(8,128)(2,1)} %copy-done.6) | copy-start | bytes 1966084
  117.2 17.5 %all-to-all-start.3 = ((bf16[32,4,1280]{2,1,0:T(4,128)(2,1)}), bf16[32,4,1280]{2,1,0:T(4,128)(2,1)S(1)}, u32[]{:S(2)}, u32[]{:S(2)}) async-start(bf16[32,4,1280]{2,1,0:T(4,128)(2,1)} %copy.54), calls=%async_computation.3 | async-start | bytes 655360 | tf_op jit(solution)/shard_map/all_to_all | solution.py:22
  135.4 10.6 %copy-start.5 = (bf16[1,192,1280]{2,1,0:T(8,128)(2,1)S(1)}, bf16[1,192,1280]{2,1,0:T(8,128)(2,1)}, u32[]{:S(2)}) copy-start(bf16[1,192,1280]{2,1,0:T(8,128)(2,1)} %param.6) | copy-start | bytes 1474564
  135.4 10.4 %collective-permute-start.3 = (bf16[64,1280]{1,0:T(8,128)(2,1)S(1)}, bf16[64,1280]{1,0:T(8,128)(2,1)S(1)}, u32[]{:S(2)}, u32[]{:S(2)}) collective-permute-start(bf16[64,1280]{1,0:T(8,128)(2,1)S(1)} %select_bitcast_fusion.3), channel_id=1, source_target_pairs={{0,64},{64,0},{1,65},{65,1},{2,66},{66,2},{3,67},{67,3},{4,68},{68... | collective-permute-start | bytes 491528 | tf_op jit(solution)/shard_map/ppermute | solution.py:26
  143.7 29.9 %collective-permute-start.4 = (bf16[320,1280]{1,0:T(8,128)(2,1)}, bf16[320,1280]{1,0:T(8,128)(2,1)}, u32[]{:S(2)}, u32[]{:S(2)}) collective-permute-start(bf16[320,1280]{1,0:T(8,128)(2,1)} %broadcast_select_fusion.1), channel_id=1, source_target_pairs={{0,64},{64,0},{1,65},{65,1},{2,66},{66,2},{3,67},{67,3},{4,68},{68... | collective-permute-start | bytes 2457608 | tf_op jit(solution)/shard_map/ppermute | solution.py:26
  166.3 21.5 %all-to-all-start.5 = ((bf16[32,4,1280]{2,1,0:T(4,128)(2,1)}), bf16[32,4,1280]{2,1,0:T(4,128)(2,1)S(1)}, u32[]{:S(2)}, u32[]{:S(2)}) async-start(bf16[32,4,1280]{2,1,0:T(4,128)(2,1)} %broadcast_in_dim.17), calls=%async_computation.5 | async-start | bytes 655360 | tf_op jit(solution)/shard_map/all_to_all | solution.py:22
  188.7 14.5 %all-to-all-start.6 = ((bf16[16,4,1280]{2,1,0:T(4,128)(2,1)}), bf16[16,4,1280]{2,1,0:T(4,128)(2,1)S(1)}, u32[]{:S(2)}, u32[]{:S(2)}) async-start(bf16[16,4,1280]{2,1,0:T(4,128)(2,1)} %broadcast_in_dim.18), calls=%async_computation.6 | async-start | bytes 327680 | tf_op jit(solution)/shard_map/all_to_all | solution.py:22

commit v2 on v1

--- a/solution.py
+++ b/solution.py
@@ -6,10 +6,7 @@
 SWAP = [(0, 1), (1, 0)]
 DP = ("y_lo", "core")
 EXPERT = ("y_hi", "x", "z")
-PLANE = ("x", "z")
-COLUMN = ("y_lo", "y_hi")
-RING = ("y_lo", "x")
-REST = ("core", "y_hi", "z")
+CHIPS = ("y_lo",) + EXPERT
 BF = jnp.bfloat16
 F32 = jnp.float32
 
@@ -18,8 +15,8 @@
     return jax.vjp(jax.nn.gelu, preact)[1](upstream)[0]
 
 
-def exchange(blocks, axes):
-    return lax.all_to_all(blocks, axes, split_axis=0, concat_axis=0, tiled=True)
+def exchange(blocks):
+    return lax.all_to_all(blocks, CHIPS, split_axis=0, concat_axis=0, tiled=True)
 
 
 def swap(value):
@@ -38,7 +35,6 @@
     weight = jnp.concatenate(
         [jnp.where(first, weight_kept, weight_got), jnp.where(first, weight_got, weight_kept)]
     )
-    router = router.reshape(1280, 2, 32).swapaxes(1, 2).reshape(1280, 64)
     logits = dot("md,ds->ms", tokens, router)
     dispatch = jax.nn.softmax(logits, axis=0)
     combine = jax.nn.softmax(logits, axis=1)
@@ -49,22 +45,15 @@
     pair = jnp.stack(
         [jnp.where(first, own_in, got), jnp.where(first, got, own_grad)], axis=1
     )
-    blocks = pair.reshape(32, 4, 1280)
-    moved = exchange(blocks, PLANE).reshape(32, 2, 2, 1280)
-    moved = moved.swapaxes(0, 1).reshape(1, 2, 64, 1280)
-    rows = exchange(
-        jnp.broadcast_to(moved, (4, 2, 64, 1280)).reshape(8, 64, 1280), COLUMN
-    ).reshape(512, 1280)
+    blocks = jnp.broadcast_to(pair[None], (4, 64, 2, 1280)).reshape(256, 2, 1280)
+    rows = exchange(blocks).reshape(512, 1280)
     act = dot("id,hd->ih", rows, weight)
     other = swap(jnp.where(first, jax.nn.gelu(act), act).astype(BF))
     hid = jnp.where(first, gelu_back(act, other.astype(F32)).astype(BF), other)
     partial = dot("ih,hd->id", hid, weight).astype(BF)
     d_weight = dot("ih,id->hd", hid, rows).astype(BF)
-    parts = exchange(partial.reshape(8, 64, 1280), COLUMN).reshape(4, 2, 32, 2, 1280)
-    summed = jnp.sum(parts.astype(F32), axis=0).astype(BF)
-    back = exchange(
-        summed.swapaxes(0, 1).reshape(32, 4, 1280), PLANE
-    ).reshape(64, 2, 1280)
+    parts = exchange(partial.reshape(256, 2, 1280)).reshape(4, 64, 2, 1280)
+    back = jnp.sum(parts.astype(F32), axis=0).astype(BF)
     kept = jnp.where(first, back[:, 0], back[:, 1])
     got = swap(jnp.where(first, back[:, 1], back[:, 0]))
     slot_in_grad = jnp.where(first, kept, got)
@@ -80,11 +69,14 @@
         dot("ms,ds->md", logit_grad, router) + dot("ms,sd->md", dispatch_cast, slot_in_grad)
     ).astype(BF)
     term = dot("ms,md->sd", logit_grad, tokens)
-    term = jnp.sum(exchange(term.reshape(16, 4, 1280), RING), axis=0)
-    term = jnp.broadcast_to(term.astype(BF)[None], (32, 4, 1280))
-    term = jnp.sum(exchange(term, REST).astype(F32), axis=0).astype(BF)
-    term = exchange(jnp.broadcast_to(term[None], (16, 4, 1280)), RING)
-    d_router = term.reshape(32, 2, 1280).transpose(2, 1, 0).reshape(1280, 64)
+    half = jnp.where(first, term[:32], term[32:]) + swap(jnp.where(first, term[32:], term[:32]))
+    half = half.reshape(32, 5, 2, 128).swapaxes(0, 1).reshape(160, 2, 128)
+    half = jnp.concatenate([half, jnp.zeros((96, 2, 128), F32)])
+    piece = jnp.sum(exchange(half), axis=0).astype(BF)
+    pieces = exchange(jnp.broadcast_to(piece[None], (256, 2, 128)))
+    half = pieces[:160].reshape(5, 32, 2, 128).swapaxes(0, 1).reshape(32, 1280)
+    got = swap(half)
+    d_router = jnp.concatenate([jnp.where(first, half, got), jnp.where(first, got, half)]).T
     d_kept = jnp.where(first, d_weight[:320], d_weight[320:])
     d_got = swap(jnp.where(first, d_weight[320:], d_weight[:320]))
     d_w_in = jnp.where(first, d_kept, d_got)

time: 205 us -> 198 us (0.966)
  waiting for transfers between devices: 49.8 us -> 43 us
  matrix products: 11.7 us -> 14.7 us
  starting transfers between devices: 57.6 us -> 54.8 us
    all_to_all x4 -> x2, waiting for transfers between devices: 45.1 us -> 38.3 us  [exchange(): lax.all_to_all(blocks, CHIPS, split_axis=0, concat_axis=0, tiled=True)]
    dot_general x11, matrix products: 11.7 us -> 14.7 us  [dot(): return jnp.einsum(spec, left, right, preferred_element_type=F32)]
    unnamed x18 -> x30, local copies, waits for them, and re-layouts: 0.05 us -> 2.86 us
    reshape x9 -> x5, local copies, waits for them, and re-layouts: 3.42 us -> 1.19 us  [the longest x1 0.54 us: local(): parts = exchange(partial.reshape(256, 2, 1280)).reshape(4, 64, 2, 1280)]
    all_to_all x4 -> x2, starting transfers between devices: 28.2 us -> 26.5 us  [exchange(): lax.all_to_all(blocks, CHIPS, split_axis=0, concat_axis=0, tiled=True)]
    ppermute x5 -> x7, starting transfers between devices: 29.3 us -> 28.3 us  [swap(): return lax.ppermute(value, 'core', SWAP)]
    all_to_all x3 -> x2, blocking collectives: 68.8 us -> 68.3 us  [exchange(): lax.all_to_all(blocks, CHIPS, split_axis=0, concat_axis=0, tiled=True)]
    ppermute x5 -> x7, waiting for transfers between devices: 4.65 us -> 4.66 us  [swap(): return lax.ppermute(value, 'core', SWAP)]
  transfers between devices with their start and end apart: 9 -> 9, of which waited for: 7 -> 5; matrix products, arithmetic and copies ran while one was open for 6% -> 5% of each run, Pallas kernels for 0% -> 0%
where the time goes in v2:
time: 198 us
  blocking collectives  68.3 us (34%)
  starting transfers between devices  54.8 us (28%)
  waiting for transfers between devices  43 us (22%)
  matrix products  14.7 us (7%)
  other arithmetic  8.2 us (4%)
  local copies, waits for them, and re-layouts  7.54 us (4%)
    all_to_all x2, blocking collectives, exchange(): lax.all_to_all(blocks, CHIPS, split_axis=0, concat_axis=0, tiled=True)  68.3 us
    all_to_all x2, waiting for transfers between devices, exchange(): lax.all_to_all(blocks, CHIPS, split_axis=0, concat_axis=0, tiled=True)  38.3 us
    ppermute x7, starting transfers between devices, swap(): return lax.ppermute(value, 'core', SWAP)  28.3 us
    all_to_all x2, starting transfers between devices, exchange(): lax.all_to_all(blocks, CHIPS, split_axis=0, concat_axis=0, tiled=True)  26.5 us
    dot_general x11, matrix products, dot(): return jnp.einsum(spec, left, right, preferred_element_type=F32)  14.7 us
    ppermute x7, waiting for transfers between devices, swap(): return lax.ppermute(value, 'core', SWAP)  4.66 us
  transfers between devices with their start and end apart: 9, of which 5 were waited for; matrix products, arithmetic and copies ran while one was open for 5% of the time, Pallas kernels for 0%

profile of v2, /device:TPU:1, one launch (start us, length us, event | category | flops | bytes accessed | tf_op | source)
XLA Modules:
  0.0 197.6 jit_solution(3579182440760745644)
XLA Ops:
  0.7 1.0 copy-done
  1.7 1.3 fusion.42
  3.7 8.8 %collective-permute-start = (bf16[64,1280]{1,0:T(8,128)(2,1)S(1)}, bf16[64,1280]{1,0:T(8,128)(2,1)S(1)}, u32[]{:S(2)}, u32[]{:S(2)}) collective-permute-start(bf16[64,1280]{1,0:T(8,128)(2,1)S(1)} %get-tuple-element.22), channel_id=1, source_target_pairs={{0,64},{64,0},{1,65},{65,1},{2,66},{66,2},{3,67},{67,3},{4,68},{68... | collective-permute-start | bytes 491528 | tf_op jit(solution)/shard_map/ppermute | solution.py:23
  12.5 1.0 collective-permute-done
  13.9 1.8 broadcast_in_dim.10
  15.7 17.1 %all-to-all-start = ((bf16[256,2,1280]{2,1,0:T(2,128)(2,1)}), bf16[256,2,1280]{2,1,0:T(2,128)(2,1)S(1)}, u32[]{:S(2)}, u32[]{:S(2)}) async-start(bf16[256,2,1280]{2,1,0:T(2,128)(2,1)} %bitcast.4), calls=%async_computation | async-start | bytes 2621440 | tf_op jit(solution)/shard_map/all_to_all | solution.py:19
  33.0 2.6 %collective-permute-start.1 = (bf16[320,1280]{1,0:T(8,128)(2,1)S(1)}, bf16[320,1280]{1,0:T(8,128)(2,1)S(1)}, u32[]{:S(2)}, u32[]{:S(2)}) collective-permute-start(bf16[320,1280]{1,0:T(8,128)(2,1)S(1)} %select_bitcast_fusion.2), channel_id=1, source_target_pairs={{0,64},{64,0},{1,65},{65,1},{2,66},{66,2},{3,67},{67,3},{4,68},{68... | collective-permute-start | bytes 2457608 | tf_op jit(solution)/shard_map/ppermute | solution.py:23
  35.5 1.9 collective-permute-done.1
  37.5 1.3 bitcast_select_fusion.1
  38.8 29.8 %all-to-all-done = bf16[256,2,1280]{2,1,0:T(2,128)(2,1)S(1)} async-done(((bf16[256,2,1280]{2,1,0:T(2,128)(2,1)}), bf16[256,2,1280]{2,1,0:T(2,128)(2,1)S(1)}, u32[]{:S(2)}, u32[]{:S(2)}) %all-to-all-start) | async-done | bytes 1310752 | tf_op jit(solution)/shard_map/all_to_all | solution.py:19
  69.1 4.3 %fusion.12 = (bf16[512,640]{1,0:T(8,128)(2,1)S(1)}, f32[512,640]{1,0:T(8,128)}) fusion(pred[]{:T(512)S(6)} %eq.3, bf16[512,1280]{1,0:T(8,128)(2,1)S(1)} %reshape.51, bf16[320,1280]{1,0:T(8,128)(2,1)} %get-tuple-element.14, bf16[320,1280]{1,0:T(8,128)(2,1)} %get-tuple-element.13), kind=kOutput, calls=%fused_computation.23 | convolution fusion | flops 845414400 | bytes 4915201 | tf_op jit(solution)/shard_map/id,hd->ih/dot_general | solution.py:27
  73.4 4.3 %collective-permute-start.2 = (bf16[512,640]{1,0:T(8,128)(2,1)S(1)}, bf16[512,640]{1,0:T(8,128)(2,1)S(1)}, u32[]{:S(2)}, u32[]{:S(2)}) collective-permute-start(bf16[512,640]{1,0:T(8,128)(2,1)S(1)} %get-tuple-element.24), channel_id=1, source_target_pairs={{0,64},{64,0},{1,65},{65,1},{2,66},{66,2},{3,67},{67,3},{4,68},{68... | collective-permute-start | bytes 1966088 | tf_op jit(solution)/shard_map/ppermute | solution.py:23
  77.6 1.7 collective-permute-done.2
  79.3 0.8 copy-done.12
  80.2 3.3 %convolution_convert_fusion.1 = bf16[512,1280]{1,0:T(8,128)(2,1)S(1)} fusion(bf16[320,1280]{1,0:T(8,128)(2,1)S(1)} %copy-done.8, bf16[320,1280]{1,0:T(8,128)(2,1)S(1)} %copy-done.7, bf16[512,640]{1,0:T(8,128)(2,1)S(1)} %collective-permute-done.2, f32[512,640]{1,0:T(8,128)} %get-tuple-element.25, pred[]{:T(512)S(6)} %eq.3), kind=kOutput, calls=%fused_computation.1 | convolution fusion | flops 850001920 | bytes 4915201 | tf_op jit(solution)/shard_map/ih,hd->id/dot_general | solution.py:27
  83.5 0.5 reshape.52
  84.0 45.2 %all_to_all.20 = bf16[256,2,1280]{2,1,0:T(2,128)(2,1)S(1)} all-to-all(bf16[256,2,1280]{2,1,0:T(2,128)(2,1)S(1)} %reshape.52), channel_id=1, replica_groups=mesh['y_lo'=4,'core'=2,'y_hi'=2,'x'=4,'z'=8] {'y_lo','y_hi','x','z'}, dimensions={0} | all-to-all | bytes 2621440 | tf_op jit(solution)/shard_map/all_to_all | solution.py:19
  129.2 1.8 reduce_sum.59
  131.6 4.0 %collective-permute-start.3 = (bf16[64,1280]{1,0:T(8,128)(2,1)S(1)}, bf16[64,1280]{1,0:T(8,128)(2,1)S(1)}, u32[]{:S(2)}, u32[]{:S(2)}) collective-permute-start(bf16[64,1280]{1,0:T(8,128)(2,1)S(1)} %select_bitcast_fusion.3), channel_id=1, source_target_pairs={{0,64},{64,0},{1,65},{65,1},{2,66},{66,2},{3,67},{67,3},{4,68},{68... | collective-permute-start | bytes 491528 | tf_op jit(solution)/shard_map/ppermute | solution.py:23
  135.6 3.1 %convolution_convert_fusion = bf16[640,1280]{1,0:T(8,128)(2,1)S(1)} fusion(bf16[512,1280]{1,0:T(8,128)(2,1)S(1)} %copy-done.6, bf16[512,640]{1,0:T(8,128)(2,1)S(1)} %copy-done.13, f32[512,640]{1,0:T(8,128)} %get-tuple-element.25, pred[]{:T(512)S(6)} %eq.3), kind=kOutput, calls=%fused_computation | convolution fusion | flops 846888960 | bytes 4915201 | tf_op jit(solution)/shard_map/ih,id->hd/dot_general | solution.py:27
  138.9 0.8 copy-done.11
  140.5 1.9 collective-permute-start.4
  142.5 1.0 broadcast_select_fusion.1
  143.4 2.4 %collective-permute-start.6 = (bf16[320,1280]{1,0:T(8,128)(2,1)}, bf16[320,1280]{1,0:T(8,128)(2,1)}, u32[]{:S(2)}, u32[]{:S(2)}) collective-permute-start(bf16[320,1280]{1,0:T(8,128)(2,1)} %broadcast_select_fusion.1), channel_id=1, source_target_pairs={{0,64},{64,0},{1,65},{65,1},{2,66},{66,2},{3,67},{67,3},{4,68},{68... | collective-permute-start | bytes 2457608 | tf_op jit(solution)/shard_map/ppermute | solution.py:23
  146.2 23.1 %all_to_all.21 = f32[256,2,128]{2,1,0:T(2,128)S(1)} all-to-all(f32[256,2,128]{2,1,0:T(2,128)S(1)} %concatenate.10.clone), channel_id=1, replica_groups=mesh['y_lo'=4,'core'=2,'y_hi'=2,'x'=4,'z'=8] {'y_lo','y_hi','x','z'}, dimensions={0} | all-to-all | bytes 524288 | tf_op jit(solution)/shard_map/all_to_all | solution.py:19
  169.6 0.7 broadcast_in_dim.12
  170.3 9.4 %all-to-all-start.3 = ((bf16[256,2,128]{2,1,0:T(2,128)(2,1)}), bf16[256,2,128]{2,1,0:T(2,128)(2,1)S(1)}, u32[]{:S(2)}, u32[]{:S(2)}) async-start(bf16[256,2,128]{2,1,0:T(2,128)(2,1)} %broadcast_in_dim.12), calls=%async_computation.3 | async-start | bytes 262144 | tf_op jit(solution)/shard_map/all_to_all | solution.py:19
  179.7 2.5 %select_bitcast_fusion = (bf16[1,320,1280]{2,1,0:T(8,128)(2,1)}, bf16[1,320,1280]{2,1,0:T(8,128)(2,1)}) fusion(bf16[320,1280]{1,0:T(8,128)(2,1)} %collective-permute-done.6, pred[]{:T(512)S(6)} %eq.3, bf16[640,1280]{1,0:T(8,128)(2,1)S(1)} %convolution_convert_fusion), kind=kLoop, calls=%fused_computation.34 | loop fusion | flops 1228800 | bytes 4096001 | tf_op jit(solution)/shard_map/broadcast_in_dim | solution.py:84
  182.5 8.5 %all-to-all-done.3 = bf16[256,2,128]{2,1,0:T(2,128)(2,1)S(1)} async-done(((bf16[256,2,128]{2,1,0:T(2,128)(2,1)}), bf16[256,2,128]{2,1,0:T(2,128)(2,1)S(1)}, u32[]{:S(2)}, u32[]{:S(2)}) %all-to-all-start.3) | async-done | bytes 131104 | tf_op jit(solution)/shard_map/all_to_all | solution.py:19
  191.3 4.4 %collective-permute-start.5 = (bf16[32,1280]{1,0:T(8,128)(2,1)S(1)}, bf16[32,1280]{1,0:T(8,128)(2,1)S(1)}, u32[]{:S(2)}, u32[]{:S(2)}) collective-permute-start(bf16[32,1280]{1,0:T(8,128)(2,1)S(1)} %reshape.57), channel_id=1, source_target_pairs={{0,64},{64,0},{1,65},{65,1},{2,66},{66,2},{3,67},{67,3},{4,68},{68... | collective-permute-start | bytes 245768 | tf_op jit(solution)/shard_map/ppermute | solution.py:23
  195.7 1.2 fusion.1
  196.9 0.7 maximum_bitcast_fusion
  (56 shorter events, 4.4 us)
Async XLA Ops:
  0.6 1.0 copy-start
  0.6 2.8 %copy-start.10 = (bf16[1,192,1280]{2,1,0:T(8,128)(2,1)S(1)}, bf16[1,192,1280]{2,1,0:T(8,128)(2,1)}, u32[]{:S(2)}) copy-start(bf16[1,192,1280]{2,1,0:T(8,128)(2,1)} %param.6) | copy-start | bytes 1474564
  3.5 10.5 %copy-start.3 = (bf16[64,1280]{1,0:T(8,128)(2,1)}, bf16[64,1280]{1,0:T(8,128)(2,1)S(1)}, u32[]{:S(2)}) copy-start(bf16[64,1280]{1,0:T(8,128)(2,1)S(1)} %convolution_convert_fusion.3) | copy-start | bytes 491524
  3.7 9.8 %collective-permute-start = (bf16[64,1280]{1,0:T(8,128)(2,1)S(1)}, bf16[64,1280]{1,0:T(8,128)(2,1)S(1)}, u32[]{:S(2)}, u32[]{:S(2)}) collective-permute-start(bf16[64,1280]{1,0:T(8,128)(2,1)S(1)} %get-tuple-element.22), channel_id=1, source_target_pairs={{0,64},{64,0},{1,65},{65,1},{2,66},{66,2},{3,67},{67,3},{4,68},{68... | collective-permute-start | bytes 491528 | tf_op jit(solution)/shard_map/ppermute | solution.py:23
  15.7 17.1 %copy-start.1 = (bf16[1,320,1280]{2,1,0:T(8,128)(2,1)S(1)}, bf16[1,320,1280]{2,1,0:T(8,128)(2,1)}, u32[]{:S(2)}) copy-start(bf16[1,320,1280]{2,1,0:T(8,128)(2,1)} %param.9) | copy-start | bytes 2457604
  15.7 17.1 %copy-start.2 = (bf16[1,320,1280]{2,1,0:T(8,128)(2,1)S(1)}, bf16[1,320,1280]{2,1,0:T(8,128)(2,1)}, u32[]{:S(2)}) copy-start(bf16[1,320,1280]{2,1,0:T(8,128)(2,1)} %param.8) | copy-start | bytes 2457604
  15.7 52.9 %all-to-all-start = ((bf16[256,2,1280]{2,1,0:T(2,128)(2,1)}), bf16[256,2,1280]{2,1,0:T(2,128)(2,1)S(1)}, u32[]{:S(2)}, u32[]{:S(2)}) async-start(bf16[256,2,1280]{2,1,0:T(2,128)(2,1)} %bitcast.4), calls=%async_computation | async-start | bytes 2621440 | tf_op jit(solution)/shard_map/all_to_all | solution.py:19
  33.0 4.5 %collective-permute-start.1 = (bf16[320,1280]{1,0:T(8,128)(2,1)S(1)}, bf16[320,1280]{1,0:T(8,128)(2,1)S(1)}, u32[]{:S(2)}, u32[]{:S(2)}) collective-permute-start(bf16[320,1280]{1,0:T(8,128)(2,1)S(1)} %select_bitcast_fusion.2), channel_id=1, source_target_pairs={{0,64},{64,0},{1,65},{65,1},{2,66},{66,2},{3,67},{67,3},{4,68},{68... | collective-permute-start | bytes 2457608 | tf_op jit(solution)/shard_map/ppermute | solution.py:23
  69.1 4.3 %copy-start.5 = (bf16[512,1280]{1,0:T(8,128)(2,1)}, bf16[512,1280]{1,0:T(8,128)(2,1)S(1)}, u32[]{:S(2)}) copy-start(bf16[512,1280]{1,0:T(8,128)(2,1)S(1)} %reshape.51) | copy-start | bytes 3932164
  69.1 11.1 %copy-start.7 = (bf16[320,1280]{1,0:T(8,128)(2,1)S(1)}, bf16[320,1280]{1,0:T(8,128)(2,1)}, u32[]{:S(2)}) copy-start(bf16[320,1280]{1,0:T(8,128)(2,1)} %get-tuple-element.13) | copy-start | bytes 2457604
  69.1 11.1 %copy-start.8 = (bf16[320,1280]{1,0:T(8,128)(2,1)S(1)}, bf16[320,1280]{1,0:T(8,128)(2,1)}, u32[]{:S(2)}) copy-start(bf16[320,1280]{1,0:T(8,128)(2,1)} %get-tuple-element.14) | copy-start | bytes 2457604
  73.4 6.0 %collective-permute-start.2 = (bf16[512,640]{1,0:T(8,128)(2,1)S(1)}, bf16[512,640]{1,0:T(8,128)(2,1)S(1)}, u32[]{:S(2)}, u32[]{:S(2)}) collective-permute-start(bf16[512,640]{1,0:T(8,128)(2,1)S(1)} %get-tuple-element.24), channel_id=1, source_target_pairs={{0,64},{64,0},{1,65},{65,1},{2,66},{66,2},{3,67},{67,3},{4,68},{68... | collective-permute-start | bytes 1966088 | tf_op jit(solution)/shard_map/ppermute | solution.py:23
  79.3 0.8 copy-start.12
  131.0 4.5 %copy-start.6 = (bf16[512,1280]{1,0:T(8,128)(2,1)S(1)}, bf16[512,1280]{1,0:T(8,128)(2,1)}, u32[]{:S(2)}) copy-start(bf16[512,1280]{1,0:T(8,128)(2,1)} %copy-done.5) | copy-start | bytes 3932164
  131.0 4.5 %copy-start.13 = (bf16[512,640]{1,0:T(8,128)(2,1)S(1)}, bf16[512,640]{1,0:T(8,128)(2,1)}, u32[]{:S(2)}) copy-start(bf16[512,640]{1,0:T(8,128)(2,1)} %copy-done.12) | copy-start | bytes 1966084
  131.5 7.1 %copy-start.4 = (bf16[64,1280]{1,0:T(8,128)(2,1)S(1)}, bf16[64,1280]{1,0:T(8,128)(2,1)}, u32[]{:S(2)}) copy-start(bf16[64,1280]{1,0:T(8,128)(2,1)} %copy-done.3) | copy-start | bytes 491524
  131.6 7.1 %collective-permute-start.3 = (bf16[64,1280]{1,0:T(8,128)(2,1)S(1)}, bf16[64,1280]{1,0:T(8,128)(2,1)S(1)}, u32[]{:S(2)}, u32[]{:S(2)}) collective-permute-start(bf16[64,1280]{1,0:T(8,128)(2,1)S(1)} %select_bitcast_fusion.3), channel_id=1, source_target_pairs={{0,64},{64,0},{1,65},{65,1},{2,66},{66,2},{3,67},{67,3},{4,68},{68... | collective-permute-start | bytes 491528 | tf_op jit(solution)/shard_map/ppermute | solution.py:23
  138.6 1.0 copy-start.11
  140.5 5.3 %collective-permute-start.4 = (f32[32,1280]{1,0:T(8,128)S(1)}, f32[32,1280]{1,0:T(8,128)S(1)}, u32[]{:S(2)}, u32[]{:S(2)}) collective-permute-start(f32[32,1280]{1,0:T(8,128)S(1)} %slice_select_fusion), channel_id=1, source_target_pairs={{0,64},{64,0},{1,65},{65,1},{2,66},{66,2},{3,67},{67,3},{4,68},{68... | collective-permute-start | bytes 491528 | tf_op jit(solution)/shard_map/ppermute | solution.py:23
  143.4 36.3 %collective-permute-start.6 = (bf16[320,1280]{1,0:T(8,128)(2,1)}, bf16[320,1280]{1,0:T(8,128)(2,1)}, u32[]{:S(2)}, u32[]{:S(2)}) collective-permute-start(bf16[320,1280]{1,0:T(8,128)(2,1)} %broadcast_select_fusion.1), channel_id=1, source_target_pairs={{0,64},{64,0},{1,65},{65,1},{2,66},{66,2},{3,67},{67,3},{4,68},{68... | collective-permute-start | bytes 2457608 | tf_op jit(solution)/shard_map/ppermute | solution.py:23
  170.3 20.7 %all-to-all-start.3 = ((bf16[256,2,128]{2,1,0:T(2,128)(2,1)}), bf16[256,2,128]{2,1,0:T(2,128)(2,1)S(1)}, u32[]{:S(2)}, u32[]{:S(2)}) async-start(bf16[256,2,128]{2,1,0:T(2,128)(2,1)} %broadcast_in_dim.12), calls=%async_computation.3 | async-start | bytes 262144 | tf_op jit(solution)/shard_map/all_to_all | solution.py:19
  179.7 2.5 %copy-start.9 = (bf16[1280,64]{0,1:T(8,128)(2,1)S(1)}, bf16[1280,64]{0,1:T(8,128)(2,1)}, u32[]{:S(2)}) copy-start(bf16[1280,64]{0,1:T(8,128)(2,1)} %param.7) | copy-start | bytes 491524
  191.3 5.6 %collective-permute-start.5 = (bf16[32,1280]{1,0:T(8,128)(2,1)S(1)}, bf16[32,1280]{1,0:T(8,128)(2,1)S(1)}, u32[]{:S(2)}, u32[]{:S(2)}) collective-permute-start(bf16[32,1280]{1,0:T(8,128)(2,1)S(1)} %reshape.57), channel_id=1, source_target_pairs={{0,64},{64,0},{1,65},{65,1},{2,66},{66,2},{3,67},{67,3},{4,68},{68... | collective-permute-start | bytes 245768 | tf_op jit(solution)/shard_map/ppermute | solution.py:23

commit v3 on v2

--- a/solution.py
+++ b/solution.py
@@ -53,6 +53,9 @@
     partial = dot("ih,hd->id", hid, weight).astype(BF)
     d_weight = dot("ih,id->hd", hid, rows).astype(BF)
     parts = exchange(partial.reshape(256, 2, 1280)).reshape(4, 64, 2, 1280)
+    d_kept = jnp.where(first, d_weight[:320], d_weight[320:])
+    d_got = swap(jnp.where(first, d_weight[320:], d_weight[:320]))
+    parts, d_kept, d_got = lax.optimization_barrier((parts, d_kept, d_got))
     back = jnp.sum(parts.astype(F32), axis=0).astype(BF)
     kept = jnp.where(first, back[:, 0], back[:, 1])
     got = swap(jnp.where(first, back[:, 1], back[:, 0]))
@@ -68,17 +71,13 @@
     d_tokens = (
         dot("ms,ds->md", logit_grad, router) + dot("ms,sd->md", dispatch_cast, slot_in_grad)
     ).astype(BF)
-    term = dot("ms,md->sd", logit_grad, tokens)
-    half = jnp.where(first, term[:32], term[32:]) + swap(jnp.where(first, term[32:], term[:32]))
-    half = half.reshape(32, 5, 2, 128).swapaxes(0, 1).reshape(160, 2, 128)
-    half = jnp.concatenate([half, jnp.zeros((96, 2, 128), F32)])
-    piece = jnp.sum(exchange(half), axis=0).astype(BF)
-    pieces = exchange(jnp.broadcast_to(piece[None], (256, 2, 128)))
-    half = pieces[:160].reshape(5, 32, 2, 128).swapaxes(0, 1).reshape(32, 1280)
-    got = swap(half)
-    d_router = jnp.concatenate([jnp.where(first, half, got), jnp.where(first, got, half)]).T
-    d_kept = jnp.where(first, d_weight[:320], d_weight[320:])
-    d_got = swap(jnp.where(first, d_weight[320:], d_weight[:320]))
+    term = dot("ms,md->sd", logit_grad, tokens).astype(BF)
+    term = term.reshape(16, 4, 10, 128).swapaxes(1, 2).reshape(160, 4, 128)
+    term = jnp.concatenate([term, jnp.zeros((96, 4, 128), BF)])
+    piece = jnp.sum(exchange(term).astype(F32), axis=0).astype(BF)
+    pieces = exchange(jnp.broadcast_to(piece[None], (256, 4, 128)))
+    total = pieces[:160].reshape(16, 10, 4, 128).swapaxes(1, 2).reshape(64, 1280)
+    d_router = (total.astype(F32) + swap(total).astype(F32)).astype(BF).T
     d_w_in = jnp.where(first, d_kept, d_got)
     d_w_out = jnp.where(first, d_got, d_kept)
     return (d_tokens[None], d_router, d_w_in[None], d_w_out[None])

time: 198 us -> 193 us (0.975)
  blocking collectives: 68.3 us -> 23.5 us
  waiting for transfers between devices: 43 us -> 77.5 us
  starting transfers between devices: 54.8 us -> 62.2 us
  other arithmetic: 8.2 us -> 6.08 us
    all_to_all x2 -> x1, blocking collectives: 68.3 us -> 23.5 us  [exchange(): lax.all_to_all(blocks, CHIPS, split_axis=0, concat_axis=0, tiled=True)]
    all_to_all x2 -> x3, waiting for transfers between devices: 38.3 us -> 69.8 us  [exchange(): lax.all_to_all(blocks, CHIPS, split_axis=0, concat_axis=0, tiled=True)]
    all_to_all x2 -> x3, starting transfers between devices: 26.5 us -> 35.9 us  [exchange(): lax.all_to_all(blocks, CHIPS, split_axis=0, concat_axis=0, tiled=True)]
    ppermute x7 -> x6, waiting for transfers between devices: 4.66 us -> 7.72 us  [swap(): return lax.ppermute(value, 'core', SWAP)]
    ppermute x7 -> x6, starting transfers between devices: 28.3 us -> 26.3 us  [swap(): return lax.ppermute(value, 'core', SWAP)]
  transfers between devices with their start and end apart: 9 -> 9, of which waited for: 5 -> 8; matrix products, arithmetic and copies ran while one was open for 5% -> 4% of each run, Pallas kernels for 0% -> 0%
where the time goes in v3:
time: 193 us; the launch traced here: 192 us
  waiting for transfers between devices  77.5 us (40%)
  starting transfers between devices  62.2 us (32%)
  blocking collectives  23.5 us (12%)
  matrix products  15.3 us (8%)
  local copies, waits for them, and re-layouts  6.72 us (3%)
  other arithmetic  6.08 us (3%)
    all_to_all x3, waiting for transfers between devices, exchange(): lax.all_to_all(blocks, CHIPS, split_axis=0, concat_axis=0, tiled=True)  69.8 us
    all_to_all x3, starting transfers between devices, exchange(): lax.all_to_all(blocks, CHIPS, split_axis=0, concat_axis=0, tiled=True)  35.9 us
    ppermute x6, starting transfers between devices, swap(): return lax.ppermute(value, 'core', SWAP)  26.3 us
    all_to_all x1, blocking collectives, exchange(): lax.all_to_all(blocks, CHIPS, split_axis=0, concat_axis=0, tiled=True)  23.5 us
    dot_general x11, matrix products, dot(): return jnp.einsum(spec, left, right, preferred_element_type=F32)  15.3 us
    ppermute x6, waiting for transfers between devices, swap(): return lax.ppermute(value, 'core', SWAP)  7.72 us
  transfers between devices with their start and end apart: 9, of which 8 were waited for; matrix products, arithmetic and copies ran while one was open for 4% of the time, Pallas kernels for 0%

profile of v3, /device:TPU:1, one launch (start us, length us, event | category | flops | bytes accessed | tf_op | source)
XLA Modules:
  0.0 192.3 jit_solution(5783385913288438371)
XLA Ops:
  0.7 1.0 copy-done
  1.7 1.3 fusion.42
  3.7 8.8 %collective-permute-start = (bf16[64,1280]{1,0:T(8,128)(2,1)S(1)}, bf16[64,1280]{1,0:T(8,128)(2,1)S(1)}, u32[]{:S(2)}, u32[]{:S(2)}) collective-permute-start(bf16[64,1280]{1,0:T(8,128)(2,1)S(1)} %get-tuple-element.28), channel_id=1, source_target_pairs={{0,64},{64,0},{1,65},{65,1},{2,66},{66,2},{3,67},{67,3},{4,68},{68... | collective-permute-start | bytes 491528 | tf_op jit(solution)/shard_map/ppermute | solution.py:23
  12.5 1.0 collective-permute-done
  13.9 1.8 broadcast_in_dim.10
  15.7 17.1 %all-to-all-start = ((bf16[256,2,1280]{2,1,0:T(2,128)(2,1)}), bf16[256,2,1280]{2,1,0:T(2,128)(2,1)S(1)}, u32[]{:S(2)}, u32[]{:S(2)}) async-start(bf16[256,2,1280]{2,1,0:T(2,128)(2,1)} %bitcast.4), calls=%async_computation | async-start | bytes 2621440 | tf_op jit(solution)/shard_map/all_to_all | solution.py:19
  33.0 2.6 %collective-permute-start.1 = (bf16[320,1280]{1,0:T(8,128)(2,1)S(1)}, bf16[320,1280]{1,0:T(8,128)(2,1)S(1)}, u32[]{:S(2)}, u32[]{:S(2)}) collective-permute-start(bf16[320,1280]{1,0:T(8,128)(2,1)S(1)} %select_bitcast_fusion.2), channel_id=1, source_target_pairs={{0,64},{64,0},{1,65},{65,1},{2,66},{66,2},{3,67},{67,3},{4,68},{68... | collective-permute-start | bytes 2457608 | tf_op jit(solution)/shard_map/ppermute | solution.py:23
  35.5 1.9 %collective-permute-done.1 = bf16[320,1280]{1,0:T(8,128)(2,1)S(1)} collective-permute-done((bf16[320,1280]{1,0:T(8,128)(2,1)S(1)}, bf16[320,1280]{1,0:T(8,128)(2,1)S(1)}, u32[]{:S(2)}, u32[]{:S(2)}) %collective-permute-start.1) | collective-permute-done | bytes 819232 | tf_op jit(solution)/shard_map/ppermute | solution.py:23
  37.5 1.3 bitcast_select_fusion.1
  38.8 29.8 %all-to-all-done = bf16[256,2,1280]{2,1,0:T(2,128)(2,1)S(1)} async-done(((bf16[256,2,1280]{2,1,0:T(2,128)(2,1)}), bf16[256,2,1280]{2,1,0:T(2,128)(2,1)S(1)}, u32[]{:S(2)}, u32[]{:S(2)}) %all-to-all-start) | async-done | bytes 1310752 | tf_op jit(solution)/shard_map/all_to_all | solution.py:19
  68.6 0.5 reshape.49
  69.1 3.9 %fusion.12 = (bf16[512,640]{1,0:T(8,128)(2,1)S(1)}, f32[512,640]{1,0:T(8,128)}) fusion(pred[]{:T(512)S(6)} %eq.3, bf16[512,1280]{1,0:T(8,128)(2,1)S(1)} %reshape.49, bf16[320,1280]{1,0:T(8,128)(2,1)} %get-tuple-element.18, bf16[320,1280]{1,0:T(8,128)(2,1)} %get-tuple-element.17), kind=kOutput, calls=%fused_computation.24 | convolution fusion | flops 845414400 | bytes 4915201 | tf_op jit(solution)/shard_map/id,hd->ih/dot_general | solution.py:27
  73.0 4.3 %collective-permute-start.2 = (bf16[512,640]{1,0:T(8,128)(2,1)S(1)}, bf16[512,640]{1,0:T(8,128)(2,1)}, u32[]{:S(2)}, u32[]{:S(2)}) collective-permute-start(bf16[512,640]{1,0:T(8,128)(2,1)S(1)} %get-tuple-element.30), channel_id=1, source_target_pairs={{0,64},{64,0},{1,65},{65,1},{2,66},{66,2},{3,67},{67,3},{4,68},{68... | collective-permute-start | bytes 1966088 | tf_op jit(solution)/shard_map/ppermute | solution.py:23
  77.2 1.8 collective-permute-done.2
  79.1 3.8 %convolution_convert_fusion.1 = bf16[512,1280]{1,0:T(8,128)(2,1)S(1)} fusion(bf16[320,1280]{1,0:T(8,128)(2,1)S(1)} %copy-done.8, bf16[320,1280]{1,0:T(8,128)(2,1)S(1)} %copy-done.7, bf16[512,640]{1,0:T(8,128)(2,1)} %collective-permute-done.2, f32[512,640]{1,0:T(8,128)} %get-tuple-element.31, pred[]{:T(512)S(6)} %eq.3), kind=kOutput, calls=%fused_computation.1 | convolution fusion | flops 850001920 | bytes 4915201 | tf_op jit(solution)/shard_map/ih,hd->id/dot_general | solution.py:27
  82.8 1.4 reshape.50
  84.2 9.4 %all-to-all-start.1 = ((bf16[256,2,1280]{2,1,0:T(2,128)(2,1)}), bf16[256,2,1280]{2,1,0:T(2,128)(2,1)S(1)}, u32[]{:S(2)}, u32[]{:S(2)}) async-start(bf16[256,2,1280]{2,1,0:T(2,128)(2,1)} %reshape.50), calls=%async_computation.1 | async-start | bytes 2621440 | tf_op jit(solution)/shard_map/all_to_all | solution.py:19
  93.6 3.5 %convolution_convert_fusion = bf16[640,1280]{1,0:T(8,128)(2,1)S(1)} fusion(bf16[512,1280]{1,0:T(8,128)(2,1)S(1)} %reshape.49, bf16[512,640]{1,0:T(8,128)(2,1)} %collective-permute-done.2, f32[512,640]{1,0:T(8,128)} %get-tuple-element.31, pred[]{:T(512)S(6)} %eq.3), kind=kOutput, calls=%fused_computation | convolution fusion | flops 846888960 | bytes 4915201 | tf_op jit(solution)/shard_map/ih,id->hd/dot_general | solution.py:27
  97.2 2.3 %collective-permute-start.3 = (bf16[320,1280]{1,0:T(8,128)(2,1)S(1)}, bf16[320,1280]{1,0:T(8,128)(2,1)S(1)}, u32[]{:S(2)}, u32[]{:S(2)}) collective-permute-start(bf16[320,1280]{1,0:T(8,128)(2,1)S(1)} %get-tuple-element.21), channel_id=1, source_target_pairs={{0,64},{64,0},{1,65},{65,1},{2,66},{66,2},{3,67},{67,3},{4,68},{68... | collective-permute-start | bytes 2457608 | tf_op jit(solution)/shard_map/ppermute | solution.py:23
  99.5 1.9 %collective-permute-done.3 = bf16[320,1280]{1,0:T(8,128)(2,1)S(1)} collective-permute-done((bf16[320,1280]{1,0:T(8,128)(2,1)S(1)}, bf16[320,1280]{1,0:T(8,128)(2,1)S(1)}, u32[]{:S(2)}, u32[]{:S(2)}) %collective-permute-start.3) | collective-permute-done | bytes 819232 | tf_op jit(solution)/shard_map/ppermute | solution.py:23
  101.5 28.3 %all-to-all-done.1 = bf16[256,2,1280]{2,1,0:T(2,128)(2,1)S(1)} async-done(((bf16[256,2,1280]{2,1,0:T(2,128)(2,1)}), bf16[256,2,1280]{2,1,0:T(2,128)(2,1)S(1)}, u32[]{:S(2)}, u32[]{:S(2)}) %all-to-all-start.1) | async-done | bytes 1310752 | tf_op jit(solution)/shard_map/all_to_all | solution.py:19
  129.7 1.8 reduce_sum.62
  132.1 4.0 %collective-permute-start.4 = (bf16[64,1280]{1,0:T(8,128)(2,1)S(1)}, bf16[64,1280]{1,0:T(8,128)(2,1)S(1)}, u32[]{:S(2)}, u32[]{:S(2)}) collective-permute-start(bf16[64,1280]{1,0:T(8,128)(2,1)S(1)} %select_bitcast_fusion.3), channel_id=1, source_target_pairs={{0,64},{64,0},{1,65},{65,1},{2,66},{66,2},{3,67},{67,3},{4,68},{68... | collective-permute-start | bytes 491528 | tf_op jit(solution)/shard_map/ppermute | solution.py:23
  136.1 1.0 collective-permute-done.4
  138.4 23.5 %all_to_all.20 = bf16[256,4,128]{2,1,0:T(4,128)(2,1)S(1)} all-to-all(bf16[256,4,128]{2,1,0:T(4,128)(2,1)S(1)} %concatenate.7), channel_id=1, replica_groups=mesh['y_lo'=4,'core'=2,'y_hi'=2,'x'=4,'z'=8] {'y_lo','y_hi','x','z'}, dimensions={0} | all-to-all | bytes 524288 | tf_op jit(solution)/shard_map/all_to_all | solution.py:19
  162.2 0.8 broadcast_in_dim.12
  163.0 9.4 %all-to-all-start.3 = ((bf16[256,4,128]{2,1,0:T(4,128)(2,1)}), bf16[256,4,128]{2,1,0:T(4,128)(2,1)S(1)}, u32[]{:S(2)}, u32[]{:S(2)}) async-start(bf16[256,4,128]{2,1,0:T(4,128)(2,1)} %broadcast_in_dim.12), calls=%async_computation.3 | async-start | bytes 524288 | tf_op jit(solution)/shard_map/all_to_all | solution.py:19
  172.4 1.3 select_bitcast_fusion
  173.7 11.8 %all-to-all-done.3 = bf16[256,4,128]{2,1,0:T(4,128)(2,1)S(1)} async-done(((bf16[256,4,128]{2,1,0:T(4,128)(2,1)}), bf16[256,4,128]{2,1,0:T(4,128)(2,1)S(1)}, u32[]{:S(2)}, u32[]{:S(2)}) %all-to-all-start.3) | async-done | bytes 262176 | tf_op jit(solution)/shard_map/all_to_all | solution.py:19
  185.7 4.4 %collective-permute-start.5 = (bf16[64,1280]{1,0:T(8,128)(2,1)S(1)}, bf16[64,1280]{1,0:T(8,128)(2,1)S(1)}, u32[]{:S(2)}, u32[]{:S(2)}) collective-permute-start(bf16[64,1280]{1,0:T(8,128)(2,1)S(1)} %bitcast.84), channel_id=1, source_target_pairs={{0,64},{64,0},{1,65},{65,1},{2,66},{66,2},{3,67},{67,3},{4,68},{68... | collective-permute-start | bytes 491528 | tf_op jit(solution)/shard_map/ppermute | solution.py:23
  190.4 1.2 fusion.1
  191.6 0.7 fusion.26
  (50 shorter events, 3.9 us)
Async XLA Ops:
  0.6 1.0 copy-start
  0.6 2.8 %copy-start.12 = (bf16[1,192,1280]{2,1,0:T(8,128)(2,1)S(1)}, bf16[1,192,1280]{2,1,0:T(8,128)(2,1)}, u32[]{:S(2)}) copy-start(bf16[1,192,1280]{2,1,0:T(8,128)(2,1)} %param.6) | copy-start | bytes 1474564
  3.5 10.5 %copy-start.3 = (bf16[64,1280]{1,0:T(8,128)(2,1)}, bf16[64,1280]{1,0:T(8,128)(2,1)S(1)}, u32[]{:S(2)}) copy-start(bf16[64,1280]{1,0:T(8,128)(2,1)S(1)} %convolution_convert_fusion.4) | copy-start | bytes 491524
  3.7 9.8 %collective-permute-start = (bf16[64,1280]{1,0:T(8,128)(2,1)S(1)}, bf16[64,1280]{1,0:T(8,128)(2,1)S(1)}, u32[]{:S(2)}, u32[]{:S(2)}) collective-permute-start(bf16[64,1280]{1,0:T(8,128)(2,1)S(1)} %get-tuple-element.28), channel_id=1, source_target_pairs={{0,64},{64,0},{1,65},{65,1},{2,66},{66,2},{3,67},{67,3},{4,68},{68... | collective-permute-start | bytes 491528 | tf_op jit(solution)/shard_map/ppermute | solution.py:23
  15.7 17.1 %copy-start.1 = (bf16[1,320,1280]{2,1,0:T(8,128)(2,1)S(1)}, bf16[1,320,1280]{2,1,0:T(8,128)(2,1)}, u32[]{:S(2)}) copy-start(bf16[1,320,1280]{2,1,0:T(8,128)(2,1)} %param.9) | copy-start | bytes 2457604
  15.7 17.2 %copy-start.2 = (bf16[1,320,1280]{2,1,0:T(8,128)(2,1)S(1)}, bf16[1,320,1280]{2,1,0:T(8,128)(2,1)}, u32[]{:S(2)}) copy-start(bf16[1,320,1280]{2,1,0:T(8,128)(2,1)} %param.8) | copy-start | bytes 2457604
  15.7 52.9 %all-to-all-start = ((bf16[256,2,1280]{2,1,0:T(2,128)(2,1)}), bf16[256,2,1280]{2,1,0:T(2,128)(2,1)S(1)}, u32[]{:S(2)}, u32[]{:S(2)}) async-start(bf16[256,2,1280]{2,1,0:T(2,128)(2,1)} %bitcast.4), calls=%async_computation | async-start | bytes 2621440 | tf_op jit(solution)/shard_map/all_to_all | solution.py:19
  33.0 4.5 %collective-permute-start.1 = (bf16[320,1280]{1,0:T(8,128)(2,1)S(1)}, bf16[320,1280]{1,0:T(8,128)(2,1)S(1)}, u32[]{:S(2)}, u32[]{:S(2)}) collective-permute-start(bf16[320,1280]{1,0:T(8,128)(2,1)S(1)} %select_bitcast_fusion.2), channel_id=1, source_target_pairs={{0,64},{64,0},{1,65},{65,1},{2,66},{66,2},{3,67},{67,3},{4,68},{68... | collective-permute-start | bytes 2457608 | tf_op jit(solution)/shard_map/ppermute | solution.py:23
  69.1 10.0 %copy-start.7 = (bf16[320,1280]{1,0:T(8,128)(2,1)S(1)}, bf16[320,1280]{1,0:T(8,128)(2,1)}, u32[]{:S(2)}) copy-start(bf16[320,1280]{1,0:T(8,128)(2,1)} %get-tuple-element.17) | copy-start | bytes 2457604
  69.1 10.0 %copy-start.8 = (bf16[320,1280]{1,0:T(8,128)(2,1)S(1)}, bf16[320,1280]{1,0:T(8,128)(2,1)}, u32[]{:S(2)}) copy-start(bf16[320,1280]{1,0:T(8,128)(2,1)} %get-tuple-element.18) | copy-start | bytes 2457604
  73.0 6.1 %collective-permute-start.2 = (bf16[512,640]{1,0:T(8,128)(2,1)S(1)}, bf16[512,640]{1,0:T(8,128)(2,1)}, u32[]{:S(2)}, u32[]{:S(2)}) collective-permute-start(bf16[512,640]{1,0:T(8,128)(2,1)S(1)} %get-tuple-element.30), channel_id=1, source_target_pairs={{0,64},{64,0},{1,65},{65,1},{2,66},{66,2},{3,67},{67,3},{4,68},{68... | collective-permute-start | bytes 1966088 | tf_op jit(solution)/shard_map/ppermute | solution.py:23
  84.2 45.5 %all-to-all-start.1 = ((bf16[256,2,1280]{2,1,0:T(2,128)(2,1)}), bf16[256,2,1280]{2,1,0:T(2,128)(2,1)S(1)}, u32[]{:S(2)}, u32[]{:S(2)}) async-start(bf16[256,2,1280]{2,1,0:T(2,128)(2,1)} %reshape.50), calls=%async_computation.1 | async-start | bytes 2621440 | tf_op jit(solution)/shard_map/all_to_all | solution.py:19
  97.2 4.2 %collective-permute-start.3 = (bf16[320,1280]{1,0:T(8,128)(2,1)S(1)}, bf16[320,1280]{1,0:T(8,128)(2,1)S(1)}, u32[]{:S(2)}, u32[]{:S(2)}) collective-permute-start(bf16[320,1280]{1,0:T(8,128)(2,1)S(1)} %get-tuple-element.21), channel_id=1, source_target_pairs={{0,64},{64,0},{1,65},{65,1},{2,66},{66,2},{3,67},{67,3},{4,68},{68... | collective-permute-start | bytes 2457608 | tf_op jit(solution)/shard_map/ppermute | solution.py:23
  101.5 28.3 %copy-start.5 = (bf16[320,1280]{1,0:T(8,128)(2,1)}, bf16[320,1280]{1,0:T(8,128)(2,1)S(1)}, u32[]{:S(2)}) copy-start(bf16[320,1280]{1,0:T(8,128)(2,1)S(1)} %collective-permute-done.3) | copy-start | bytes 2457604
  131.5 5.5 %copy-start.4 = (bf16[64,1280]{1,0:T(8,128)(2,1)S(1)}, bf16[64,1280]{1,0:T(8,128)(2,1)}, u32[]{:S(2)}) copy-start(bf16[64,1280]{1,0:T(8,128)(2,1)} %copy-done.3) | copy-start | bytes 491524
  132.0 5.3 %copy-start.13 = (bf16[1,192,1280]{2,1,0:T(8,128)(2,1)S(1)}, bf16[1,192,1280]{2,1,0:T(8,128)(2,1)}, u32[]{:S(2)}) copy-start(bf16[1,192,1280]{2,1,0:T(8,128)(2,1)} %param.6) | copy-start | bytes 1474564
  132.1 5.0 %collective-permute-start.4 = (bf16[64,1280]{1,0:T(8,128)(2,1)S(1)}, bf16[64,1280]{1,0:T(8,128)(2,1)S(1)}, u32[]{:S(2)}, u32[]{:S(2)}) collective-permute-start(bf16[64,1280]{1,0:T(8,128)(2,1)S(1)} %select_bitcast_fusion.3), channel_id=1, source_target_pairs={{0,64},{64,0},{1,65},{65,1},{2,66},{66,2},{3,67},{67,3},{4,68},{68... | collective-permute-start | bytes 491528 | tf_op jit(solution)/shard_map/ppermute | solution.py:23
  137.3 0.9 copy-start.10
  138.3 34.2 %copy-start.6 = (bf16[320,1280]{1,0:T(8,128)(2,1)S(1)}, bf16[320,1280]{1,0:T(8,128)(2,1)}, u32[]{:S(2)}) copy-start(bf16[320,1280]{1,0:T(8,128)(2,1)} %copy-done.5) | copy-start | bytes 2457604
  163.0 22.5 %all-to-all-start.3 = ((bf16[256,4,128]{2,1,0:T(4,128)(2,1)}), bf16[256,4,128]{2,1,0:T(4,128)(2,1)S(1)}, u32[]{:S(2)}, u32[]{:S(2)}) async-start(bf16[256,4,128]{2,1,0:T(4,128)(2,1)} %broadcast_in_dim.12), calls=%async_computation.3 | async-start | bytes 524288 | tf_op jit(solution)/shard_map/all_to_all | solution.py:19
  172.4 17.7 %copy-start.9 = (bf16[1280,64]{0,1:T(8,128)(2,1)S(1)}, bf16[1280,64]{0,1:T(8,128)(2,1)}, u32[]{:S(2)}) copy-start(bf16[1280,64]{0,1:T(8,128)(2,1)} %param.7) | copy-start | bytes 491524
  173.7 16.7 %copy-start.11 = (bf16[64,1280]{1,0:T(8,128)(2,1)S(1)}, bf16[64,1280]{1,0:T(8,128)(2,1)}, u32[]{:S(2)}) copy-start(bf16[64,1280]{1,0:T(8,128)(2,1)} %copy-done.10) | copy-start | bytes 491524
  185.7 5.9 %collective-permute-start.5 = (bf16[64,1280]{1,0:T(8,128)(2,1)S(1)}, bf16[64,1280]{1,0:T(8,128)(2,1)S(1)}, u32[]{:S(2)}, u32[]{:S(2)}) collective-permute-start(bf16[64,1280]{1,0:T(8,128)(2,1)S(1)} %bitcast.84), channel_id=1, source_target_pairs={{0,64},{64,0},{1,65},{65,1},{2,66},{66,2},{3,67},{67,3},{4,68},{68... | collective-permute-start | bytes 491528 | tf_op jit(solution)/shard_map/ppermute | solution.py:23

commit v4 on v3

--- a/solution.py
+++ b/solution.py
@@ -7,6 +7,8 @@
 DP = ("y_lo", "core")
 EXPERT = ("y_hi", "x", "z")
 CHIPS = ("y_lo",) + EXPERT
+PLANE = ("x", "z")
+LINE = ("y_lo", "core", "y_hi")
 BF = jnp.bfloat16
 F32 = jnp.float32
 
@@ -15,8 +17,8 @@
     return jax.vjp(jax.nn.gelu, preact)[1](upstream)[0]
 
 
-def exchange(blocks):
-    return lax.all_to_all(blocks, CHIPS, split_axis=0, concat_axis=0, tiled=True)
+def exchange(blocks, axes):
+    return lax.all_to_all(blocks, axes, split_axis=0, concat_axis=0, tiled=True)
 
 
 def swap(value):
@@ -46,19 +48,23 @@
         [jnp.where(first, own_in, got), jnp.where(first, got, own_grad)], axis=1
     )
     blocks = jnp.broadcast_to(pair[None], (4, 64, 2, 1280)).reshape(256, 2, 1280)
-    rows = exchange(blocks).reshape(512, 1280)
+    rows = exchange(blocks, CHIPS).reshape(512, 1280)
     act = dot("id,hd->ih", rows, weight)
     other = swap(jnp.where(first, jax.nn.gelu(act), act).astype(BF))
     hid = jnp.where(first, gelu_back(act, other.astype(F32)).astype(BF), other)
     partial = dot("ih,hd->id", hid, weight).astype(BF)
     d_weight = dot("ih,id->hd", hid, rows).astype(BF)
-    parts = exchange(partial.reshape(256, 2, 1280)).reshape(4, 64, 2, 1280)
+    parts = exchange(partial.reshape(256, 2, 1280), CHIPS).reshape(512, 1280)
     d_kept = jnp.where(first, d_weight[:320], d_weight[320:])
     d_got = swap(jnp.where(first, d_weight[320:], d_weight[:320]))
     parts, d_kept, d_got = lax.optimization_barrier((parts, d_kept, d_got))
-    back = jnp.sum(parts.astype(F32), axis=0).astype(BF)
-    kept = jnp.where(first, back[:, 0], back[:, 1])
-    got = swap(jnp.where(first, back[:, 1], back[:, 0]))
+    row = lax.broadcasted_iota(jnp.int32, (128, 512), 0)
+    col = lax.broadcasted_iota(jnp.int32, (128, 512), 1)
+    image = jnp.where(first, row // 64, 1 - row // 64)
+    adder = (col % 128 == (row % 64) * 2 + image).astype(BF)
+    back = dot("sr,rd->sd", adder, parts).astype(BF)
+    kept = back[:64]
+    got = swap(back[64:])
     slot_in_grad = jnp.where(first, kept, got)
     slot_out = jnp.where(first, got, kept)
     slot_stat = jnp.sum(own_in.astype(F32) * slot_in_grad.astype(F32), axis=1)
@@ -72,12 +78,11 @@
         dot("ms,ds->md", logit_grad, router) + dot("ms,sd->md", dispatch_cast, slot_in_grad)
     ).astype(BF)
     term = dot("ms,md->sd", logit_grad, tokens).astype(BF)
-    term = term.reshape(16, 4, 10, 128).swapaxes(1, 2).reshape(160, 4, 128)
-    term = jnp.concatenate([term, jnp.zeros((96, 4, 128), BF)])
-    piece = jnp.sum(exchange(term).astype(F32), axis=0).astype(BF)
-    pieces = exchange(jnp.broadcast_to(piece[None], (256, 4, 128)))
-    total = pieces[:160].reshape(16, 10, 4, 128).swapaxes(1, 2).reshape(64, 1280)
-    d_router = (total.astype(F32) + swap(total).astype(F32)).astype(BF).T
+    term = jnp.sum(exchange(term.reshape(32, 2, 1280), PLANE).astype(F32), axis=0).astype(BF)
+    term = exchange(jnp.broadcast_to(term[None], (16, 2, 1280)), LINE)
+    term = jnp.sum(term.astype(F32), axis=0).astype(BF)
+    term = exchange(jnp.broadcast_to(term[None], (32, 2, 1280)), PLANE)
+    d_router = term.reshape(64, 1280).T
     d_w_in = jnp.where(first, d_kept, d_got)
     d_w_out = jnp.where(first, d_got, d_kept)
     return (d_tokens[None], d_router, d_w_in[None], d_w_out[None])

time: 193 us -> 180 us (0.933)
  blocking collectives: 23.5 us -> 12.2 us
  starting transfers between devices: 62.2 us -> 58.1 us
  local copies, waits for them, and re-layouts: 6.72 us -> 8.65 us
    all_to_all x1, blocking collectives: 23.5 us -> 12.2 us  [exchange(): return lax.all_to_all(blocks, axes, split_axis=0, concat_axis=0, tiled=True)]
    ppermute x6 -> x5, starting transfers between devices: 26.3 us -> 21.7 us  [swap(): return lax.ppermute(value, 'core', SWAP)]
    all_to_all x3 -> x4, waiting for transfers between devices: 69.8 us -> 73 us  [exchange(): return lax.all_to_all(blocks, axes, split_axis=0, concat_axis=0, tiled=True)]
    reshape x3 -> x5, local copies, waits for them, and re-layouts: 2 us -> 4.05 us  [the longest x2 2.73 us: local(): parts = exchange(partial.reshape(256, 2, 1280), CHIPS).reshape(512, 1280)]
    ppermute x6 -> x5, waiting for transfers between devices: 7.72 us -> 5.79 us  [swap(): return lax.ppermute(value, 'core', SWAP)]
    all_to_all x3 -> x4, starting transfers between devices: 35.9 us -> 36.4 us  [exchange(): return lax.all_to_all(blocks, axes, split_axis=0, concat_axis=0, tiled=True)]
    dot_general x11 -> x12, matrix products: 15.3 us -> 15.7 us  [dot(): return jnp.einsum(spec, left, right, preferred_element_type=F32)]
  transfers between devices with their start and end apart: 9 -> 9, of which waited for: 8 -> 8; matrix products, arithmetic and copies ran while one was open for 4% -> 6% of each run, Pallas kernels for 0% -> 0%
where the time goes in v4:
time: 180 us; the launch traced here: 179 us
  waiting for transfers between devices  78.8 us (44%)
  starting transfers between devices  58.1 us (32%)
  matrix products  15.7 us (9%)
  blocking collectives  12.2 us (7%)
  local copies, waits for them, and re-layouts  8.65 us (5%)
  other arithmetic  4.87 us (3%)
    all_to_all x4, waiting for transfers between devices, exchange(): return lax.all_to_all(blocks, axes, split_axis=0, concat_axis=0, tiled=True)  73 us
    all_to_all x4, starting transfers between devices, exchange(): return lax.all_to_all(blocks, axes, split_axis=0, concat_axis=0, tiled=True)  36.4 us
    ppermute x5, starting transfers between devices, swap(): return lax.ppermute(value, 'core', SWAP)  21.7 us
    dot_general x12, matrix products, dot(): return jnp.einsum(spec, left, right, preferred_element_type=F32)  15.7 us
    all_to_all x1, blocking collectives, exchange(): return lax.all_to_all(blocks, axes, split_axis=0, concat_axis=0, tiled=True)  12.2 us
    ppermute x5, waiting for transfers between devices, swap(): return lax.ppermute(value, 'core', SWAP)  5.79 us
  transfers between devices with their start and end apart: 9, of which 8 were waited for; matrix products, arithmetic and copies ran while one was open for 6% of the time, Pallas kernels for 0%

profile of v4, /device:TPU:1, one launch (start us, length us, event | category | flops | bytes accessed | tf_op | source)
XLA Modules:
  0.0 179.3 jit_solution(3064477949362165873)
XLA Ops:
  0.7 1.0 copy-done
  1.7 1.3 fusion.64
  3.7 8.8 %collective-permute-start = (bf16[64,1280]{1,0:T(8,128)(2,1)S(1)}, bf16[64,1280]{1,0:T(8,128)(2,1)S(1)}, u32[]{:S(2)}, u32[]{:S(2)}) collective-permute-start(bf16[64,1280]{1,0:T(8,128)(2,1)S(1)} %get-tuple-element.25), channel_id=1, source_target_pairs={{0,64},{64,0},{1,65},{65,1},{2,66},{66,2},{3,67},{67,3},{4,68},{68... | collective-permute-start | bytes 491528 | tf_op jit(solution)/shard_map/ppermute | solution.py:25
  12.5 1.0 collective-permute-done
  13.9 1.8 broadcast_in_dim.12
  15.7 17.1 %all-to-all-start = ((bf16[256,2,1280]{2,1,0:T(2,128)(2,1)}), bf16[256,2,1280]{2,1,0:T(2,128)(2,1)S(1)}, u32[]{:S(2)}, u32[]{:S(2)}) async-start(bf16[256,2,1280]{2,1,0:T(2,128)(2,1)} %bitcast.4), calls=%async_computation | async-start | bytes 2621440 | tf_op jit(solution)/shard_map/all_to_all | solution.py:21
  32.9 2.6 %collective-permute-start.1 = (bf16[320,1280]{1,0:T(8,128)(2,1)S(1)}, bf16[320,1280]{1,0:T(8,128)(2,1)S(1)}, u32[]{:S(2)}, u32[]{:S(2)}) collective-permute-start(bf16[320,1280]{1,0:T(8,128)(2,1)S(1)} %select_bitcast_fusion.2), channel_id=1, source_target_pairs={{0,64},{64,0},{1,65},{65,1},{2,66},{66,2},{3,67},{67,3},{4,68},{68... | collective-permute-start | bytes 2457608 | tf_op jit(solution)/shard_map/ppermute | solution.py:25
  35.5 1.9 %collective-permute-done.1 = bf16[320,1280]{1,0:T(8,128)(2,1)S(1)} collective-permute-done((bf16[320,1280]{1,0:T(8,128)(2,1)S(1)}, bf16[320,1280]{1,0:T(8,128)(2,1)S(1)}, u32[]{:S(2)}, u32[]{:S(2)}) %collective-permute-start.1) | collective-permute-done | bytes 819232 | tf_op jit(solution)/shard_map/ppermute | solution.py:25
  37.4 1.3 bitcast_select_fusion.1
  38.8 29.8 %all-to-all-done = bf16[256,2,1280]{2,1,0:T(2,128)(2,1)S(1)} async-done(((bf16[256,2,1280]{2,1,0:T(2,128)(2,1)}), bf16[256,2,1280]{2,1,0:T(2,128)(2,1)S(1)}, u32[]{:S(2)}, u32[]{:S(2)}) %all-to-all-start) | async-done | bytes 1310752 | tf_op jit(solution)/shard_map/all_to_all | solution.py:21
  69.1 2.9 %fusion.12 = (bf16[512,640]{1,0:T(8,128)(2,1)S(1)}, f32[512,640]{1,0:T(8,128)S(1)}) fusion(pred[]{:T(512)S(6)} %eq.9, bf16[512,1280]{1,0:T(8,128)(2,1)S(1)} %reshape.40, bf16[320,1280]{1,0:T(8,128)(2,1)} %get-tuple-element.17, bf16[320,1280]{1,0:T(8,128)(2,1)} %get-tuple-element.16), kind=kOutput, calls=%fused_computation.25 | convolution fusion | flops 845414400 | bytes 4915201 | tf_op jit(solution)/shard_map/id,hd->ih/dot_general | solution.py:29
  72.0 4.3 %collective-permute-start.2 = (bf16[512,640]{1,0:T(8,128)(2,1)S(1)}, bf16[512,640]{1,0:T(8,128)(2,1)}, u32[]{:S(2)}, u32[]{:S(2)}) collective-permute-start(bf16[512,640]{1,0:T(8,128)(2,1)S(1)} %get-tuple-element.27), channel_id=1, source_target_pairs={{0,64},{64,0},{1,65},{65,1},{2,66},{66,2},{3,67},{67,3},{4,68},{68... | collective-permute-start | bytes 1966088 | tf_op jit(solution)/shard_map/ppermute | solution.py:25
  76.3 1.8 %collective-permute-done.2 = bf16[512,640]{1,0:T(8,128)(2,1)} collective-permute-done((bf16[512,640]{1,0:T(8,128)(2,1)S(1)}, bf16[512,640]{1,0:T(8,128)(2,1)}, u32[]{:S(2)}, u32[]{:S(2)}) %collective-permute-start.2) | collective-permute-done | bytes 655392 | tf_op jit(solution)/shard_map/ppermute | solution.py:25
  78.1 3.3 %convolution_convert_fusion.1 = bf16[512,1280]{1,0:T(8,128)(2,1)S(1)} fusion(bf16[320,1280]{1,0:T(8,128)(2,1)S(1)} %copy-done.6, bf16[320,1280]{1,0:T(8,128)(2,1)S(1)} %copy-done.5, bf16[512,640]{1,0:T(8,128)(2,1)} %collective-permute-done.2, f32[512,640]{1,0:T(8,128)S(1)} %get-tuple-element.28, pred[]{:T(512)S(6)} %eq.9), kind=kOutput, calls=%fused_computation.1 | convolution fusion | flops 850001920 | bytes 4915201 | tf_op jit(solution)/shard_map/ih,hd->id/dot_general | solution.py:29
  81.5 1.4 reshape.41
  82.8 9.4 %all-to-all-start.1 = ((bf16[256,2,1280]{2,1,0:T(2,128)(2,1)}), bf16[256,2,1280]{2,1,0:T(2,128)(2,1)S(1)}, u32[]{:S(2)}, u32[]{:S(2)}) async-start(bf16[256,2,1280]{2,1,0:T(2,128)(2,1)} %reshape.41), calls=%async_computation.1 | async-start | bytes 2621440 | tf_op jit(solution)/shard_map/all_to_all | solution.py:21
  92.2 3.5 %convolution_convert_fusion = bf16[640,1280]{1,0:T(8,128)(2,1)S(1)} fusion(bf16[512,1280]{1,0:T(8,128)(2,1)S(1)} %reshape.40, bf16[512,640]{1,0:T(8,128)(2,1)} %collective-permute-done.2, f32[512,640]{1,0:T(8,128)} %copy-done.10, pred[]{:T(512)S(6)} %eq.9), kind=kOutput, calls=%fused_computation | convolution fusion | flops 846888960 | bytes 4915201 | tf_op jit(solution)/shard_map/ih,id->hd/dot_general | solution.py:29
  95.7 1.0 broadcast_select_fusion.1
  96.7 2.3 %collective-permute-start.3 = (bf16[320,1280]{1,0:T(8,128)(2,1)}, bf16[320,1280]{1,0:T(8,128)(2,1)S(1)}, u32[]{:S(2)}, u32[]{:S(2)}) collective-permute-start(bf16[320,1280]{1,0:T(8,128)(2,1)} %get-tuple-element.20), channel_id=1, source_target_pairs={{0,64},{64,0},{1,65},{65,1},{2,66},{66,2},{3,67},{67,3},{4,68},{68... | collective-permute-start | bytes 2457608 | tf_op jit(solution)/shard_map/ppermute | solution.py:25
  99.6 28.8 %all-to-all-done.1 = bf16[256,2,1280]{2,1,0:T(2,128)(2,1)S(1)} async-done(((bf16[256,2,1280]{2,1,0:T(2,128)(2,1)}), bf16[256,2,1280]{2,1,0:T(2,128)(2,1)S(1)}, u32[]{:S(2)}, u32[]{:S(2)}) %all-to-all-start.1) | async-done | bytes 1310752 | tf_op jit(solution)/shard_map/all_to_all | solution.py:21
  128.3 1.4 reshape.42
  129.7 1.8 %convolution_convert_fusion.2 = bf16[128,1280]{1,0:T(8,128)(2,1)S(1)} fusion(bf16[512,1280]{1,0:T(8,128)(2,1)} %reshape.42, s32[128]{0:T(128)S(1)} %get-tuple-element.35, s32[128]{0:T(128)S(1)} %get-tuple-element.37, s32[128]{0:T(128)S(1)} %get-tuple-element.36, s32[128]{0:T(128)S(1)} %get-tuple-element.38, s32[512]{0:T(512)S(1)} %get-tuple-element.31, ...), kind=kOutput, calls=%fused_computation.5 | convolution fusion | flops 168460288 | bytes 1645313 | tf_op jit(solution)/shard_map/sr,rd->sd/dot_general | solution.py:29
  131.6 3.8 %collective-permute-start.4 = (bf16[64,1280]{1,0:T(8,128)(2,1)S(1)}, bf16[64,1280]{1,0:T(8,128)(2,1)S(1)}, u32[]{:S(2)}, u32[]{:S(2)}) collective-permute-start(bf16[64,1280]{1,0:T(8,128)(2,1)S(1)} %slice.21), channel_id=1, source_target_pairs={{0,64},{64,0},{1,65},{65,1},{2,66},{66,2},{3,67},{67,3},{4,68},{68... | collective-permute-start | bytes 491528 | tf_op jit(solution)/shard_map/ppermute | solution.py:25
  135.4 1.0 collective-permute-done.4
  137.5 12.2 %all_to_all.25 = bf16[32,2,1280]{2,1,0:T(2,128)(2,1)S(1)} all-to-all(bf16[32,2,1280]{2,1,0:T(2,128)(2,1)S(1)} %reshape.43), channel_id=1, replica_groups=mesh['y_lo'=4,'core'=2,'y_hi'=2,'x'=4,'z'=8] {'x','z'}, dimensions={0} | all-to-all | bytes 327680 | tf_op jit(solution)/shard_map/all_to_all | solution.py:21
  150.6 6.0 %all-to-all-start.3 = ((bf16[16,2,1280]{2,1,0:T(2,128)(2,1)}), bf16[16,2,1280]{2,1,0:T(2,128)(2,1)S(1)}, u32[]{:S(2)}, u32[]{:S(2)}) async-start(bf16[16,2,1280]{2,1,0:T(2,128)(2,1)} %broadcast_in_dim.14), calls=%async_computation.3 | async-start | bytes 163840 | tf_op jit(solution)/shard_map/all_to_all | solution.py:21
  156.6 1.3 select_bitcast_fusion
  157.9 6.7 %all-to-all-done.3 = bf16[16,2,1280]{2,1,0:T(2,128)(2,1)S(1)} async-done(((bf16[16,2,1280]{2,1,0:T(2,128)(2,1)}), bf16[16,2,1280]{2,1,0:T(2,128)(2,1)S(1)}, u32[]{:S(2)}, u32[]{:S(2)}) %all-to-all-start.3) | async-done | bytes 81952 | tf_op jit(solution)/shard_map/all_to_all | solution.py:21
  164.7 0.8 broadcast_in_dim.15
  165.4 3.9 %all-to-all-start.4 = ((bf16[32,2,1280]{2,1,0:T(2,128)(2,1)}), bf16[32,2,1280]{2,1,0:T(2,128)(2,1)S(1)}, u32[]{:S(2)}, u32[]{:S(2)}) async-start(bf16[32,2,1280]{2,1,0:T(2,128)(2,1)} %broadcast_in_dim.15), calls=%async_computation.4 | async-start | bytes 327680 | tf_op jit(solution)/shard_map/all_to_all | solution.py:21
  169.6 1.2 fusion.1
  170.8 7.7 %all-to-all-done.4 = bf16[32,2,1280]{2,1,0:T(2,128)(2,1)S(1)} async-done(((bf16[32,2,1280]{2,1,0:T(2,128)(2,1)}), bf16[32,2,1280]{2,1,0:T(2,128)(2,1)S(1)}, u32[]{:S(2)}, u32[]{:S(2)}) %all-to-all-start.4) | async-done | bytes 163872 | tf_op jit(solution)/shard_map/all_to_all | solution.py:21
  (46 shorter events, 5.3 us)
Async XLA Ops:
  0.6 1.0 copy-start
  0.6 2.8 %copy-start.8 = (bf16[1,192,1280]{2,1,0:T(8,128)(2,1)S(1)}, bf16[1,192,1280]{2,1,0:T(8,128)(2,1)}, u32[]{:S(2)}) copy-start(bf16[1,192,1280]{2,1,0:T(8,128)(2,1)} %param.6) | copy-start | bytes 1474564
  3.5 10.5 %copy-start.3 = (bf16[64,1280]{1,0:T(8,128)(2,1)}, bf16[64,1280]{1,0:T(8,128)(2,1)S(1)}, u32[]{:S(2)}) copy-start(bf16[64,1280]{1,0:T(8,128)(2,1)S(1)} %convolution_convert_fusion.5) | copy-start | bytes 491524
  3.7 9.8 %collective-permute-start = (bf16[64,1280]{1,0:T(8,128)(2,1)S(1)}, bf16[64,1280]{1,0:T(8,128)(2,1)S(1)}, u32[]{:S(2)}, u32[]{:S(2)}) collective-permute-start(bf16[64,1280]{1,0:T(8,128)(2,1)S(1)} %get-tuple-element.25), channel_id=1, source_target_pairs={{0,64},{64,0},{1,65},{65,1},{2,66},{66,2},{3,67},{67,3},{4,68},{68... | collective-permute-start | bytes 491528 | tf_op jit(solution)/shard_map/ppermute | solution.py:25
  15.7 17.1 %copy-start.1 = (bf16[1,320,1280]{2,1,0:T(8,128)(2,1)S(1)}, bf16[1,320,1280]{2,1,0:T(8,128)(2,1)}, u32[]{:S(2)}) copy-start(bf16[1,320,1280]{2,1,0:T(8,128)(2,1)} %param.9) | copy-start | bytes 2457604
  15.7 17.2 %copy-start.2 = (bf16[1,320,1280]{2,1,0:T(8,128)(2,1)S(1)}, bf16[1,320,1280]{2,1,0:T(8,128)(2,1)}, u32[]{:S(2)}) copy-start(bf16[1,320,1280]{2,1,0:T(8,128)(2,1)} %param.8) | copy-start | bytes 2457604
  15.7 52.9 %all-to-all-start = ((bf16[256,2,1280]{2,1,0:T(2,128)(2,1)}), bf16[256,2,1280]{2,1,0:T(2,128)(2,1)S(1)}, u32[]{:S(2)}, u32[]{:S(2)}) async-start(bf16[256,2,1280]{2,1,0:T(2,128)(2,1)} %bitcast.4), calls=%async_computation | async-start | bytes 2621440 | tf_op jit(solution)/shard_map/all_to_all | solution.py:21
  32.9 4.5 %collective-permute-start.1 = (bf16[320,1280]{1,0:T(8,128)(2,1)S(1)}, bf16[320,1280]{1,0:T(8,128)(2,1)S(1)}, u32[]{:S(2)}, u32[]{:S(2)}) collective-permute-start(bf16[320,1280]{1,0:T(8,128)(2,1)S(1)} %select_bitcast_fusion.2), channel_id=1, source_target_pairs={{0,64},{64,0},{1,65},{65,1},{2,66},{66,2},{3,67},{67,3},{4,68},{68... | collective-permute-start | bytes 2457608 | tf_op jit(solution)/shard_map/ppermute | solution.py:25
  69.1 9.0 %copy-start.5 = (bf16[320,1280]{1,0:T(8,128)(2,1)S(1)}, bf16[320,1280]{1,0:T(8,128)(2,1)}, u32[]{:S(2)}) copy-start(bf16[320,1280]{1,0:T(8,128)(2,1)} %get-tuple-element.16) | copy-start | bytes 2457604
  69.1 9.0 %copy-start.6 = (bf16[320,1280]{1,0:T(8,128)(2,1)S(1)}, bf16[320,1280]{1,0:T(8,128)(2,1)}, u32[]{:S(2)}) copy-start(bf16[320,1280]{1,0:T(8,128)(2,1)} %get-tuple-element.17) | copy-start | bytes 2457604
  72.0 6.1 %copy-start.10 = (f32[512,640]{1,0:T(8,128)}, f32[512,640]{1,0:T(8,128)S(1)}, u32[]{:S(2)}) copy-start(f32[512,640]{1,0:T(8,128)S(1)} %get-tuple-element.28) | copy-start | bytes 3932164
  72.0 6.1 %collective-permute-start.2 = (bf16[512,640]{1,0:T(8,128)(2,1)S(1)}, bf16[512,640]{1,0:T(8,128)(2,1)}, u32[]{:S(2)}, u32[]{:S(2)}) collective-permute-start(bf16[512,640]{1,0:T(8,128)(2,1)S(1)} %get-tuple-element.27), channel_id=1, source_target_pairs={{0,64},{64,0},{1,65},{65,1},{2,66},{66,2},{3,67},{67,3},{4,68},{68... | collective-permute-start | bytes 1966088 | tf_op jit(solution)/shard_map/ppermute | solution.py:25
  82.8 45.5 %all-to-all-start.1 = ((bf16[256,2,1280]{2,1,0:T(2,128)(2,1)}), bf16[256,2,1280]{2,1,0:T(2,128)(2,1)S(1)}, u32[]{:S(2)}, u32[]{:S(2)}) async-start(bf16[256,2,1280]{2,1,0:T(2,128)(2,1)} %reshape.41), calls=%async_computation.1 | async-start | bytes 2621440 | tf_op jit(solution)/shard_map/all_to_all | solution.py:21
  96.7 33.0 %collective-permute-start.3 = (bf16[320,1280]{1,0:T(8,128)(2,1)}, bf16[320,1280]{1,0:T(8,128)(2,1)S(1)}, u32[]{:S(2)}, u32[]{:S(2)}) collective-permute-start(bf16[320,1280]{1,0:T(8,128)(2,1)} %get-tuple-element.20), channel_id=1, source_target_pairs={{0,64},{64,0},{1,65},{65,1},{2,66},{66,2},{3,67},{67,3},{4,68},{68... | collective-permute-start | bytes 2457608 | tf_op jit(solution)/shard_map/ppermute | solution.py:25
  129.7 6.7 %copy-start.4 = (bf16[64,1280]{1,0:T(8,128)(2,1)S(1)}, bf16[64,1280]{1,0:T(8,128)(2,1)}, u32[]{:S(2)}) copy-start(bf16[64,1280]{1,0:T(8,128)(2,1)} %copy-done.3) | copy-start | bytes 491524
  129.7 6.9 %copy-start.9 = (bf16[1,192,1280]{2,1,0:T(8,128)(2,1)S(1)}, bf16[1,192,1280]{2,1,0:T(8,128)(2,1)}, u32[]{:S(2)}) copy-start(bf16[1,192,1280]{2,1,0:T(8,128)(2,1)} %param.6) | copy-start | bytes 1474564
  131.6 4.9 %collective-permute-start.4 = (bf16[64,1280]{1,0:T(8,128)(2,1)S(1)}, bf16[64,1280]{1,0:T(8,128)(2,1)S(1)}, u32[]{:S(2)}, u32[]{:S(2)}) collective-permute-start(bf16[64,1280]{1,0:T(8,128)(2,1)S(1)} %slice.21), channel_id=1, source_target_pairs={{0,64},{64,0},{1,65},{65,1},{2,66},{66,2},{3,67},{67,3},{4,68},{68... | collective-permute-start | bytes 491528 | tf_op jit(solution)/shard_map/ppermute | solution.py:25
  150.6 14.0 %all-to-all-start.3 = ((bf16[16,2,1280]{2,1,0:T(2,128)(2,1)}), bf16[16,2,1280]{2,1,0:T(2,128)(2,1)S(1)}, u32[]{:S(2)}, u32[]{:S(2)}) async-start(bf16[16,2,1280]{2,1,0:T(2,128)(2,1)} %broadcast_in_dim.14), calls=%async_computation.3 | async-start | bytes 163840 | tf_op jit(solution)/shard_map/all_to_all | solution.py:21
  156.6 12.7 %copy-start.7 = (bf16[1280,64]{0,1:T(8,128)(2,1)S(1)}, bf16[1280,64]{0,1:T(8,128)(2,1)}, u32[]{:S(2)}) copy-start(bf16[1280,64]{0,1:T(8,128)(2,1)} %param.7) | copy-start | bytes 491524
  165.4 13.1 %all-to-all-start.4 = ((bf16[32,2,1280]{2,1,0:T(2,128)(2,1)}), bf16[32,2,1280]{2,1,0:T(2,128)(2,1)S(1)}, u32[]{:S(2)}, u32[]{:S(2)}) async-start(bf16[32,2,1280]{2,1,0:T(2,128)(2,1)} %broadcast_in_dim.15), calls=%async_computation.4 | async-start | bytes 327680 | tf_op jit(solution)/shard_map/all_to_all | solution.py:21

commit v5 on v4

--- a/solution.py
+++ b/solution.py
@@ -1,6 +1,10 @@
+import math
+
 import jax
 import jax.numpy as jnp
 from jax import lax
+from jax.experimental import pallas as pl
+from jax.experimental.pallas import tpu as pltpu
 from jax.sharding import Mesh, PartitionSpec as P
 
 SWAP = [(0, 1), (1, 0)]
@@ -13,8 +17,117 @@
 F32 = jnp.float32
 
 
-def gelu_back(preact, upstream):
-    return jax.vjp(jax.nn.gelu, preact)[1](upstream)[0]
+VMEM = pl.BlockSpec(memory_space=pltpu.VMEM)
+HBM = pl.BlockSpec(memory_space=pltpu.HBM)
+STEP = 128
+GELU_A = math.sqrt(2.0 / math.pi)
+GELU_B = 0.044715
+
+
+def on_core(kernel, outs, out_specs, scratch=()):
+    def call(*args):
+        return pl.pallas_call(
+            kernel,
+            out_shape=outs,
+            in_specs=[VMEM] * len(args),
+            out_specs=out_specs,
+            scratch_shapes=list(scratch),
+            compiler_params=pltpu.CompilerParams(vmem_limit_bytes=32 * 2**20),
+        )(*args)
+
+    return call
+
+
+def shape(*dims, dtype=BF):
+    return jax.ShapeDtypeStruct(dims, dtype)
+
+
+def spread_kernel(kept_ref, got_ref, out_ref, pair, sems):
+    core = lax.axis_index("core")
+    row = lax.broadcasted_iota(jnp.int32, (128, 64), 0)
+    col = lax.broadcasted_iota(jnp.int32, (128, 64), 1)
+    own = (row == 2 * col + core).astype(BF)
+    other = (row == 2 * col + 1 - core).astype(BF)
+    rows = jnp.dot(own, kept_ref[...], preferred_element_type=F32) + jnp.dot(
+        other, got_ref[...], preferred_element_type=F32
+    )
+    pair.reshape(128, 1280)[...] = rows.astype(BF)
+    copies = [pltpu.make_async_copy(pair, out_ref.at[i], sems.at[i]) for i in range(4)]
+    for copy in copies:
+        copy.start()
+    for copy in copies:
+        copy.wait()
+
+
+def enter_kernel(blocks_ref, weight_ref, slope_ref, send_ref):
+    first = lax.axis_index("core") == 0
+    blocks = blocks_ref.reshape(512, 1280)
+    for at in range(0, 512, STEP):
+        part = pl.ds(at, STEP)
+        v = lax.dot_general(
+            blocks[part], weight_ref[...], (((1,), (1,)), ((), ())), preferred_element_type=F32
+        )
+        square = v * v
+        t = jnp.tanh(GELU_A * v * (1.0 + GELU_B * square))
+        half = 0.5 * (1.0 + t)
+        send_ref[part] = jnp.where(first, v * half, v).astype(BF)
+        slope_ref[part] = half + (0.5 * GELU_A) * v * (1.0 - t * t) * (
+            1.0 + (3.0 * GELU_B) * square
+        )
+
+
+def leave_kernel(slope_ref, other_ref, weight_ref, hid_ref, out_ref, hids, blocks, hid_sems, sems):
+    first = lax.axis_index("core") == 0
+    copies = []
+    for i in range(512 // STEP):
+        part = pl.ds(i * STEP, STEP)
+        other = other_ref[part].astype(F32)
+        hid = jnp.where(first, slope_ref[part] * other, other).astype(BF)
+        hids[part] = hid
+        copies.append(pltpu.make_async_copy(hids.at[part], hid_ref.at[part], hid_sems.at[i]))
+        copies[-1].start()
+        rows = jnp.dot(hid, weight_ref[...], preferred_element_type=F32)
+        blocks.reshape(512, 1280)[part] = rows.astype(BF)
+        half = pl.ds(i * STEP // 2, STEP // 2)
+        copies.append(pltpu.make_async_copy(blocks.at[half], out_ref.at[half], sems.at[i]))
+        copies[-1].start()
+    for copy in copies:
+        copy.wait()
+
+
+def add_kernel(parts_ref, kept_ref, send_ref):
+    core = lax.axis_index("core")
+    row = lax.broadcasted_iota(jnp.int32, (64, 512), 0)
+    col = lax.broadcasted_iota(jnp.int32, (64, 512), 1) & 127
+    parts = parts_ref.reshape(512, 1280)[...]
+    for out_ref, image in ((kept_ref, core), (send_ref, 1 - core)):
+        adder = (col == 2 * row + image).astype(BF)
+        out_ref[...] = jnp.dot(adder, parts, preferred_element_type=F32).astype(BF)
+
+
+spread = on_core(
+    spread_kernel,
+    shape(4, 64, 2, 1280),
+    HBM,
+    (pltpu.VMEM((64, 2, 1280), BF), pltpu.SemaphoreType.DMA((4,))),
+)
+enter = on_core(
+    enter_kernel,
+    (shape(512, 640, dtype=F32), shape(512, 640)),
+    (VMEM, VMEM),
+)
+leave = on_core(
+    leave_kernel,
+    (shape(512, 640), shape(256, 2, 1280)),
+    (HBM, HBM),
+    (
+        pltpu.VMEM((512, 640), BF),
+        pltpu.VMEM((256, 2, 1280), BF),
+        pltpu.SemaphoreType.DMA((512 // STEP,)),
+        pltpu.SemaphoreType.DMA((512 // STEP,)),
+    ),
+)
+add4 = on_core(add_kernel, (shape(64, 1280), shape(64, 1280)), (VMEM, VMEM))
 
 
 def exchange(blocks, axes):
@@ -43,28 +156,18 @@
     dispatch_cast = dispatch.astype(BF)
     own_in = dot("ms,md->sd", dispatch_cast, tokens).astype(BF)
     own_grad = dot("ms,md->sd", combine.astype(BF), grad_out).astype(BF)
+    kept = jnp.where(first, own_in, own_grad)
     got = swap(jnp.where(first, own_grad, own_in))
-    pair = jnp.stack(
-        [jnp.where(first, own_in, got), jnp.where(first, got, own_grad)], axis=1
-    )
-    blocks = jnp.broadcast_to(pair[None], (4, 64, 2, 1280)).reshape(256, 2, 1280)
-    rows = exchange(blocks, CHIPS).reshape(512, 1280)
-    act = dot("id,hd->ih", rows, weight)
-    other = swap(jnp.where(first, jax.nn.gelu(act), act).astype(BF))
-    hid = jnp.where(first, gelu_back(act, other.astype(F32)).astype(BF), other)
-    partial = dot("ih,hd->id", hid, weight).astype(BF)
-    d_weight = dot("ih,id->hd", hid, rows).astype(BF)
-    parts = exchange(partial.reshape(256, 2, 1280), CHIPS).reshape(512, 1280)
+    blocks = exchange(spread(kept, got).reshape(256, 2, 1280), CHIPS)
+    slope, send = enter(blocks, weight)
+    hid, partial = leave(slope, swap(send), weight)
+    d_weight = dot("ih,id->hd", hid, blocks.reshape(512, 1280)).astype(BF)
+    parts = exchange(partial, CHIPS)
     d_kept = jnp.where(first, d_weight[:320], d_weight[320:])
     d_got = swap(jnp.where(first, d_weight[320:], d_weight[:320]))
     parts, d_kept, d_got = lax.optimization_barrier((parts, d_kept, d_got))
-    row = lax.broadcasted_iota(jnp.int32, (128, 512), 0)
-    col = lax.broadcasted_iota(jnp.int32, (128, 512), 1)
-    image = jnp.where(first, row // 64, 1 - row // 64)
-    adder = (col % 128 == (row % 64) * 2 + image).astype(BF)
-    back = dot("sr,rd->sd", adder, parts).astype(BF)
-    kept = back[:64]
-    got = swap(back[64:])
+    kept, send = add4(parts)
+    got = swap(send)
     slot_in_grad = jnp.where(first, kept, got)
     slot_out = jnp.where(first, got, kept)
     slot_stat = jnp.sum(own_in.astype(F32) * slot_in_grad.astype(F32), axis=1)

time: 180 us -> 178 us (0.989)
  Pallas kernels: 0 us -> 7.83 us
  matrix products: 15.7 us -> 8.82 us
  local copies, waits for them, and re-layouts: 8.65 us -> 6.56 us
    pallas_call x0 -> x4, Pallas kernels: none -> 7.83 us  [call(): pl.pallas_call(kernel, out_shape=outs, in_specs=[VMEM] * len(args), out_s...]
    dot_general x12 -> x9, matrix products: 15.7 us -> 8.82 us  [dot(): return jnp.einsum(spec, left, right, preferred_element_type=F32)]
    ppermute x5, waiting for transfers between devices: 5.79 us -> 7.72 us  [swap(): return lax.ppermute(value, 'core', SWAP)]
    unnamed x22 -> x16, local copies, waits for them, and re-layouts: 1.06 us -> 2.95 us
    reshape x3 -> x1, local copies, waits for them, and re-layouts: 3.25 us -> 1.38 us  [local(): d_weight = dot('ih,id->hd', hid, blocks.reshape(512, 1280)).astype(BF)]
  transfers between devices with their start and end apart: 9 -> 9, of which waited for: 8 -> 9; matrix products, arithmetic and copies ran while one was open for 6% -> 5% of each run, Pallas kernels for 0% -> 0%
where the time goes in v5:
time: 178 us
  waiting for transfers between devices  79.5 us (45%)
  starting transfers between devices  58.2 us (33%)
  blocking collectives  12.2 us (7%)
  matrix products  8.82 us (5%)
  Pallas kernels  7.83 us (4%)
  local copies, waits for them, and re-layouts  6.56 us (4%)
  other arithmetic  3.52 us (2%)
    all_to_all x4, waiting for transfers between devices, exchange(): return lax.all_to_all(blocks, axes, split_axis=0, concat_axis=0, tiled=True)  71.8 us
    all_to_all x4, starting transfers between devices, exchange(): return lax.all_to_all(blocks, axes, split_axis=0, concat_axis=0, tiled=True)  36.4 us
    ppermute x5, starting transfers between devices, swap(): return lax.ppermute(value, 'core', SWAP)  21.8 us
    all_to_all x1, blocking collectives, exchange(): return lax.all_to_all(blocks, axes, split_axis=0, concat_axis=0, tiled=True)  12.2 us
    dot_general x9, matrix products, dot(): return jnp.einsum(spec, left, right, preferred_element_type=F32)  8.82 us
    pallas_call x4, Pallas kernels, call(): pl.pallas_call(kernel, out_shape=outs, in_specs=[VMEM] * len(args), out_s...  7.83 us
    ppermute x5, waiting for transfers between devices, swap(): return lax.ppermute(value, 'core', SWAP)  7.72 us
  transfers between devices with their start and end apart: 9, of which 9 were waited for; matrix products, arithmetic and copies ran while one was open for 5% of the time, Pallas kernels for 0%

profile of v5, /device:TPU:1, one launch (start us, length us, event | category | flops | bytes accessed | tf_op | source)
XLA Modules:
  0.0 177.5 jit_solution(18387263152854200067)
XLA Ops:
  0.6 1.0 copy-done
  1.7 1.3 fusion.25
  3.5 1.3 broadcast_select_fusion.4
  4.8 8.8 %collective-permute-start = (bf16[64,1280]{1,0:T(8,128)(2,1)S(1)}, bf16[64,1280]{1,0:T(8,128)(2,1)S(1)}, u32[]{:S(2)}, u32[]{:S(2)}) collective-permute-start(bf16[64,1280]{1,0:T(8,128)(2,1)S(1)} %get-tuple-element.34), channel_id=1, source_target_pairs={{0,64},{64,0},{1,65},{65,1},{2,66},{66,2},{3,67},{67,3},{4,68},{68... | collective-permute-start | bytes 491528 | tf_op jit(solution)/shard_map/ppermute | solution.py:138
  13.6 1.0 collective-permute-done.got_ref
  14.6 1.4 shard_map.84
  16.1 17.1 %all-to-all-start = ((bf16[256,2,1280]{2,1,0:T(2,128)(2,1)}), bf16[256,2,1280]{2,1,0:T(2,128)(2,1)S(1)}, u32[]{:S(2)}, u32[]{:S(2)}) async-start(bf16[256,2,1280]{2,1,0:T(2,128)(2,1)} %bitcast.2), calls=%async_computation | async-start | bytes 2621440 | tf_op jit(solution)/shard_map/all_to_all | solution.py:134
  33.3 2.6 %collective-permute-start.1 = (bf16[320,1280]{1,0:T(8,128)(2,1)S(1)}, bf16[320,1280]{1,0:T(8,128)(2,1)S(1)}, u32[]{:S(2)}, u32[]{:S(2)}) collective-permute-start(bf16[320,1280]{1,0:T(8,128)(2,1)S(1)} %select_bitcast_fusion.2), channel_id=1, source_target_pairs={{0,64},{64,0},{1,65},{65,1},{2,66},{66,2},{3,67},{67,3},{4,68},{68... | collective-permute-start | bytes 2457608 | tf_op jit(solution)/shard_map/ppermute | solution.py:138
  35.9 1.9 %collective-permute-done.1 = bf16[320,1280]{1,0:T(8,128)(2,1)S(1)} collective-permute-done((bf16[320,1280]{1,0:T(8,128)(2,1)S(1)}, bf16[320,1280]{1,0:T(8,128)(2,1)S(1)}, u32[]{:S(2)}, u32[]{:S(2)}) %collective-permute-start.1) | collective-permute-done | bytes 819232 | tf_op jit(solution)/shard_map/ppermute | solution.py:138
  38.1 30.8 %all-to-all-done.blocks_ref = bf16[256,2,1280]{2,1,0:T(2,128)(2,1)S(1)} async-done(((bf16[256,2,1280]{2,1,0:T(2,128)(2,1)}), bf16[256,2,1280]{2,1,0:T(2,128)(2,1)S(1)}, u32[]{:S(2)}, u32[]{:S(2)}) %all-to-all-start) | async-done | bytes 1310752 | tf_op jit(solution)/shard_map/all_to_all | solution.py:134
  68.9 2.4 %shard_map.85 = (f32[512,640]{1,0:T(8,128)S(1)}, bf16[512,640]{1,0:T(8,128)(2,1)S(1)}) custom-call(bf16[256,2,1280]{2,1,0:T(2,128)(2,1)S(1)} %all-to-all-done.blocks_ref, bf16[640,1280]{1,0:T(8,128)(2,1)S(1)} %pad_maximum_fusion.weight_ref), custom_call_target="tpu_custom_call" | custom-call | tf_op jit(solution)/shard_map/pallas_call | solution.py:29
  71.3 4.3 %collective-permute-start.2 = (bf16[512,640]{1,0:T(8,128)(2,1)S(1)}, bf16[512,640]{1,0:T(8,128)(2,1)S(1)}, u32[]{:S(2)}, u32[]{:S(2)}) collective-permute-start(bf16[512,640]{1,0:T(8,128)(2,1)S(1)} %get-tuple-element.14), channel_id=1, source_target_pairs={{0,64},{64,0},{1,65},{65,1},{2,66},{66,2},{3,67},{67,3},{4,68},{68... | collective-permute-start | bytes 1966088 | tf_op jit(solution)/shard_map/ppermute | solution.py:138
  75.6 1.7 collective-permute-done.2.other_ref
  77.3 3.4 %shard_map.86 = (bf16[512,640]{1,0:T(8,128)(2,1)S(1)}, bf16[256,2,1280]{2,1,0:T(2,128)(2,1)S(1)}) custom-call(f32[512,640]{1,0:T(8,128)S(1)} %get-tuple-element.13.slope_ref, bf16[512,640]{1,0:T(8,128)(2,1)S(1)} %collective-permute-done.2.other_ref, bf16[640,1280]{1,0:T(8,128)(2,1)S(1)} %pad_maximum_fusion.weight_ref), custom_call_target="tpu_custom_call" | custom-call | tf_op jit(solution)/shard_map/pallas_call | solution.py:29
  80.7 1.1 copy-done.1
  81.8 0.8 copy-done.2
  82.6 9.4 %all-to-all-start.1 = ((bf16[256,2,1280]{2,1,0:T(2,128)(2,1)}), bf16[256,2,1280]{2,1,0:T(2,128)(2,1)S(1)}, u32[]{:S(2)}, u32[]{:S(2)}) async-start(bf16[256,2,1280]{2,1,0:T(2,128)(2,1)} %copy-done.1), calls=%async_computation.1 | async-start | bytes 2621440 | tf_op jit(solution)/shard_map/all_to_all | solution.py:134
  92.0 1.4 reshape.33
  93.4 2.6 %convolution_convert_fusion = bf16[640,1280]{1,0:T(8,128)(2,1)S(1)} fusion(bf16[512,640]{1,0:T(8,128)(2,1)} %copy-done.2, bf16[512,1280]{1,0:T(8,128)(2,1)} %reshape.33), kind=kOutput, calls=%fused_computation | convolution fusion | flops 839680000 | bytes 3604480 | tf_op jit(solution)/shard_map/ih,id->hd/dot_general | solution.py:142
  96.1 2.3 %collective-permute-start.3 = (bf16[320,1280]{1,0:T(8,128)(2,1)S(1)}, bf16[320,1280]{1,0:T(8,128)(2,1)}, u32[]{:S(2)}, u32[]{:S(2)}) collective-permute-start(bf16[320,1280]{1,0:T(8,128)(2,1)S(1)} %get-tuple-element.32), channel_id=1, source_target_pairs={{0,64},{64,0},{1,65},{65,1},{2,66},{66,2},{3,67},{67,3},{4,68},{68... | collective-permute-start | bytes 2457608 | tf_op jit(solution)/shard_map/ppermute | solution.py:138
  98.4 2.1 %collective-permute-done.3 = bf16[320,1280]{1,0:T(8,128)(2,1)} collective-permute-done((bf16[320,1280]{1,0:T(8,128)(2,1)S(1)}, bf16[320,1280]{1,0:T(8,128)(2,1)}, u32[]{:S(2)}, u32[]{:S(2)}) %collective-permute-start.3) | collective-permute-done | bytes 819232 | tf_op jit(solution)/shard_map/ppermute | solution.py:138
  100.4 27.7 %all-to-all-done.1.parts_ref = bf16[256,2,1280]{2,1,0:T(2,128)(2,1)S(1)} async-done(((bf16[256,2,1280]{2,1,0:T(2,128)(2,1)}), bf16[256,2,1280]{2,1,0:T(2,128)(2,1)S(1)}, u32[]{:S(2)}, u32[]{:S(2)}) %all-to-all-start.1) | async-done | bytes 1310752 | tf_op jit(solution)/shard_map/all_to_all | solution.py:134
  128.7 3.8 %collective-permute-start.4 = (bf16[64,1280]{1,0:T(8,128)(2,1)S(1)}, bf16[64,1280]{1,0:T(8,128)(2,1)S(1)}, u32[]{:S(2)}, u32[]{:S(2)}) collective-permute-start(bf16[64,1280]{1,0:T(8,128)(2,1)S(1)} %get-tuple-element.19), channel_id=1, source_target_pairs={{0,64},{64,0},{1,65},{65,1},{2,66},{66,2},{3,67},{67,3},{4,68},{68... | collective-permute-start | bytes 491528 | tf_op jit(solution)/shard_map/ppermute | solution.py:138
  132.6 1.0 collective-permute-done.4
  133.8 1.3 multiply_reduce_fusion.1
  135.7 12.2 %all_to_all.25 = bf16[32,2,1280]{2,1,0:T(2,128)(2,1)S(1)} all-to-all(bf16[32,2,1280]{2,1,0:T(2,128)(2,1)S(1)} %reshape.34), channel_id=1, replica_groups=mesh['y_lo'=4,'core'=2,'y_hi'=2,'x'=4,'z'=8] {'x','z'}, dimensions={0} | all-to-all | bytes 327680 | tf_op jit(solution)/shard_map/all_to_all | solution.py:134
  148.8 6.1 %all-to-all-start.3 = ((bf16[16,2,1280]{2,1,0:T(2,128)(2,1)}), bf16[16,2,1280]{2,1,0:T(2,128)(2,1)S(1)}, u32[]{:S(2)}, u32[]{:S(2)}) async-start(bf16[16,2,1280]{2,1,0:T(2,128)(2,1)} %broadcast_in_dim.11), calls=%async_computation.3 | async-start | bytes 163840 | tf_op jit(solution)/shard_map/all_to_all | solution.py:134
  154.9 2.5 %select_bitcast_fusion = (bf16[1,320,1280]{2,1,0:T(8,128)(2,1)}, bf16[1,320,1280]{2,1,0:T(8,128)(2,1)}) fusion(bf16[320,1280]{1,0:T(8,128)(2,1)} %collective-permute-done.3, bf16[320,1280]{1,0:T(8,128)(2,1)S(1)} %get-tuple-element.20, pred[]{:T(512)S(6)} %eq.3), kind=kLoop, calls=%fused_computation.16 | loop fusion | flops 819200 | bytes 3276801 | tf_op jit(solution)/shard_map/broadcast_in_dim | solution.py:191
  157.3 5.5 %all-to-all-done.3 = bf16[16,2,1280]{2,1,0:T(2,128)(2,1)S(1)} async-done(((bf16[16,2,1280]{2,1,0:T(2,128)(2,1)}), bf16[16,2,1280]{2,1,0:T(2,128)(2,1)S(1)}, u32[]{:S(2)}, u32[]{:S(2)}) %all-to-all-start.3) | async-done | bytes 81952 | tf_op jit(solution)/shard_map/all_to_all | solution.py:134
  163.7 3.9 %all-to-all-start.4 = ((bf16[32,2,1280]{2,1,0:T(2,128)(2,1)}), bf16[32,2,1280]{2,1,0:T(2,128)(2,1)S(1)}, u32[]{:S(2)}, u32[]{:S(2)}) async-start(bf16[32,2,1280]{2,1,0:T(2,128)(2,1)} %broadcast_in_dim.12), calls=%async_computation.4 | async-start | bytes 327680 | tf_op jit(solution)/shard_map/all_to_all | solution.py:134
  167.9 1.2 fusion.1
  169.1 7.7 %all-to-all-done.4 = bf16[32,2,1280]{2,1,0:T(2,128)(2,1)S(1)} async-done(((bf16[32,2,1280]{2,1,0:T(2,128)(2,1)}), bf16[32,2,1280]{2,1,0:T(2,128)(2,1)S(1)}, u32[]{:S(2)}, u32[]{:S(2)}) %all-to-all-start.4) | async-done | bytes 163872 | tf_op jit(solution)/shard_map/all_to_all | solution.py:134
  (30 shorter events, 5.0 us)
Async XLA Ops:
  0.6 1.0 copy-start
  3.5 12.6 %copy-start.5 = (bf16[64,1280]{1,0:T(8,128)(2,1)}, bf16[64,1280]{1,0:T(8,128)(2,1)S(1)}, u32[]{:S(2)}) copy-start(bf16[64,1280]{1,0:T(8,128)(2,1)S(1)} %convolution_convert_fusion.3) | copy-start | bytes 491524
  4.8 9.8 %collective-permute-start = (bf16[64,1280]{1,0:T(8,128)(2,1)S(1)}, bf16[64,1280]{1,0:T(8,128)(2,1)S(1)}, u32[]{:S(2)}, u32[]{:S(2)}) collective-permute-start(bf16[64,1280]{1,0:T(8,128)(2,1)S(1)} %get-tuple-element.34), channel_id=1, source_target_pairs={{0,64},{64,0},{1,65},{65,1},{2,66},{66,2},{3,67},{67,3},{4,68},{68... | collective-permute-start | bytes 491528 | tf_op jit(solution)/shard_map/ppermute | solution.py:138
  16.0 17.2 %copy-start.3 = (bf16[1,320,1280]{2,1,0:T(8,128)(2,1)S(1)}, bf16[1,320,1280]{2,1,0:T(8,128)(2,1)}, u32[]{:S(2)}) copy-start(bf16[1,320,1280]{2,1,0:T(8,128)(2,1)} %param.9) | copy-start | bytes 2457604
  16.0 17.2 %copy-start.4 = (bf16[1,320,1280]{2,1,0:T(8,128)(2,1)S(1)}, bf16[1,320,1280]{2,1,0:T(8,128)(2,1)}, u32[]{:S(2)}) copy-start(bf16[1,320,1280]{2,1,0:T(8,128)(2,1)} %param.8) | copy-start | bytes 2457604
  16.1 52.8 %all-to-all-start = ((bf16[256,2,1280]{2,1,0:T(2,128)(2,1)}), bf16[256,2,1280]{2,1,0:T(2,128)(2,1)S(1)}, u32[]{:S(2)}, u32[]{:S(2)}) async-start(bf16[256,2,1280]{2,1,0:T(2,128)(2,1)} %bitcast.2), calls=%async_computation | async-start | bytes 2621440 | tf_op jit(solution)/shard_map/all_to_all | solution.py:134
  33.3 4.5 %collective-permute-start.1 = (bf16[320,1280]{1,0:T(8,128)(2,1)S(1)}, bf16[320,1280]{1,0:T(8,128)(2,1)S(1)}, u32[]{:S(2)}, u32[]{:S(2)}) collective-permute-start(bf16[320,1280]{1,0:T(8,128)(2,1)S(1)} %select_bitcast_fusion.2), channel_id=1, source_target_pairs={{0,64},{64,0},{1,65},{65,1},{2,66},{66,2},{3,67},{67,3},{4,68},{68... | collective-permute-start | bytes 2457608 | tf_op jit(solution)/shard_map/ppermute | solution.py:138
  71.3 6.0 %collective-permute-start.2 = (bf16[512,640]{1,0:T(8,128)(2,1)S(1)}, bf16[512,640]{1,0:T(8,128)(2,1)S(1)}, u32[]{:S(2)}, u32[]{:S(2)}) collective-permute-start(bf16[512,640]{1,0:T(8,128)(2,1)S(1)} %get-tuple-element.14), channel_id=1, source_target_pairs={{0,64},{64,0},{1,65},{65,1},{2,66},{66,2},{3,67},{67,3},{4,68},{68... | collective-permute-start | bytes 1966088 | tf_op jit(solution)/shard_map/ppermute | solution.py:138
  80.7 1.1 copy-start.1
  81.8 0.8 copy-start.2
  82.6 45.5 %all-to-all-start.1 = ((bf16[256,2,1280]{2,1,0:T(2,128)(2,1)}), bf16[256,2,1280]{2,1,0:T(2,128)(2,1)S(1)}, u32[]{:S(2)}, u32[]{:S(2)}) async-start(bf16[256,2,1280]{2,1,0:T(2,128)(2,1)} %copy-done.1), calls=%async_computation.1 | async-start | bytes 2621440 | tf_op jit(solution)/shard_map/all_to_all | solution.py:134
  95.9 37.7 %copy-start.6 = (bf16[64,1280]{1,0:T(8,128)(2,1)S(1)}, bf16[64,1280]{1,0:T(8,128)(2,1)}, u32[]{:S(2)}) copy-start(bf16[64,1280]{1,0:T(8,128)(2,1)} %copy-done.5) | copy-start | bytes 491524
  96.1 4.4 %collective-permute-start.3 = (bf16[320,1280]{1,0:T(8,128)(2,1)S(1)}, bf16[320,1280]{1,0:T(8,128)(2,1)}, u32[]{:S(2)}, u32[]{:S(2)}) collective-permute-start(bf16[320,1280]{1,0:T(8,128)(2,1)S(1)} %get-tuple-element.32), channel_id=1, source_target_pairs={{0,64},{64,0},{1,65},{65,1},{2,66},{66,2},{3,67},{67,3},{4,68},{68... | collective-permute-start | bytes 2457608 | tf_op jit(solution)/shard_map/ppermute | solution.py:138
  128.7 4.9 %collective-permute-start.4 = (bf16[64,1280]{1,0:T(8,128)(2,1)S(1)}, bf16[64,1280]{1,0:T(8,128)(2,1)S(1)}, u32[]{:S(2)}, u32[]{:S(2)}) collective-permute-start(bf16[64,1280]{1,0:T(8,128)(2,1)S(1)} %get-tuple-element.19), channel_id=1, source_target_pairs={{0,64},{64,0},{1,65},{65,1},{2,66},{66,2},{3,67},{67,3},{4,68},{68... | collective-permute-start | bytes 491528 | tf_op jit(solution)/shard_map/ppermute | solution.py:138
  148.8 14.0 %all-to-all-start.3 = ((bf16[16,2,1280]{2,1,0:T(2,128)(2,1)}), bf16[16,2,1280]{2,1,0:T(2,128)(2,1)S(1)}, u32[]{:S(2)}, u32[]{:S(2)}) async-start(bf16[16,2,1280]{2,1,0:T(2,128)(2,1)} %broadcast_in_dim.11), calls=%async_computation.3 | async-start | bytes 163840 | tf_op jit(solution)/shard_map/all_to_all | solution.py:134
  154.9 12.7 %copy-start.7 = (bf16[1280,64]{0,1:T(8,128)(2,1)S(1)}, bf16[1280,64]{0,1:T(8,128)(2,1)}, u32[]{:S(2)}) copy-start(bf16[1280,64]{0,1:T(8,128)(2,1)} %param.7) | copy-start | bytes 491524
  163.7 13.1 %all-to-all-start.4 = ((bf16[32,2,1280]{2,1,0:T(2,128)(2,1)}), bf16[32,2,1280]{2,1,0:T(2,128)(2,1)S(1)}, u32[]{:S(2)}, u32[]{:S(2)}) async-start(bf16[32,2,1280]{2,1,0:T(2,128)(2,1)} %broadcast_in_dim.12), calls=%async_computation.4 | async-start | bytes 327680 | tf_op jit(solution)/shard_map/all_to_all | solution.py:134

commit v6 on v5

--- a/solution.py
+++ b/solution.py
@@ -24,15 +24,28 @@
 GELU_B = 0.044715
 
 
-def on_core(kernel, outs, out_specs, scratch=()):
+def dot_last(left, right):
+    return lax.dot_general(
+        left, right, (((1,), (1,)), ((), ())), preferred_element_type=F32
+    )
+
+
+def dot_first(left, right):
+    return lax.dot_general(
+        left, right, (((0,), (0,)), ((), ())), preferred_element_type=F32
+    )
+
+
+def on_core(kernel, outs, out_specs, scratch=(), in_specs=None, aliases=None, grant=32 * 2**20):
     def call(*args):
         return pl.pallas_call(
             kernel,
             out_shape=outs,
-            in_specs=[VMEM] * len(args),
+            in_specs=[(in_specs or {}).get(i, VMEM) for i in range(len(args))],
             out_specs=out_specs,
             scratch_shapes=list(scratch),
-            compiler_params=pltpu.CompilerParams(vmem_limit_bytes=32 * 2**20),
+            input_output_aliases=aliases or {},
+            compiler_params=pltpu.CompilerParams(vmem_limit_bytes=grant),
         )(*args)
 
     return call
@@ -64,9 +77,7 @@
     blocks = blocks_ref.reshape(512, 1280)
     for at in range(0, 512, STEP):
         part = pl.ds(at, STEP)
-        v = lax.dot_general(
-            blocks[part], weight_ref[...], (((1,), (1,)), ((), ())), preferred_element_type=F32
-        )
+        v = dot_last(blocks[part], weight_ref[...])
         square = v * v
         t = jnp.tanh(GELU_A * v * (1.0 + GELU_B * square))
         half = 0.5 * (1.0 + t)
@@ -76,7 +87,10 @@
         )
 
 
-def leave_kernel(slope_ref, other_ref, weight_ref, hid_ref, out_ref, hids, blocks, hid_sems, sems):
+def leave_kernel(
+    slope_ref, other_ref, weight_ref, spent_ref, out_ref, hid_ref, blocks, hids, sems
+):
+    del spent_ref
     first = lax.axis_index("core") == 0
     copies = []
     for i in range(512 // STEP):
@@ -84,15 +98,64 @@
         other = other_ref[part].astype(F32)
         hid = jnp.where(first, slope_ref[part] * other, other).astype(BF)
         hids[part] = hid
-        copies.append(pltpu.make_async_copy(hids.at[part], hid_ref.at[part], hid_sems.at[i]))
+        copies.append(pltpu.make_async_copy(hids.at[part], hid_ref.at[part], sems.at[0, i]))
         copies[-1].start()
         rows = jnp.dot(hid, weight_ref[...], preferred_element_type=F32)
         blocks.reshape(512, 1280)[part] = rows.astype(BF)
         half = pl.ds(i * STEP // 2, STEP // 2)
-        copies.append(pltpu.make_async_copy(blocks.at[half], out_ref.at[half], sems.at[i]))
+        copies.append(pltpu.make_async_copy(blocks.at[half], out_ref.at[half], sems.at[1, i]))
         copies[-1].start()
     for copy in copies:
         copy.wait()
+
+
+def image_kernel(
+    tokens_ref, router_ref, grad_hbm, dispatch_ref, combine_ref, own_ref, kept_ref, send_ref, grad, sem
+):
+    copy = pltpu.make_async_copy(grad_hbm, grad, sem)
+    copy.start()
+    first = lax.axis_index("core") == 0
+    tokens = tokens_ref[...]
+    logits = dot_last(tokens, router_ref[...])
+    dispatch = jnp.exp(logits - jnp.max(logits, axis=0, keepdims=True))
+    dispatch = dispatch / jnp.sum(dispatch, axis=0, keepdims=True)
+    dispatch_ref[...] = dispatch
+    own_in = dot_first(dispatch.astype(BF), tokens).astype(BF)
+    own_ref[...] = own_in
+    combine = jnp.exp(logits - jnp.max(logits, axis=1, keepdims=True))
+    combine = combine / jnp.sum(combine, axis=1, keepdims=True)
+    combine_ref[...] = combine
+    copy.wait()
+    own_grad = dot_first(combine.astype(BF), grad[...]).astype(BF)
+    kept_ref[...] = jnp.where(first, own_in, own_grad)
+    send_ref[...] = jnp.where(first, own_grad, own_in)
+
+
+def logit_kernel(
+    tokens_ref, grad_hbm, dispatch_ref, combine_ref, own_ref, kept_ref, got_ref,
+    slot_ref, logit_ref, term_ref, grad, sem,
+):
+    copy = pltpu.make_async_copy(grad_hbm, grad, sem)
+    copy.start()
+    first = lax.axis_index("core") == 0
+    tokens = tokens_ref[...]
+    kept, got = kept_ref[...], got_ref[...]
+    slot_in_grad = jnp.where(first, kept, got)
+    slot_out = jnp.where(first, got, kept)
+    slot_ref[...] = slot_in_grad
+    row = lax.broadcasted_iota(jnp.int32, (64, 64), 0)
+    col = lax.broadcasted_iota(jnp.int32, (64, 64), 1)
+    stat = jnp.sum(
+        jnp.where(row == col, dot_last(own_ref[...], slot_in_grad), 0.0), axis=0, keepdims=True
+    )
+    slot_part = dispatch_ref[...] * (dot_last(tokens, slot_in_grad) - stat)
+    copy.wait()
+    combine = combine_ref[...]
+    combine_grad = dot_last(grad[...], slot_out)
+    mean = jnp.sum(combine * combine_grad, axis=1, keepdims=True)
+    logit_grad = (slot_part + combine * (combine_grad - mean)).astype(BF)
+    logit_ref[...] = logit_grad
+    term_ref.reshape(64, 1280)[...] = dot_first(logit_grad, tokens).astype(BF)
 
 
 def add_kernel(parts_ref, kept_ref, send_ref):
@@ -118,14 +181,31 @@
 )
 leave = on_core(
     leave_kernel,
-    (shape(512, 640), shape(256, 2, 1280)),
+    (shape(256, 2, 1280), shape(512, 640)),
     (HBM, HBM),
     (
+        pltpu.VMEM((256, 2, 1280), BF),
         pltpu.VMEM((512, 640), BF),
-        pltpu.VMEM((256, 2, 1280), BF),
-        pltpu.SemaphoreType.DMA((512 // STEP,)),
-        pltpu.SemaphoreType.DMA((512 // STEP,)),
+        pltpu.SemaphoreType.DMA((2, 512 // STEP)),
     ),
+    {3: HBM},
+    {3: 0},
+)
+GRAD = (pltpu.VMEM((192, 1280), BF), pltpu.SemaphoreType.DMA(()))
+enter_slots = on_core(
+    image_kernel,
+    (shape(192, 64, dtype=F32), shape(192, 64, dtype=F32)) + (shape(64, 1280),) * 3,
+    (VMEM,) * 5,
+    GRAD,
+    {1: VMEM, 2: HBM},
+    grant=63_000_000,
+)
+logits_back = on_core(
+    logit_kernel,
+    (shape(64, 1280), shape(192, 64), shape(32, 2, 1280)),
+    (VMEM,) * 3,
+    GRAD,
+    {1: HBM},
 )
 add4 = on_core(add_kernel, (shape(64, 1280), shape(64, 1280)), (VMEM, VMEM))
 
@@ -150,38 +230,25 @@
     weight = jnp.concatenate(
         [jnp.where(first, weight_kept, weight_got), jnp.where(first, weight_got, weight_kept)]
     )
-    logits = dot("md,ds->ms", tokens, router)
-    dispatch = jax.nn.softmax(logits, axis=0)
-    combine = jax.nn.softmax(logits, axis=1)
-    dispatch_cast = dispatch.astype(BF)
-    own_in = dot("ms,md->sd", dispatch_cast, tokens).astype(BF)
-    own_grad = dot("ms,md->sd", combine.astype(BF), grad_out).astype(BF)
-    kept = jnp.where(first, own_in, own_grad)
-    got = swap(jnp.where(first, own_grad, own_in))
-    blocks = exchange(spread(kept, got).reshape(256, 2, 1280), CHIPS)
+    dispatch, combine, own_in, kept, send = enter_slots(tokens, router.T, grad_out)
+    spent = spread(kept, swap(send)).reshape(256, 2, 1280)
+    blocks = exchange(spent, CHIPS)
     slope, send = enter(blocks, weight)
-    hid, partial = leave(slope, swap(send), weight)
+    partial, hid = leave(slope, swap(send), weight, spent)
+    parts = exchange(partial, CHIPS)
     d_weight = dot("ih,id->hd", hid, blocks.reshape(512, 1280)).astype(BF)
-    parts = exchange(partial, CHIPS)
     d_kept = jnp.where(first, d_weight[:320], d_weight[320:])
     d_got = swap(jnp.where(first, d_weight[320:], d_weight[:320]))
     parts, d_kept, d_got = lax.optimization_barrier((parts, d_kept, d_got))
     kept, send = add4(parts)
-    got = swap(send)
-    slot_in_grad = jnp.where(first, kept, got)
-    slot_out = jnp.where(first, got, kept)
-    slot_stat = jnp.sum(own_in.astype(F32) * slot_in_grad.astype(F32), axis=1)
-    combine_grad = dot("md,sd->ms", grad_out, slot_out)
-    combine_logit = combine * (
-        combine_grad - jnp.sum(combine * combine_grad, axis=1, keepdims=True)
-    )
-    dispatch_grad = dot("md,sd->ms", tokens, slot_in_grad)
-    logit_grad = (dispatch * (dispatch_grad - slot_stat[None]) + combine_logit).astype(BF)
+    slot_in_grad, logit_grad, term = logits_back(
+        tokens, grad_out, dispatch, combine, own_in, kept, swap(send)
+    )
     d_tokens = (
-        dot("ms,ds->md", logit_grad, router) + dot("ms,sd->md", dispatch_cast, slot_in_grad)
+        dot("ms,ds->md", logit_grad, router)
+        + dot("ms,sd->md", dispatch.astype(BF), slot_in_grad)
     ).astype(BF)
-    term = dot("ms,md->sd", logit_grad, tokens).astype(BF)
-    term = jnp.sum(exchange(term.reshape(32, 2, 1280), PLANE).astype(F32), axis=0).astype(BF)
+    term = jnp.sum(exchange(term, PLANE).astype(F32), axis=0).astype(BF)
     term = exchange(jnp.broadcast_to(term[None], (16, 2, 1280)), LINE)
     term = jnp.sum(term.astype(F32), axis=0).astype(BF)
     term = exchange(jnp.broadcast_to(term[None], (32, 2, 1280)), PLANE)

time: 178 us -> 177 us (level)
  matrix products: 8.82 us -> 3.66 us
  Pallas kernels: 7.83 us -> 12.7 us
    dot_general x9 -> x3, matrix products: 8.82 us -> 3.66 us  [dot(): return jnp.einsum(spec, left, right, preferred_element_type=F32)]
    pallas_call x4 -> x6, Pallas kernels: 7.83 us -> 12.7 us  [call(): pl.pallas_call(kernel, out_shape=outs, in_specs=[(in_specs or {}).get(i,...]
where the time goes in v6:
time: 177 us; the launch traced here: 176 us
  waiting for transfers between devices  79.1 us (45%)
  starting transfers between devices  58.4 us (33%)
  Pallas kernels  12.7 us (7%)
  blocking collectives  12.2 us (7%)
  local copies, waits for them, and re-layouts  5.34 us (3%)
  other arithmetic  4 us (2%)
  matrix products  3.66 us (2%)
    all_to_all x4, waiting for transfers between devices, exchange(): return lax.all_to_all(blocks, axes, split_axis=0, concat_axis=0, tiled=True)  71.2 us
    all_to_all x4, starting transfers between devices, exchange(): return lax.all_to_all(blocks, axes, split_axis=0, concat_axis=0, tiled=True)  36.4 us
    ppermute x5, starting transfers between devices, swap(): return lax.ppermute(value, 'core', SWAP)  22 us
    pallas_call x6, Pallas kernels, call(): pl.pallas_call(kernel, out_shape=outs, in_specs=[(in_specs or {}).get(i,...  12.7 us
    all_to_all x1, blocking collectives, exchange(): return lax.all_to_all(blocks, axes, split_axis=0, concat_axis=0, tiled=True)  12.2 us
    ppermute x5, waiting for transfers between devices, swap(): return lax.ppermute(value, 'core', SWAP)  7.93 us
    dot_general x3, matrix products, dot(): return jnp.einsum(spec, left, right, preferred_element_type=F32)  3.66 us
  transfers between devices with their start and end apart: 9, of which 9 were waited for; matrix products, arithmetic and copies ran while one was open for 5% of the time, Pallas kernels for 0%

profile of v6, /device:TPU:1, one launch (start us, length us, event | category | flops | bytes accessed | tf_op | source)
XLA Modules:
  0.0 176.3 jit_solution(11802585534488823590)
XLA Ops:
  0.6 3.1 %shard_map.84 = (f32[192,64]{1,0:T(8,128)}, f32[192,64]{1,0:T(8,128)}, bf16[64,1280]{1,0:T(8,128)(2,1)}, bf16[64,1280]{1,0:T(8,128)(2,1)}, bf16[64,1280]{1,0:T(8,128)(2,1)}) custom-call(bf16[192,1280]{1,0:T(8,128)(2,1)} %bitcast.21, bf16[64,1280]{1,0:T(8,128)(2,1)} %bitcast.25, bf16[192,1280]{1,0:T(8,128)(2,1)} %bitcast.23), custom_call_target="tpu_custom_call" | custom-call | tf_op jit(solution)/shard_map/pallas_call | solution.py:41
  3.8 8.8 %collective-permute-start = (bf16[64,1280]{1,0:T(8,128)(2,1)}, bf16[64,1280]{1,0:T(8,128)(2,1)S(1)}, u32[]{:S(2)}, u32[]{:S(2)}) collective-permute-start(bf16[64,1280]{1,0:T(8,128)(2,1)} %get-tuple-element.25), channel_id=1, source_target_pairs={{0,64},{64,0},{1,65},{65,1},{2,66},{66,2},{3,67},{67,3},{4,68},{68... | collective-permute-start | bytes 491528 | tf_op jit(solution)/shard_map/ppermute | solution.py:218
  12.6 1.2 collective-permute-done.got_ref
  13.8 0.9 copy-done.4
  14.7 1.4 shard_map.85
  16.2 17.1 %all-to-all-start = ((bf16[256,2,1280]{2,1,0:T(2,128)(2,1)}), bf16[256,2,1280]{2,1,0:T(2,128)(2,1)S(1)}, u32[]{:S(2)}, u32[]{:S(2)}) async-start(bf16[256,2,1280]{2,1,0:T(2,128)(2,1)} %bitcast.3.spent_ref), calls=%async_computation | async-start | bytes 2621440 | tf_op jit(solution)/shard_map/all_to_all | solution.py:214
  33.4 2.6 %collective-permute-start.1 = (bf16[320,1280]{1,0:T(8,128)(2,1)S(1)}, bf16[320,1280]{1,0:T(8,128)(2,1)S(1)}, u32[]{:S(2)}, u32[]{:S(2)}) collective-permute-start(bf16[320,1280]{1,0:T(8,128)(2,1)S(1)} %select_bitcast_fusion.2), channel_id=1, source_target_pairs={{0,64},{64,0},{1,65},{65,1},{2,66},{66,2},{3,67},{67,3},{4,68},{68... | collective-permute-start | bytes 2457608 | tf_op jit(solution)/shard_map/ppermute | solution.py:218
  36.0 1.9 %collective-permute-done.1 = bf16[320,1280]{1,0:T(8,128)(2,1)S(1)} collective-permute-done((bf16[320,1280]{1,0:T(8,128)(2,1)S(1)}, bf16[320,1280]{1,0:T(8,128)(2,1)S(1)}, u32[]{:S(2)}, u32[]{:S(2)}) %collective-permute-start.1) | collective-permute-done | bytes 819232 | tf_op jit(solution)/shard_map/ppermute | solution.py:218
  38.2 30.7 %all-to-all-done.blocks_ref = bf16[256,2,1280]{2,1,0:T(2,128)(2,1)S(1)} async-done(((bf16[256,2,1280]{2,1,0:T(2,128)(2,1)}), bf16[256,2,1280]{2,1,0:T(2,128)(2,1)S(1)}, u32[]{:S(2)}, u32[]{:S(2)}) %all-to-all-start) | async-done | bytes 1310752 | tf_op jit(solution)/shard_map/all_to_all | solution.py:214
  68.9 2.4 %shard_map.86 = (f32[512,640]{1,0:T(8,128)S(1)}, bf16[512,640]{1,0:T(8,128)(2,1)S(1)}) custom-call(bf16[256,2,1280]{2,1,0:T(2,128)(2,1)S(1)} %all-to-all-done.blocks_ref, bf16[640,1280]{1,0:T(8,128)(2,1)S(1)} %pad_maximum_fusion.weight_ref), custom_call_target="tpu_custom_call" | custom-call | tf_op jit(solution)/shard_map/pallas_call | solution.py:41
  71.3 4.4 %collective-permute-start.2 = (bf16[512,640]{1,0:T(8,128)(2,1)S(1)}, bf16[512,640]{1,0:T(8,128)(2,1)S(1)}, u32[]{:S(2)}, u32[]{:S(2)}) collective-permute-start(bf16[512,640]{1,0:T(8,128)(2,1)S(1)} %get-tuple-element.27), channel_id=1, source_target_pairs={{0,64},{64,0},{1,65},{65,1},{2,66},{66,2},{3,67},{67,3},{4,68},{68... | collective-permute-start | bytes 1966088 | tf_op jit(solution)/shard_map/ppermute | solution.py:218
  75.7 1.7 collective-permute-done.2.other_ref
  77.4 3.6 %shard_map.87 = (bf16[256,2,1280]{2,1,0:T(2,128)(2,1)}, bf16[512,640]{1,0:T(8,128)(2,1)S(1)}) custom-call(f32[512,640]{1,0:T(8,128)S(1)} %get-tuple-element.26.slope_ref, bf16[512,640]{1,0:T(8,128)(2,1)S(1)} %collective-permute-done.2.other_ref, bf16[640,1280]{1,0:T(8,128)(2,1)S(1)} %pad_maximum_fusion.weight_ref, ...), custom_call_target="tpu_custom_call", output_to_operand_aliasing={{0}: (3, {})} | custom-call | tf_op jit(solution)/shard_map/pallas_call | solution.py:41
  81.0 0.8 copy-done.6
  81.9 9.4 %all-to-all-start.1 = ((bf16[256,2,1280]{2,1,0:T(2,128)(2,1)}), bf16[256,2,1280]{2,1,0:T(2,128)(2,1)S(1)}, u32[]{:S(2)}, u32[]{:S(2)}) async-start(bf16[256,2,1280]{2,1,0:T(2,128)(2,1)} %get-tuple-element.28), calls=%async_computation.1 | async-start | bytes 2621440 | tf_op jit(solution)/shard_map/all_to_all | solution.py:214
  91.2 1.4 reshape.24
  92.6 2.4 %convolution_convert_fusion = bf16[640,1280]{1,0:T(8,128)(2,1)S(1)} fusion(bf16[512,640]{1,0:T(8,128)(2,1)S(1)} %copy-done.7, bf16[512,1280]{1,0:T(8,128)(2,1)} %reshape.24), kind=kOutput, calls=%fused_computation | convolution fusion | flops 839680000 | bytes 3604480 | tf_op jit(solution)/shard_map/ih,id->hd/dot_general | solution.py:222
  95.0 1.0 broadcast_select_fusion.1
  96.0 2.3 %collective-permute-start.3 = (bf16[320,1280]{1,0:T(8,128)(2,1)S(1)}, bf16[320,1280]{1,0:T(8,128)(2,1)}, u32[]{:S(2)}, u32[]{:S(2)}) collective-permute-start(bf16[320,1280]{1,0:T(8,128)(2,1)S(1)} %get-tuple-element.42), channel_id=1, source_target_pairs={{0,64},{64,0},{1,65},{65,1},{2,66},{66,2},{3,67},{67,3},{4,68},{68... | collective-permute-start | bytes 2457608 | tf_op jit(solution)/shard_map/ppermute | solution.py:218
  98.3 2.1 %collective-permute-done.3 = bf16[320,1280]{1,0:T(8,128)(2,1)} collective-permute-done((bf16[320,1280]{1,0:T(8,128)(2,1)S(1)}, bf16[320,1280]{1,0:T(8,128)(2,1)}, u32[]{:S(2)}, u32[]{:S(2)}) %collective-permute-start.3) | collective-permute-done | bytes 819232 | tf_op jit(solution)/shard_map/ppermute | solution.py:218
  100.4 27.0 %all-to-all-done.1.parts_ref = bf16[256,2,1280]{2,1,0:T(2,128)(2,1)S(1)} async-done(((bf16[256,2,1280]{2,1,0:T(2,128)(2,1)}), bf16[256,2,1280]{2,1,0:T(2,128)(2,1)S(1)}, u32[]{:S(2)}, u32[]{:S(2)}) %all-to-all-start.1) | async-done | bytes 1310752 | tf_op jit(solution)/shard_map/all_to_all | solution.py:214
  128.0 4.0 %collective-permute-start.4 = (bf16[64,1280]{1,0:T(8,128)(2,1)S(1)}, bf16[64,1280]{1,0:T(8,128)(2,1)S(1)}, u32[]{:S(2)}, u32[]{:S(2)}) collective-permute-start(bf16[64,1280]{1,0:T(8,128)(2,1)S(1)} %get-tuple-element.32), channel_id=1, source_target_pairs={{0,64},{64,0},{1,65},{65,1},{2,66},{66,2},{3,67},{67,3},{4,68},{68... | collective-permute-start | bytes 491528 | tf_op jit(solution)/shard_map/ppermute | solution.py:218
  132.0 1.0 collective-permute-done.4.got_ref
  133.0 1.5 shard_map.89
  134.5 12.2 %all_to_all.25 = bf16[32,2,1280]{2,1,0:T(2,128)(2,1)S(1)} all-to-all(bf16[32,2,1280]{2,1,0:T(2,128)(2,1)S(1)} %get-tuple-element.35), channel_id=1, replica_groups=mesh['y_lo'=4,'core'=2,'y_hi'=2,'x'=4,'z'=8] {'x','z'}, dimensions={0} | all-to-all | bytes 327680 | tf_op jit(solution)/shard_map/all_to_all | solution.py:214
  147.6 6.1 %all-to-all-start.3 = ((bf16[16,2,1280]{2,1,0:T(2,128)(2,1)}), bf16[16,2,1280]{2,1,0:T(2,128)(2,1)S(1)}, u32[]{:S(2)}, u32[]{:S(2)}) async-start(bf16[16,2,1280]{2,1,0:T(2,128)(2,1)} %broadcast_in_dim.22), calls=%async_computation.3 | async-start | bytes 163840 | tf_op jit(solution)/shard_map/all_to_all | solution.py:214
  153.6 2.4 %select_bitcast_fusion = (bf16[1,320,1280]{2,1,0:T(8,128)(2,1)}, bf16[1,320,1280]{2,1,0:T(8,128)(2,1)}) fusion(bf16[320,1280]{1,0:T(8,128)(2,1)} %collective-permute-done.3, bf16[320,1280]{1,0:T(8,128)(2,1)S(1)} %copy-done.8, pred[]{:T(512)S(6)} %eq.3), kind=kLoop, calls=%fused_computation.7 | loop fusion | flops 819200 | bytes 3276801 | tf_op jit(solution)/shard_map/broadcast_in_dim | solution.py:258
  156.1 5.6 %all-to-all-done.3 = bf16[16,2,1280]{2,1,0:T(2,128)(2,1)S(1)} async-done(((bf16[16,2,1280]{2,1,0:T(2,128)(2,1)}), bf16[16,2,1280]{2,1,0:T(2,128)(2,1)S(1)}, u32[]{:S(2)}, u32[]{:S(2)}) %all-to-all-start.3) | async-done | bytes 81952 | tf_op jit(solution)/shard_map/all_to_all | solution.py:214
  161.7 0.8 broadcast_in_dim.23
  162.4 3.9 %all-to-all-start.4 = ((bf16[32,2,1280]{2,1,0:T(2,128)(2,1)}), bf16[32,2,1280]{2,1,0:T(2,128)(2,1)S(1)}, u32[]{:S(2)}, u32[]{:S(2)}) async-start(bf16[32,2,1280]{2,1,0:T(2,128)(2,1)} %broadcast_in_dim.23), calls=%async_computation.4 | async-start | bytes 327680 | tf_op jit(solution)/shard_map/all_to_all | solution.py:214
  166.6 1.1 fusion.1
  167.6 7.9 %all-to-all-done.4 = bf16[32,2,1280]{2,1,0:T(2,128)(2,1)S(1)} async-done(((bf16[32,2,1280]{2,1,0:T(2,128)(2,1)}), bf16[32,2,1280]{2,1,0:T(2,128)(2,1)S(1)}, u32[]{:S(2)}, u32[]{:S(2)}) %all-to-all-start.4) | async-done | bytes 163872 | tf_op jit(solution)/shard_map/all_to_all | solution.py:214
  (31 shorter events, 2.9 us)
Async XLA Ops:
  3.8 10.0 %collective-permute-start = (bf16[64,1280]{1,0:T(8,128)(2,1)}, bf16[64,1280]{1,0:T(8,128)(2,1)S(1)}, u32[]{:S(2)}, u32[]{:S(2)}) collective-permute-start(bf16[64,1280]{1,0:T(8,128)(2,1)} %get-tuple-element.25), channel_id=1, source_target_pairs={{0,64},{64,0},{1,65},{65,1},{2,66},{66,2},{3,67},{67,3},{4,68},{68... | collective-permute-start | bytes 491528 | tf_op jit(solution)/shard_map/ppermute | solution.py:218
  13.8 0.9 copy-start.4
  16.1 17.2 %copy-start.9 = (bf16[1,320,1280]{2,1,0:T(8,128)(2,1)S(1)}, bf16[1,320,1280]{2,1,0:T(8,128)(2,1)}, u32[]{:S(2)}) copy-start(bf16[1,320,1280]{2,1,0:T(8,128)(2,1)} %param.9) | copy-start | bytes 2457604
  16.1 17.2 %copy-start.10 = (bf16[1,320,1280]{2,1,0:T(8,128)(2,1)S(1)}, bf16[1,320,1280]{2,1,0:T(8,128)(2,1)}, u32[]{:S(2)}) copy-start(bf16[1,320,1280]{2,1,0:T(8,128)(2,1)} %param.8) | copy-start | bytes 2457604
  16.2 52.7 %all-to-all-start = ((bf16[256,2,1280]{2,1,0:T(2,128)(2,1)}), bf16[256,2,1280]{2,1,0:T(2,128)(2,1)S(1)}, u32[]{:S(2)}, u32[]{:S(2)}) async-start(bf16[256,2,1280]{2,1,0:T(2,128)(2,1)} %bitcast.3.spent_ref), calls=%async_computation | async-start | bytes 2621440 | tf_op jit(solution)/shard_map/all_to_all | solution.py:214
  33.4 4.5 %collective-permute-start.1 = (bf16[320,1280]{1,0:T(8,128)(2,1)S(1)}, bf16[320,1280]{1,0:T(8,128)(2,1)S(1)}, u32[]{:S(2)}, u32[]{:S(2)}) collective-permute-start(bf16[320,1280]{1,0:T(8,128)(2,1)S(1)} %select_bitcast_fusion.2), channel_id=1, source_target_pairs={{0,64},{64,0},{1,65},{65,1},{2,66},{66,2},{3,67},{67,3},{4,68},{68... | collective-permute-start | bytes 2457608 | tf_op jit(solution)/shard_map/ppermute | solution.py:218
  71.3 6.1 %collective-permute-start.2 = (bf16[512,640]{1,0:T(8,128)(2,1)S(1)}, bf16[512,640]{1,0:T(8,128)(2,1)S(1)}, u32[]{:S(2)}, u32[]{:S(2)}) collective-permute-start(bf16[512,640]{1,0:T(8,128)(2,1)S(1)} %get-tuple-element.27), channel_id=1, source_target_pairs={{0,64},{64,0},{1,65},{65,1},{2,66},{66,2},{3,67},{67,3},{4,68},{68... | collective-permute-start | bytes 1966088 | tf_op jit(solution)/shard_map/ppermute | solution.py:218
  81.0 0.8 copy-start.6
  81.9 45.5 %all-to-all-start.1 = ((bf16[256,2,1280]{2,1,0:T(2,128)(2,1)}), bf16[256,2,1280]{2,1,0:T(2,128)(2,1)S(1)}, u32[]{:S(2)}, u32[]{:S(2)}) async-start(bf16[256,2,1280]{2,1,0:T(2,128)(2,1)} %get-tuple-element.28), calls=%async_computation.1 | async-start | bytes 2621440 | tf_op jit(solution)/shard_map/all_to_all | solution.py:214
  91.2 1.4 copy-start.7
  95.0 38.0 %copy-start = (bf16[1,192,1280]{2,1,0:T(8,128)(2,1)S(1)}, bf16[1,192,1280]{2,1,0:T(8,128)(2,1)}, u32[]{:S(2)}) copy-start(bf16[1,192,1280]{2,1,0:T(8,128)(2,1)} %param.5) | copy-start | bytes 1474564
  95.0 38.0 %copy-start.1 = (bf16[1,192,1280]{2,1,0:T(8,128)(2,1)S(1)}, bf16[1,192,1280]{2,1,0:T(8,128)(2,1)}, u32[]{:S(2)}) copy-start(bf16[1,192,1280]{2,1,0:T(8,128)(2,1)} %param.6) | copy-start | bytes 1474564
  95.0 38.0 %copy-start.2 = (f32[192,64]{1,0:T(8,128)S(1)}, f32[192,64]{1,0:T(8,128)}, u32[]{:S(2)}) copy-start(f32[192,64]{1,0:T(8,128)} %get-tuple-element.21.dispatch_ref) | copy-start | bytes 147460
  95.0 38.0 %copy-start.3 = (bf16[64,1280]{1,0:T(8,128)(2,1)S(1)}, bf16[64,1280]{1,0:T(8,128)(2,1)}, u32[]{:S(2)}) copy-start(bf16[64,1280]{1,0:T(8,128)(2,1)} %get-tuple-element.23.own_ref) | copy-start | bytes 491524
  95.0 38.0 %copy-start.5 = (f32[192,64]{1,0:T(8,128)S(1)}, f32[192,64]{1,0:T(8,128)}, u32[]{:S(2)}) copy-start(f32[192,64]{1,0:T(8,128)} %get-tuple-element.22.combine_ref) | copy-start | bytes 147460
  96.0 4.3 %collective-permute-start.3 = (bf16[320,1280]{1,0:T(8,128)(2,1)S(1)}, bf16[320,1280]{1,0:T(8,128)(2,1)}, u32[]{:S(2)}, u32[]{:S(2)}) collective-permute-start(bf16[320,1280]{1,0:T(8,128)(2,1)S(1)} %get-tuple-element.42), channel_id=1, source_target_pairs={{0,64},{64,0},{1,65},{65,1},{2,66},{66,2},{3,67},{67,3},{4,68},{68... | collective-permute-start | bytes 2457608 | tf_op jit(solution)/shard_map/ppermute | solution.py:218
  128.0 25.7 %copy-start.8 = (bf16[320,1280]{1,0:T(8,128)(2,1)S(1)}, bf16[320,1280]{1,0:T(8,128)(2,1)}, u32[]{:S(2)}) copy-start(bf16[320,1280]{1,0:T(8,128)(2,1)} %get-tuple-element.36) | copy-start | bytes 2457604
  128.0 5.0 %collective-permute-start.4 = (bf16[64,1280]{1,0:T(8,128)(2,1)S(1)}, bf16[64,1280]{1,0:T(8,128)(2,1)S(1)}, u32[]{:S(2)}, u32[]{:S(2)}) collective-permute-start(bf16[64,1280]{1,0:T(8,128)(2,1)S(1)} %get-tuple-element.32), channel_id=1, source_target_pairs={{0,64},{64,0},{1,65},{65,1},{2,66},{66,2},{3,67},{67,3},{4,68},{68... | collective-permute-start | bytes 491528 | tf_op jit(solution)/shard_map/ppermute | solution.py:218
  147.6 14.0 %all-to-all-start.3 = ((bf16[16,2,1280]{2,1,0:T(2,128)(2,1)}), bf16[16,2,1280]{2,1,0:T(2,128)(2,1)S(1)}, u32[]{:S(2)}, u32[]{:S(2)}) async-start(bf16[16,2,1280]{2,1,0:T(2,128)(2,1)} %broadcast_in_dim.22), calls=%async_computation.3 | async-start | bytes 163840 | tf_op jit(solution)/shard_map/all_to_all | solution.py:214
  156.0 10.5 %copy-start.11 = (bf16[1280,64]{0,1:T(8,128)(2,1)S(1)}, bf16[1280,64]{0,1:T(8,128)(2,1)}, u32[]{:S(2)}) copy-start(bf16[1280,64]{0,1:T(8,128)(2,1)} %param.7) | copy-start | bytes 491524
  162.4 13.1 %all-to-all-start.4 = ((bf16[32,2,1280]{2,1,0:T(2,128)(2,1)}), bf16[32,2,1280]{2,1,0:T(2,128)(2,1)S(1)}, u32[]{:S(2)}, u32[]{:S(2)}) async-start(bf16[32,2,1280]{2,1,0:T(2,128)(2,1)} %broadcast_in_dim.23), calls=%async_computation.4 | async-start | bytes 327680 | tf_op jit(solution)/shard_map/all_to_all | solution.py:214

commit v7 on v6

--- a/solution.py
+++ b/solution.py
@@ -239,7 +239,9 @@
     d_weight = dot("ih,id->hd", hid, blocks.reshape(512, 1280)).astype(BF)
     d_kept = jnp.where(first, d_weight[:320], d_weight[320:])
     d_got = swap(jnp.where(first, d_weight[320:], d_weight[:320]))
-    parts, d_kept, d_got = lax.optimization_barrier((parts, d_kept, d_got))
+    d_w_in = jnp.where(first, d_kept, d_got)
+    d_w_out = jnp.where(first, d_got, d_kept)
+    parts, d_w_in, d_w_out = lax.optimization_barrier((parts, d_w_in, d_w_out))
     kept, send = add4(parts)
     slot_in_grad, logit_grad, term = logits_back(
         tokens, grad_out, dispatch, combine, own_in, kept, swap(send)
@@ -248,13 +250,12 @@
         dot("ms,ds->md", logit_grad, router)
         + dot("ms,sd->md", dispatch.astype(BF), slot_in_grad)
     ).astype(BF)
-    term = jnp.sum(exchange(term, PLANE).astype(F32), axis=0).astype(BF)
+    term, d_tokens = lax.optimization_barrier((exchange(term, PLANE), d_tokens))
+    term = jnp.sum(term.astype(F32), axis=0).astype(BF)
     term = exchange(jnp.broadcast_to(term[None], (16, 2, 1280)), LINE)
     term = jnp.sum(term.astype(F32), axis=0).astype(BF)
     term = exchange(jnp.broadcast_to(term[None], (32, 2, 1280)), PLANE)
     d_router = term.reshape(64, 1280).T
-    d_w_in = jnp.where(first, d_kept, d_got)
-    d_w_out = jnp.where(first, d_got, d_kept)
     return (d_tokens[None], d_router, d_w_in[None], d_w_out[None])
 
 

time: 177 us -> 177 us (level)
  blocking collectives: 12.2 us -> 26.5 us
  starting transfers between devices: 58.4 us -> 52.4 us
  waiting for transfers between devices: 79.1 us -> 73.1 us
  other arithmetic: 4 us -> 1.99 us
    all_to_all x1 -> x2, blocking collectives: 12.2 us -> 26.5 us  [exchange(): return lax.all_to_all(blocks, axes, split_axis=0, concat_axis=0, tiled=True)]
    all_to_all x4 -> x3, starting transfers between devices: 36.4 us -> 30.4 us  [exchange(): return lax.all_to_all(blocks, axes, split_axis=0, concat_axis=0, tiled=True)]
    all_to_all x4 -> x3, waiting for transfers between devices: 71.2 us -> 65.3 us  [exchange(): return lax.all_to_all(blocks, axes, split_axis=0, concat_axis=0, tiled=True)]
    broadcast_in_dim x1 -> x0, other arithmetic: 2.42 us -> none  [local(): return (d_tokens[None], d_router, d_w_in[None], d_w_out[None])]
  transfers between devices with their start and end apart: 9 -> 8, of which waited for: 9 -> 8; matrix products, arithmetic and copies ran while one was open for 5% -> 4% of each run, Pallas kernels for 0% -> 0%
where the time goes in v7:
time: 177 us; the launch traced here: 176 us
  waiting for transfers between devices  73.1 us (41%)
  starting transfers between devices  52.4 us (30%)
  blocking collectives  26.5 us (15%)
  Pallas kernels  13.3 us (8%)
  local copies, waits for them, and re-layouts  4.01 us (2%)
  matrix products  3.66 us (2%)
  other arithmetic  1.99 us (1%)
    all_to_all x3, waiting for transfers between devices, exchange(): return lax.all_to_all(blocks, axes, split_axis=0, concat_axis=0, tiled=True)  65.3 us
    all_to_all x3, starting transfers between devices, exchange(): return lax.all_to_all(blocks, axes, split_axis=0, concat_axis=0, tiled=True)  30.4 us
    all_to_all x2, blocking collectives, exchange(): return lax.all_to_all(blocks, axes, split_axis=0, concat_axis=0, tiled=True)  26.5 us
    ppermute x5, starting transfers between devices, swap(): return lax.ppermute(value, 'core', SWAP)  22 us
    pallas_call x6, Pallas kernels, call(): pl.pallas_call(kernel, out_shape=outs, in_specs=[(in_specs or {}).get(i,...  13.3 us
    ppermute x5, waiting for transfers between devices, swap(): return lax.ppermute(value, 'core', SWAP)  7.8 us
    dot_general x3, matrix products, dot(): return jnp.einsum(spec, left, right, preferred_element_type=F32)  3.66 us
  transfers between devices with their start and end apart: 8, of which 8 were waited for; matrix products, arithmetic and copies ran while one was open for 4% of the time, Pallas kernels for 0%

profile of v7, /device:TPU:1, one launch (start us, length us, event | category | flops | bytes accessed | tf_op | source)
XLA Modules:
  0.0 175.9 jit_solution(5480683640334773308)
XLA Ops:
  0.6 3.1 %shard_map.84 = (f32[192,64]{1,0:T(8,128)}, f32[192,64]{1,0:T(8,128)}, bf16[64,1280]{1,0:T(8,128)(2,1)}, bf16[64,1280]{1,0:T(8,128)(2,1)}, bf16[64,1280]{1,0:T(8,128)(2,1)}) custom-call(bf16[192,1280]{1,0:T(8,128)(2,1)} %bitcast.18, bf16[64,1280]{1,0:T(8,128)(2,1)} %bitcast.24, bf16[192,1280]{1,0:T(8,128)(2,1)} %bitcast.20), custom_call_target="tpu_custom_call" | custom-call | tf_op jit(solution)/shard_map/pallas_call | solution.py:41
  3.8 8.8 %collective-permute-start = (bf16[64,1280]{1,0:T(8,128)(2,1)}, bf16[64,1280]{1,0:T(8,128)(2,1)S(1)}, u32[]{:S(2)}, u32[]{:S(2)}) collective-permute-start(bf16[64,1280]{1,0:T(8,128)(2,1)} %get-tuple-element.27), channel_id=1, source_target_pairs={{0,64},{64,0},{1,65},{65,1},{2,66},{66,2},{3,67},{67,3},{4,68},{68... | collective-permute-start | bytes 491528 | tf_op jit(solution)/shard_map/ppermute | solution.py:218
  12.6 1.2 collective-permute-done.got_ref
  13.8 0.9 copy-done.4
  14.7 1.4 shard_map.85
  16.2 17.1 %all-to-all-start = ((bf16[256,2,1280]{2,1,0:T(2,128)(2,1)}), bf16[256,2,1280]{2,1,0:T(2,128)(2,1)S(1)}, u32[]{:S(2)}, u32[]{:S(2)}) async-start(bf16[256,2,1280]{2,1,0:T(2,128)(2,1)} %bitcast.3.spent_ref), calls=%async_computation | async-start | bytes 2621440 | tf_op jit(solution)/shard_map/all_to_all | solution.py:214
  33.4 2.6 %collective-permute-start.1 = (bf16[320,1280]{1,0:T(8,128)(2,1)S(1)}, bf16[320,1280]{1,0:T(8,128)(2,1)S(1)}, u32[]{:S(2)}, u32[]{:S(2)}) collective-permute-start(bf16[320,1280]{1,0:T(8,128)(2,1)S(1)} %select_bitcast_fusion), channel_id=1, source_target_pairs={{0,64},{64,0},{1,65},{65,1},{2,66},{66,2},{3,67},{67,3},{4,68},{68... | collective-permute-start | bytes 2457608 | tf_op jit(solution)/shard_map/ppermute | solution.py:218
  36.0 1.9 %collective-permute-done.1 = bf16[320,1280]{1,0:T(8,128)(2,1)S(1)} collective-permute-done((bf16[320,1280]{1,0:T(8,128)(2,1)S(1)}, bf16[320,1280]{1,0:T(8,128)(2,1)S(1)}, u32[]{:S(2)}, u32[]{:S(2)}) %collective-permute-start.1) | collective-permute-done | bytes 819232 | tf_op jit(solution)/shard_map/ppermute | solution.py:218
  38.2 30.8 %all-to-all-done.blocks_ref = bf16[256,2,1280]{2,1,0:T(2,128)(2,1)S(1)} async-done(((bf16[256,2,1280]{2,1,0:T(2,128)(2,1)}), bf16[256,2,1280]{2,1,0:T(2,128)(2,1)S(1)}, u32[]{:S(2)}, u32[]{:S(2)}) %all-to-all-start) | async-done | bytes 1310752 | tf_op jit(solution)/shard_map/all_to_all | solution.py:214
  69.0 2.4 %shard_map.86 = (f32[512,640]{1,0:T(8,128)S(1)}, bf16[512,640]{1,0:T(8,128)(2,1)S(1)}) custom-call(bf16[256,2,1280]{2,1,0:T(2,128)(2,1)S(1)} %all-to-all-done.blocks_ref, bf16[640,1280]{1,0:T(8,128)(2,1)S(1)} %pad_maximum_fusion.weight_ref), custom_call_target="tpu_custom_call" | custom-call | tf_op jit(solution)/shard_map/pallas_call | solution.py:41
  71.4 4.3 %collective-permute-start.2 = (bf16[512,640]{1,0:T(8,128)(2,1)S(1)}, bf16[512,640]{1,0:T(8,128)(2,1)S(1)}, u32[]{:S(2)}, u32[]{:S(2)}) collective-permute-start(bf16[512,640]{1,0:T(8,128)(2,1)S(1)} %get-tuple-element.29), channel_id=1, source_target_pairs={{0,64},{64,0},{1,65},{65,1},{2,66},{66,2},{3,67},{67,3},{4,68},{68... | collective-permute-start | bytes 1966088 | tf_op jit(solution)/shard_map/ppermute | solution.py:218
  75.7 1.7 collective-permute-done.2.other_ref
  77.4 3.6 %shard_map.87 = (bf16[256,2,1280]{2,1,0:T(2,128)(2,1)}, bf16[512,640]{1,0:T(8,128)(2,1)S(1)}) custom-call(f32[512,640]{1,0:T(8,128)S(1)} %get-tuple-element.28.slope_ref, bf16[512,640]{1,0:T(8,128)(2,1)S(1)} %collective-permute-done.2.other_ref, bf16[640,1280]{1,0:T(8,128)(2,1)S(1)} %pad_maximum_fusion.weight_ref, ...), custom_call_target="tpu_custom_call", output_to_operand_aliasing={{0}: (3, {})} | custom-call | tf_op jit(solution)/shard_map/pallas_call | solution.py:41
  81.0 0.8 copy-done.6
  81.9 9.4 %all-to-all-start.1 = ((bf16[256,2,1280]{2,1,0:T(2,128)(2,1)}), bf16[256,2,1280]{2,1,0:T(2,128)(2,1)S(1)}, u32[]{:S(2)}, u32[]{:S(2)}) async-start(bf16[256,2,1280]{2,1,0:T(2,128)(2,1)} %get-tuple-element.30), calls=%async_computation.1 | async-start | bytes 2621440 | tf_op jit(solution)/shard_map/all_to_all | solution.py:214
  91.2 1.4 reshape.24
  92.6 2.4 %convolution_convert_fusion = bf16[640,1280]{1,0:T(8,128)(2,1)S(1)} fusion(bf16[512,640]{1,0:T(8,128)(2,1)S(1)} %copy-done.7, bf16[512,1280]{1,0:T(8,128)(2,1)} %reshape.24), kind=kOutput, calls=%fused_computation | convolution fusion | flops 839680000 | bytes 3604480 | tf_op jit(solution)/shard_map/ih,id->hd/dot_general | solution.py:222
  95.1 2.4 %collective-permute-start.3 = (bf16[320,1280]{1,0:T(8,128)(2,1)S(1)}, bf16[320,1280]{1,0:T(8,128)(2,1)S(1)}, u32[]{:S(2)}, u32[]{:S(2)}) collective-permute-start(bf16[320,1280]{1,0:T(8,128)(2,1)S(1)} %broadcast_select_fusion.3), channel_id=1, source_target_pairs={{0,64},{64,0},{1,65},{65,1},{2,66},{66,2},{3,67},{67,3},{4,68},{68... | collective-permute-start | bytes 2457608 | tf_op jit(solution)/shard_map/ppermute | solution.py:218
  97.5 1.9 %collective-permute-done.3 = bf16[320,1280]{1,0:T(8,128)(2,1)S(1)} collective-permute-done((bf16[320,1280]{1,0:T(8,128)(2,1)S(1)}, bf16[320,1280]{1,0:T(8,128)(2,1)S(1)}, u32[]{:S(2)}, u32[]{:S(2)}) %collective-permute-start.3) | collective-permute-done | bytes 819232 | tf_op jit(solution)/shard_map/ppermute | solution.py:218
  99.4 1.3 broadcast_select_fusion.1
  100.8 26.6 %all-to-all-done.1.parts_ref = bf16[256,2,1280]{2,1,0:T(2,128)(2,1)S(1)} async-done(((bf16[256,2,1280]{2,1,0:T(2,128)(2,1)}), bf16[256,2,1280]{2,1,0:T(2,128)(2,1)S(1)}, u32[]{:S(2)}, u32[]{:S(2)}) %all-to-all-start.1) | async-done | bytes 1310752 | tf_op jit(solution)/shard_map/all_to_all | solution.py:214
  127.4 0.6 shard_map.88
  128.0 4.0 %collective-permute-start.4 = (bf16[64,1280]{1,0:T(8,128)(2,1)S(1)}, bf16[64,1280]{1,0:T(8,128)(2,1)S(1)}, u32[]{:S(2)}, u32[]{:S(2)}) collective-permute-start(bf16[64,1280]{1,0:T(8,128)(2,1)S(1)} %get-tuple-element.34), channel_id=1, source_target_pairs={{0,64},{64,0},{1,65},{65,1},{2,66},{66,2},{3,67},{67,3},{4,68},{68... | collective-permute-start | bytes 491528 | tf_op jit(solution)/shard_map/ppermute | solution.py:218
  132.0 1.0 collective-permute-done.4.got_ref
  133.0 2.2 %shard_map.89 = (bf16[64,1280]{1,0:T(8,128)(2,1)S(1)}, bf16[192,64]{1,0:T(8,128)(2,1)S(1)}, bf16[32,2,1280]{2,1,0:T(2,128)(2,1)}) custom-call(bf16[192,1280]{1,0:T(8,128)(2,1)S(1)} %bitcast.19, bf16[192,1280]{1,0:T(8,128)(2,1)S(1)} %bitcast.21, f32[192,64]{1,0:T(8,128)S(1)} %copy-done.2, f32[192,64]{1,0:T(8,128)S(1)} %copy-done.5, ...), custom_call_target="tpu_custom_call" | custom-call | tf_op jit(solution)/shard_map/pallas_call | solution.py:41
  135.2 3.9 %all-to-all-start.2 = ((bf16[32,2,1280]{2,1,0:T(2,128)(2,1)}), bf16[32,2,1280]{2,1,0:T(2,128)(2,1)S(1)}, u32[]{:S(2)}, u32[]{:S(2)}) async-start(bf16[32,2,1280]{2,1,0:T(2,128)(2,1)} %get-tuple-element.35), calls=%async_computation.2 | async-start | bytes 327680 | tf_op jit(solution)/shard_map/all_to_all | solution.py:214
  139.0 0.3 fusion.1
  139.3 1.1 fusion
  140.4 7.9 %all-to-all-done.2 = bf16[32,2,1280]{2,1,0:T(2,128)(2,1)S(1)} async-done(((bf16[32,2,1280]{2,1,0:T(2,128)(2,1)}), bf16[32,2,1280]{2,1,0:T(2,128)(2,1)S(1)}, u32[]{:S(2)}, u32[]{:S(2)}) %all-to-all-start.2) | async-done | bytes 163872 | tf_op jit(solution)/shard_map/all_to_all | solution.py:214
  148.5 13.8 %all_to_all.25 = bf16[16,2,1280]{2,1,0:T(2,128)(2,1)S(1)} all-to-all(bf16[16,2,1280]{2,1,0:T(2,128)(2,1)S(1)} %broadcast_in_dim.22), channel_id=1, replica_groups=mesh['y_lo'=4,'core'=2,'y_hi'=2,'x'=4,'z'=8] {'y_lo','core','y_hi'}, dimensions={0} | all-to-all | bytes 163840 | tf_op jit(solution)/shard_map/all_to_all | solution.py:214
  162.5 12.6 %all_to_all.26 = bf16[32,2,1280]{2,1,0:T(2,128)(2,1)S(1)} all-to-all(bf16[32,2,1280]{2,1,0:T(2,128)(2,1)S(1)} %broadcast_in_dim.23), channel_id=1, replica_groups=mesh['y_lo'=4,'core'=2,'y_hi'=2,'x'=4,'z'=8] {'x','z'}, dimensions={0} | all-to-all | bytes 327680 | tf_op jit(solution)/shard_map/all_to_all | solution.py:214
  175.1 0.7 reshape.25
  (28 shorter events, 0.9 us)
Async XLA Ops:
  3.8 10.0 %collective-permute-start = (bf16[64,1280]{1,0:T(8,128)(2,1)}, bf16[64,1280]{1,0:T(8,128)(2,1)S(1)}, u32[]{:S(2)}, u32[]{:S(2)}) collective-permute-start(bf16[64,1280]{1,0:T(8,128)(2,1)} %get-tuple-element.27), channel_id=1, source_target_pairs={{0,64},{64,0},{1,65},{65,1},{2,66},{66,2},{3,67},{67,3},{4,68},{68... | collective-permute-start | bytes 491528 | tf_op jit(solution)/shard_map/ppermute | solution.py:218
  13.8 0.9 copy-start.4
  16.1 17.2 %copy-start.8 = (bf16[1,320,1280]{2,1,0:T(8,128)(2,1)S(1)}, bf16[1,320,1280]{2,1,0:T(8,128)(2,1)}, u32[]{:S(2)}) copy-start(bf16[1,320,1280]{2,1,0:T(8,128)(2,1)} %param.9) | copy-start | bytes 2457604
  16.1 17.2 %copy-start.9 = (bf16[1,320,1280]{2,1,0:T(8,128)(2,1)S(1)}, bf16[1,320,1280]{2,1,0:T(8,128)(2,1)}, u32[]{:S(2)}) copy-start(bf16[1,320,1280]{2,1,0:T(8,128)(2,1)} %param.8) | copy-start | bytes 2457604
  16.2 52.8 %all-to-all-start = ((bf16[256,2,1280]{2,1,0:T(2,128)(2,1)}), bf16[256,2,1280]{2,1,0:T(2,128)(2,1)S(1)}, u32[]{:S(2)}, u32[]{:S(2)}) async-start(bf16[256,2,1280]{2,1,0:T(2,128)(2,1)} %bitcast.3.spent_ref), calls=%async_computation | async-start | bytes 2621440 | tf_op jit(solution)/shard_map/all_to_all | solution.py:214
  33.4 4.5 %collective-permute-start.1 = (bf16[320,1280]{1,0:T(8,128)(2,1)S(1)}, bf16[320,1280]{1,0:T(8,128)(2,1)S(1)}, u32[]{:S(2)}, u32[]{:S(2)}) collective-permute-start(bf16[320,1280]{1,0:T(8,128)(2,1)S(1)} %select_bitcast_fusion), channel_id=1, source_target_pairs={{0,64},{64,0},{1,65},{65,1},{2,66},{66,2},{3,67},{67,3},{4,68},{68... | collective-permute-start | bytes 2457608 | tf_op jit(solution)/shard_map/ppermute | solution.py:218
  71.4 6.0 %collective-permute-start.2 = (bf16[512,640]{1,0:T(8,128)(2,1)S(1)}, bf16[512,640]{1,0:T(8,128)(2,1)S(1)}, u32[]{:S(2)}, u32[]{:S(2)}) collective-permute-start(bf16[512,640]{1,0:T(8,128)(2,1)S(1)} %get-tuple-element.29), channel_id=1, source_target_pairs={{0,64},{64,0},{1,65},{65,1},{2,66},{66,2},{3,67},{67,3},{4,68},{68... | collective-permute-start | bytes 1966088 | tf_op jit(solution)/shard_map/ppermute | solution.py:218
  81.0 0.8 copy-start.6
  81.9 45.5 %all-to-all-start.1 = ((bf16[256,2,1280]{2,1,0:T(2,128)(2,1)}), bf16[256,2,1280]{2,1,0:T(2,128)(2,1)S(1)}, u32[]{:S(2)}, u32[]{:S(2)}) async-start(bf16[256,2,1280]{2,1,0:T(2,128)(2,1)} %get-tuple-element.30), calls=%async_computation.1 | async-start | bytes 2621440 | tf_op jit(solution)/shard_map/all_to_all | solution.py:214
  91.2 1.4 copy-start.7
  95.0 37.9 %copy-start.2 = (f32[192,64]{1,0:T(8,128)S(1)}, f32[192,64]{1,0:T(8,128)}, u32[]{:S(2)}) copy-start(f32[192,64]{1,0:T(8,128)} %get-tuple-element.23.dispatch_ref) | copy-start | bytes 147460
  95.1 37.9 %copy-start.3 = (bf16[64,1280]{1,0:T(8,128)(2,1)S(1)}, bf16[64,1280]{1,0:T(8,128)(2,1)}, u32[]{:S(2)}) copy-start(bf16[64,1280]{1,0:T(8,128)(2,1)} %get-tuple-element.25.own_ref) | copy-start | bytes 491524
  95.1 37.9 %copy-start.5 = (f32[192,64]{1,0:T(8,128)S(1)}, f32[192,64]{1,0:T(8,128)}, u32[]{:S(2)}) copy-start(f32[192,64]{1,0:T(8,128)} %get-tuple-element.24.combine_ref) | copy-start | bytes 147460
  95.1 4.4 %collective-permute-start.3 = (bf16[320,1280]{1,0:T(8,128)(2,1)S(1)}, bf16[320,1280]{1,0:T(8,128)(2,1)S(1)}, u32[]{:S(2)}, u32[]{:S(2)}) collective-permute-start(bf16[320,1280]{1,0:T(8,128)(2,1)S(1)} %broadcast_select_fusion.3), channel_id=1, source_target_pairs={{0,64},{64,0},{1,65},{65,1},{2,66},{66,2},{3,67},{67,3},{4,68},{68... | collective-permute-start | bytes 2457608 | tf_op jit(solution)/shard_map/ppermute | solution.py:218
  100.7 32.2 %copy-start = (bf16[1,192,1280]{2,1,0:T(8,128)(2,1)S(1)}, bf16[1,192,1280]{2,1,0:T(8,128)(2,1)}, u32[]{:S(2)}) copy-start(bf16[1,192,1280]{2,1,0:T(8,128)(2,1)} %param.5) | copy-start | bytes 1474564
  100.8 32.2 %copy-start.1 = (bf16[1,192,1280]{2,1,0:T(8,128)(2,1)S(1)}, bf16[1,192,1280]{2,1,0:T(8,128)(2,1)}, u32[]{:S(2)}) copy-start(bf16[1,192,1280]{2,1,0:T(8,128)(2,1)} %param.6) | copy-start | bytes 1474564
  128.0 11.3 %copy-start.10 = (bf16[1280,64]{0,1:T(8,128)(2,1)S(1)}, bf16[1280,64]{0,1:T(8,128)(2,1)}, u32[]{:S(2)}) copy-start(bf16[1280,64]{0,1:T(8,128)(2,1)} %param.7) | copy-start | bytes 491524
  128.0 5.0 %collective-permute-start.4 = (bf16[64,1280]{1,0:T(8,128)(2,1)S(1)}, bf16[64,1280]{1,0:T(8,128)(2,1)S(1)}, u32[]{:S(2)}, u32[]{:S(2)}) collective-permute-start(bf16[64,1280]{1,0:T(8,128)(2,1)S(1)} %get-tuple-element.34), channel_id=1, source_target_pairs={{0,64},{64,0},{1,65},{65,1},{2,66},{66,2},{3,67},{67,3},{4,68},{68... | collective-permute-start | bytes 491528 | tf_op jit(solution)/shard_map/ppermute | solution.py:218
  135.2 13.1 %all-to-all-start.2 = ((bf16[32,2,1280]{2,1,0:T(2,128)(2,1)}), bf16[32,2,1280]{2,1,0:T(2,128)(2,1)S(1)}, u32[]{:S(2)}, u32[]{:S(2)}) async-start(bf16[32,2,1280]{2,1,0:T(2,128)(2,1)} %get-tuple-element.35), calls=%async_computation.2 | async-start | bytes 327680 | tf_op jit(solution)/shard_map/all_to_all | solution.py:214

commit v8 on v7

v8 whole, which is shorter than its diff:
```python
import math

import jax
import jax.numpy as jnp
from jax import lax
from jax.experimental import pallas as pl
from jax.experimental.pallas import tpu as pltpu
from jax.sharding import Mesh, PartitionSpec as P

SWAP = [(0, 1), (1, 0)]
DP = ("y_lo", "core")
EXPERT = ("y_hi", "x", "z")
CHIPS = ("y_lo",) + EXPERT
PLANE = ("x", "z")
LINE = ("y_lo", "core", "y_hi")
BF = jnp.bfloat16
F32 = jnp.float32


VMEM = pl.BlockSpec(memory_space=pltpu.VMEM)
HBM = pl.BlockSpec(memory_space=pltpu.HBM)
STEP = 256
GELU_A = math.sqrt(2.0 / math.pi)
GELU_B = 0.044715


def dot_last(left, right):
    return lax.dot_general(
        left, right, (((1,), (1,)), ((), ())), preferred_element_type=F32
    )


def dot_first(left, right):
    return lax.dot_general(
        left, right, (((0,), (0,)), ((), ())), preferred_element_type=F32
    )


def on_core(kernel, outs, out_specs, scratch=(), in_specs=None, aliases=None, grant=32 * 2**20):
    def call(*args):
        return pl.pallas_call(
            kernel,
            out_shape=outs,
            in_specs=[(in_specs or {}).get(i, VMEM) for i in range(len(args))],
            out_specs=out_specs,
            scratch_shapes=list(scratch),
            input_output_aliases=aliases or {},
            compiler_params=pltpu.CompilerParams(vmem_limit_bytes=grant),
        )(*args)

    return call


def shape(*dims, dtype=BF):
    return jax.ShapeDtypeStruct(dims, dtype)


def image_kernel(
    tokens_ref, router_ref, grad_hbm, dispatch_ref, combine_ref, own_ref, out_ref, grad, pair, sems
):
    copy = pltpu.make_async_copy(grad_hbm, grad, sems.at[4])
    copy.start()
    tokens = tokens_ref[...]
    logits = dot_last(tokens, router_ref[...])
    dispatch = jnp.exp(logits - jnp.max(logits, axis=0, keepdims=True))
    dispatch = dispatch / jnp.sum(dispatch, axis=0, keepdims=True)
    dispatch_ref[...] = dispatch
    own_in = dot_first(dispatch.astype(BF), tokens).astype(BF)
    own_ref[...] = own_in
    pair[:, 0, :] = own_in
    combine = jnp.exp(logits - jnp.max(logits, axis=1, keepdims=True))
    combine = combine / jnp.sum(combine, axis=1, keepdims=True)
    combine_ref[...] = combine
    copy.wait()
    pair[:, 1, :] = dot_first(combine.astype(BF), grad[...]).astype(BF)
    copies = [pltpu.make_async_copy(pair, out_ref.at[i], sems.at[i]) for i in range(4)]
    for copy in copies:
        copy.start()
    for copy in copies:
        copy.wait()


def expert_kernel(
    blocks_ref, w_in_ref, w_out_hbm, spent_ref, hid_ref, grad_ref, out_ref, buffer, w_out_ref, sems
):
    del spent_ref
    load = pltpu.make_async_copy(w_out_hbm, w_out_ref, sems.at[256 // STEP])
    load.start()
    row = lax.broadcasted_iota(jnp.int32, (STEP, 2 * STEP), 0)
    col = lax.broadcasted_iota(jnp.int32, (STEP, 2 * STEP), 1)
    copies = []
    for i in range(256 // STEP):
        part = pl.ds(i * STEP, STEP)
        both = blocks_ref.reshape(512, 1280)[pl.ds(2 * i * STEP, 2 * STEP)]
        slot_in, slot_grad = (
            jnp.dot((col == 2 * row + kind).astype(BF), both, preferred_element_type=F32).astype(BF)
            for kind in (0, 1)
        )
        v = dot_last(slot_in, w_in_ref[...])
        if i == 0:
            load.wait()
        upstream = dot_last(slot_grad, w_out_ref[...])
        square = v * v
        t = jnp.tanh(GELU_A * v * (1.0 + GELU_B * square))
        half = 0.5 * (1.0 + t)
        slope = half + (0.5 * GELU_A) * v * (1.0 - t * t) * (1.0 + (3.0 * GELU_B) * square)
        hid = (v * half).astype(BF)
        grad = (slope * upstream).astype(BF)
        hid_ref[part] = hid
        grad_ref[part] = grad
        buffer[part, 0, :] = jnp.dot(
            hid, w_out_ref[...], preferred_element_type=F32
        ).astype(BF)
        buffer[part, 1, :] = jnp.dot(
            grad, w_in_ref[...], preferred_element_type=F32
        ).astype(BF)
        copies.append(pltpu.make_async_copy(buffer.at[part], out_ref.at[part], sems.at[i]))
        copies[-1].start()
    for copy in copies:
        copy.wait()


def logit_kernel(
    tokens_ref, grad_hbm, dispatch_ref, combine_ref, own_ref, parts_ref,
    slot_ref, logit_ref, term_ref, grad, sem,
):
    copy = pltpu.make_async_copy(grad_hbm, grad, sem)
    copy.start()
    tokens = tokens_ref[...]
    row = lax.broadcasted_iota(jnp.int32, (64, 512), 0)
    col = lax.broadcasted_iota(jnp.int32, (64, 512), 1) & 127
    parts = parts_ref.reshape(512, 1280)[...]
    slot_out, slot_in_grad = (
        jnp.dot((col == 2 * row + kind).astype(BF), parts, preferred_element_type=F32).astype(BF)
        for kind in (0, 1)
    )
    slot_ref[...] = slot_in_grad
    row = lax.broadcasted_iota(jnp.int32, (64, 64), 0)
    col = lax.broadcasted_iota(jnp.int32, (64, 64), 1)
    stat = jnp.sum(
        jnp.where(row == col, dot_last(own_ref[...], slot_in_grad), 0.0), axis=0, keepdims=True
    )
    slot_part = dispatch_ref[...] * (dot_last(tokens, slot_in_grad) - stat)
    copy.wait()
    combine = combine_ref[...]
    combine_grad = dot_last(grad[...], slot_out)
    mean = jnp.sum(combine * combine_grad, axis=1, keepdims=True)
    logit_grad = (slot_part + combine * (combine_grad - mean)).astype(BF)
    logit_ref[...] = logit_grad
    term_ref.reshape(64, 1280)[...] = dot_first(logit_grad, tokens).astype(BF)


image_slots = on_core(
    image_kernel,
    (
        shape(192, 64, dtype=F32),
        shape(192, 64, dtype=F32),
        shape(64, 1280),
        shape(4, 64, 2, 1280),
    ),
    (VMEM, VMEM, VMEM, HBM),
    (
        pltpu.VMEM((192, 1280), BF),
        pltpu.VMEM((64, 2, 1280), BF),
        pltpu.SemaphoreType.DMA((5,)),
    ),
    {2: HBM},
    grant=63_000_000,
)
experts = on_core(
    expert_kernel,
    (shape(256, 640), shape(256, 640), shape(256, 2, 1280)),
    (VMEM, VMEM, HBM),
    (
        pltpu.VMEM((256, 2, 1280), BF),
        pltpu.VMEM((640, 1280), BF),
        pltpu.SemaphoreType.DMA((256 // STEP + 1,)),
    ),
    {2: HBM, 3: HBM},
    {3: 2},
    grant=48 * 2**20,
)
logits_back = on_core(
    logit_kernel,
    (shape(64, 1280), shape(192, 64), shape(32, 2, 1280)),
    (VMEM,) * 3,
    (pltpu.VMEM((192, 1280), BF), pltpu.SemaphoreType.DMA(())),
    {1: HBM},
)


def exchange(blocks, axes):
    return lax.all_to_all(blocks, axes, split_axis=0, concat_axis=0, tiled=True)


def swap(value):
    return lax.ppermute(value, "core", SWAP)


def dot(spec, left, right):
    return jnp.einsum(spec, left, right, preferred_element_type=F32)


def local(tokens, grad_out, router, w_in, w_out):
    tokens, grad_out, w_in, w_out = tokens[0], grad_out[0], w_in[0], w_out[0]
    all_in = jnp.concatenate([w_in, swap(w_in)])
    all_out = jnp.concatenate([w_out, swap(w_out)])
    dispatch, combine, own_in, spent = image_slots(tokens, router.T, grad_out)
    spent = spent.reshape(256, 2, 1280)
    blocks = exchange(spent, CHIPS)
    hid, preact_grad, partial = experts(blocks, all_in, all_out, spent)
    parts = exchange(partial, CHIPS)
    d_in = dot("ih,id->hd", preact_grad, blocks[:, 0])
    d_out = dot("ih,id->hd", hid, blocks[:, 1])
    d_w_in = (d_in[:320] + swap(d_in[320:].astype(BF)).astype(F32)).astype(BF)
    d_w_out = (d_out[:320] + swap(d_out[320:].astype(BF)).astype(F32)).astype(BF)
    parts, d_w_in, d_w_out = lax.optimization_barrier((parts, d_w_in, d_w_out))
    slot_in_grad, logit_grad, term = logits_back(
        tokens, grad_out, dispatch, combine, own_in, parts
    )
    d_tokens = (
        dot("ms,ds->md", logit_grad, router)
        + dot("ms,sd->md", dispatch.astype(BF), slot_in_grad)
    ).astype(BF)
    term, d_tokens = lax.optimization_barrier((exchange(term, PLANE), d_tokens))
    term = jnp.sum(term.astype(F32), axis=0).astype(BF)
    term = exchange(jnp.broadcast_to(term[None], (16, 2, 1280)), LINE)
    term = jnp.sum(term.astype(F32), axis=0).astype(BF)
    term = exchange(jnp.broadcast_to(term[None], (32, 2, 1280)), PLANE)
    d_router = term.reshape(64, 1280).T
    return (d_tokens[None], d_router, d_w_in[None], d_w_out[None])


def solution(mesh):
    fine = Mesh(
        mesh.devices.reshape(4, 2, 2, 4, 8), ("y_lo", "core", "y_hi", "x", "z")
    )
    image = P(DP + EXPERT, None, None)
    unit = P(EXPERT, DP, None)
    return jax.shard_map(
        local,
        mesh=fine,
        in_specs=(image, image, P(), unit, unit),
        out_specs=(image, P(), unit, unit),
        check_vma=False,
    )
```

time: 177 us -> 160 us (0.904)
  waiting for transfers between devices: 73.1 us -> 57.9 us
  starting transfers between devices: 52.4 us -> 47.7 us
  other arithmetic: 1.99 us -> 6.06 us
  blocking collectives: 26.5 us -> 28.6 us
    ppermute x5 -> x4, starting transfers between devices: 22 us -> 10.8 us  [swap(): return lax.ppermute(value, 'core', SWAP)]
    all_to_all x3, waiting for transfers between devices: 65.3 us -> 55.5 us  [exchange(): return lax.all_to_all(blocks, axes, split_axis=0, concat_axis=0, tiled=True)]
    all_to_all x3, starting transfers between devices: 30.4 us -> 36.9 us  [exchange(): return lax.all_to_all(blocks, axes, split_axis=0, concat_axis=0, tiled=True)]
    ppermute x5 -> x4, waiting for transfers between devices: 7.8 us -> 2.45 us  [swap(): return lax.ppermute(value, 'core', SWAP)]
    concatenate x1 -> x2, other arithmetic: 0.11 us -> 3.69 us  [the longest x1 2.44 us: local(): all_out = jnp.concatenate([w_out, swap(w_out)])]
    all_to_all x2, blocking collectives: 26.5 us -> 28.6 us  [exchange(): return lax.all_to_all(blocks, axes, split_axis=0, concat_axis=0, tiled=True)]
    convert_element_type x0 -> x2, other arithmetic: none -> 2.13 us  [the longest x1 1.07 us: local(): (d_out[:320] + swap(d_out[320:].astype(BF)).astype(F32)).astype(BF)]
    slice x0 -> x3, local copies, waits for them, and re-layouts: none -> 1.98 us  [the longest x1 1.82 us: local(): d_out = dot('ih,id->hd', hid, blocks[:, 1])]
  transfers between devices with their start and end apart: 8 -> 7, of which waited for: 8 -> 5; matrix products, arithmetic and copies ran while one was open for 4% -> 7% of each run, Pallas kernels for 0% -> 0%
where the time goes in v8:
time: 160 us; the launch traced here: 159 us
  waiting for transfers between devices  57.9 us (36%)
  starting transfers between devices  47.7 us (30%)
  blocking collectives  28.6 us (18%)
  Pallas kernels  11.8 us (7%)
  other arithmetic  6.06 us (4%)
  local copies, waits for them, and re-layouts  3.6 us (2%)
  matrix products  2.59 us (2%)
    all_to_all x3, waiting for transfers between devices, exchange(): return lax.all_to_all(blocks, axes, split_axis=0, concat_axis=0, tiled=True)  55.5 us
    all_to_all x3, starting transfers between devices, exchange(): return lax.all_to_all(blocks, axes, split_axis=0, concat_axis=0, tiled=True)  36.9 us
    all_to_all x2, blocking collectives, exchange(): return lax.all_to_all(blocks, axes, split_axis=0, concat_axis=0, tiled=True)  28.6 us
    pallas_call x3, Pallas kernels, call(): pl.pallas_call(kernel, out_shape=outs, in_specs=[(in_specs or {}).get(i,...  11.8 us
    ppermute x4, starting transfers between devices, swap(): return lax.ppermute(value, 'core', SWAP)  10.8 us
  transfers between devices with their start and end apart: 7, of which 5 were waited for; matrix products, arithmetic and copies ran while one was open for 7% of the time, Pallas kernels for 0%

profile of v8, /device:TPU:1, one launch (start us, length us, event | category | flops | bytes accessed | tf_op | source)
XLA Modules:
  0.0 159.2 jit_solution(8454196090166257500)
XLA Ops:
  0.6 4.3 %shard_map.84 = (f32[192,64]{1,0:T(8,128)}, f32[192,64]{1,0:T(8,128)}, bf16[64,1280]{1,0:T(8,128)(2,1)}, bf16[4,64,2,1280]{3,2,1,0:T(2,128)(2,1)}) custom-call(bf16[192,1280]{1,0:T(8,128)(2,1)} %bitcast.21, bf16[64,1280]{1,0:T(8,128)(2,1)} %bitcast.29, bf16[192,1280]{1,0:T(8,128)(2,1)} %bitcast.23), custom_call_target="tpu_custom_call" | custom-call | tf_op jit(solution)/shard_map/pallas_call | solution.py:41
  5.0 23.2 %all-to-all-start = ((bf16[256,2,1280]{2,1,0:T(2,128)(2,1)}), bf16[256,2,1280]{2,1,0:T(2,128)(2,1)S(1)}, u32[]{:S(2)}, u32[]{:S(2)}) async-start(bf16[256,2,1280]{2,1,0:T(2,128)(2,1)} %bitcast.3.spent_ref), calls=%async_computation | async-start | bytes 2621440 | tf_op jit(solution)/shard_map/all_to_all | solution.py:193
  28.2 2.9 %collective-permute-start = (bf16[320,1280]{1,0:T(8,128)(2,1)S(1)}, bf16[320,1280]{1,0:T(8,128)(2,1)S(1)}, u32[]{:S(2)}, u32[]{:S(2)}) collective-permute-start(bf16[320,1280]{1,0:T(8,128)(2,1)S(1)} %bitcast.26), channel_id=1, source_target_pairs={{0,64},{64,0},{1,65},{65,1},{2,66},{66,2},{3,67},{67,3},{4,68},{68... | collective-permute-start | bytes 2457608 | tf_op jit(solution)/shard_map/ppermute | solution.py:197
  31.1 1.9 %collective-permute-start.1 = (bf16[320,1280]{1,0:T(8,128)(2,1)}, bf16[320,1280]{1,0:T(8,128)(2,1)S(1)}, u32[]{:S(2)}, u32[]{:S(2)}) collective-permute-start(bf16[320,1280]{1,0:T(8,128)(2,1)} %bitcast.5), channel_id=1, source_target_pairs={{0,64},{64,0},{1,65},{65,1},{2,66},{66,2},{3,67},{67,3},{4,68},{68... | collective-permute-start | bytes 2457608 | tf_op jit(solution)/shard_map/ppermute | solution.py:197
  33.0 1.3 pad_maximum_fusion.w_in_ref
  34.3 1.2 collective-permute-done.1
  35.5 2.4 %pad_maximum_fusion.1.w_out_hbm = bf16[640,1280]{1,0:T(8,128)(2,1)} fusion(bf16[320,1280]{1,0:T(8,128)(2,1)S(1)} %collective-permute-done.1, bf16[320,1280]{1,0:T(8,128)(2,1)} %bitcast.5), kind=kLoop, calls=%fused_computation.9 | loop fusion | flops 3276800 | bytes 3276800 | tf_op jit(solution)/shard_map/concatenate | solution.py:207
  38.0 25.7 %all-to-all-done.blocks_ref = bf16[256,2,1280]{2,1,0:T(2,128)(2,1)S(1)} async-done(((bf16[256,2,1280]{2,1,0:T(2,128)(2,1)}), bf16[256,2,1280]{2,1,0:T(2,128)(2,1)S(1)}, u32[]{:S(2)}, u32[]{:S(2)}) %all-to-all-start) | async-done | bytes 1310752 | tf_op jit(solution)/shard_map/all_to_all | solution.py:193
  63.6 4.9 %shard_map.85 = (bf16[256,640]{1,0:T(8,128)(2,1)S(1)}, bf16[256,640]{1,0:T(8,128)(2,1)S(1)}, bf16[256,2,1280]{2,1,0:T(2,128)(2,1)}) custom-call(bf16[256,2,1280]{2,1,0:T(2,128)(2,1)S(1)} %all-to-all-done.blocks_ref, bf16[640,1280]{1,0:T(8,128)(2,1)S(1)} %pad_maximum_fusion.w_in_ref, ...), custom_call_target="tpu_custom_call", output_to_operand_aliasing={{2}: (3, {})} | custom-call | tf_op jit(solution)/shard_map/pallas_call | solution.py:41
  68.5 0.7 copy-done.3
  69.3 9.8 %all-to-all-start.1 = ((bf16[256,2,1280]{2,1,0:T(2,128)(2,1)}), bf16[256,2,1280]{2,1,0:T(2,128)(2,1)S(1)}, u32[]{:S(2)}, u32[]{:S(2)}) async-start(bf16[256,2,1280]{2,1,0:T(2,128)(2,1)} %get-tuple-element.23), calls=%async_computation.1 | async-start | bytes 2621440 | tf_op jit(solution)/shard_map/all_to_all | solution.py:193
  79.1 1.8 %fusion.10 = (bf16[256,1,1280]{2,1,0:T(2,128)(2,1)S(1)}, bf16[256,1,1280]{2,1,0:T(2,128)(2,1)S(1)}) fusion(bf16[256,2,1280]{2,1,0:T(2,128)(2,1)S(1)} %all-to-all-done.blocks_ref), kind=kLoop, calls=%fused_computation.17 | loop fusion | bytes 2621440 | tf_op jit(solution)/shard_map/slice | solution.py:214
  80.9 0.6 fusion.3
  81.6 0.1 slice.40
  81.6 4.1 %collective-permute-start.3 = (bf16[320,1280]{1,0:T(8,128)(2,1)S(1)}, bf16[320,1280]{1,0:T(8,128)(2,1)S(1)}, u32[]{:S(2)}, u32[]{:S(2)}) collective-permute-start(bf16[320,1280]{1,0:T(8,128)(2,1)S(1)} %slice.40), channel_id=1, source_target_pairs={{0,64},{64,0},{1,65},{65,1},{2,66},{66,2},{3,67},{67,3},{4,68},{68... | collective-permute-start | bytes 2457608 | tf_op jit(solution)/shard_map/ppermute | solution.py:197
  85.8 0.6 fusion.6
  86.4 0.1 slice.41
  86.5 1.9 %collective-permute-start.2 = (bf16[320,1280]{1,0:T(8,128)(2,1)S(1)}, bf16[320,1280]{1,0:T(8,128)(2,1)S(1)}, u32[]{:S(2)}, u32[]{:S(2)}) collective-permute-start(bf16[320,1280]{1,0:T(8,128)(2,1)S(1)} %slice.41), channel_id=1, source_target_pairs={{0,64},{64,0},{1,65},{65,1},{2,66},{66,2},{3,67},{67,3},{4,68},{68... | collective-permute-start | bytes 2457608 | tf_op jit(solution)/shard_map/ppermute | solution.py:197
  88.4 1.1 fusion.1
  89.5 1.2 collective-permute-done.2
  90.7 1.1 fusion.2
  91.8 21.9 %all-to-all-done.1.parts_ref = bf16[256,2,1280]{2,1,0:T(2,128)(2,1)S(1)} async-done(((bf16[256,2,1280]{2,1,0:T(2,128)(2,1)}), bf16[256,2,1280]{2,1,0:T(2,128)(2,1)S(1)}, u32[]{:S(2)}, u32[]{:S(2)}) %all-to-all-start.1) | async-done | bytes 1310752 | tf_op jit(solution)/shard_map/all_to_all | solution.py:193
  113.7 2.6 %shard_map.86 = (bf16[64,1280]{1,0:T(8,128)(2,1)S(1)}, bf16[192,64]{1,0:T(8,128)(2,1)S(1)}, bf16[32,2,1280]{2,1,0:T(2,128)(2,1)}) custom-call(bf16[192,1280]{1,0:T(8,128)(2,1)S(1)} %bitcast.22, bf16[192,1280]{1,0:T(8,128)(2,1)S(1)} %bitcast.24, f32[192,64]{1,0:T(8,128)S(1)} %copy-done.2, f32[192,64]{1,0:T(8,128)S(1)} %copy-done.6, ...), custom_call_target="tpu_custom_call" | custom-call | tf_op jit(solution)/shard_map/pallas_call | solution.py:41
  116.3 3.9 %all-to-all-start.2 = ((bf16[32,2,1280]{2,1,0:T(2,128)(2,1)}), bf16[32,2,1280]{2,1,0:T(2,128)(2,1)S(1)}, u32[]{:S(2)}, u32[]{:S(2)}) async-start(bf16[32,2,1280]{2,1,0:T(2,128)(2,1)} %get-tuple-element.27), calls=%async_computation.2 | async-start | bytes 327680 | tf_op jit(solution)/shard_map/all_to_all | solution.py:193
  120.2 0.3 fusion.11
  120.5 1.0 fusion
  121.5 7.9 %all-to-all-done.2 = bf16[32,2,1280]{2,1,0:T(2,128)(2,1)S(1)} async-done(((bf16[32,2,1280]{2,1,0:T(2,128)(2,1)}), bf16[32,2,1280]{2,1,0:T(2,128)(2,1)S(1)}, u32[]{:S(2)}, u32[]{:S(2)}) %all-to-all-start.2) | async-done | bytes 163872 | tf_op jit(solution)/shard_map/all_to_all | solution.py:193
  129.5 0.2 reduce_sum.24
  129.7 16.0 %all_to_all.25 = bf16[16,2,1280]{2,1,0:T(2,128)(2,1)S(1)} all-to-all(bf16[16,2,1280]{2,1,0:T(2,128)(2,1)S(1)} %broadcast_in_dim.22), channel_id=1, replica_groups=mesh['y_lo'=4,'core'=2,'y_hi'=2,'x'=4,'z'=8] {'y_lo','core','y_hi'}, dimensions={0} | all-to-all | bytes 163840 | tf_op jit(solution)/shard_map/all_to_all | solution.py:193
  145.7 0.1 broadcast_in_dim.23
  145.8 12.7 %all_to_all.26 = bf16[32,2,1280]{2,1,0:T(2,128)(2,1)S(1)} all-to-all(bf16[32,2,1280]{2,1,0:T(2,128)(2,1)S(1)} %broadcast_in_dim.23), channel_id=1, replica_groups=mesh['y_lo'=4,'core'=2,'y_hi'=2,'x'=4,'z'=8] {'x','z'}, dimensions={0} | all-to-all | bytes 327680 | tf_op jit(solution)/shard_map/all_to_all | solution.py:193
  158.5 0.7 reshape.17
  (21 shorter events, 0.2 us)
Async XLA Ops:
  0.6 27.6 %copy-start.7 = (bf16[1,320,1280]{2,1,0:T(8,128)(2,1)S(1)}, bf16[1,320,1280]{2,1,0:T(8,128)(2,1)}, u32[]{:S(2)}) copy-start(bf16[1,320,1280]{2,1,0:T(8,128)(2,1)} %param.8) | copy-start | bytes 2457604
  5.0 58.7 %all-to-all-start = ((bf16[256,2,1280]{2,1,0:T(2,128)(2,1)}), bf16[256,2,1280]{2,1,0:T(2,128)(2,1)S(1)}, u32[]{:S(2)}, u32[]{:S(2)}) async-start(bf16[256,2,1280]{2,1,0:T(2,128)(2,1)} %bitcast.3.spent_ref), calls=%async_computation | async-start | bytes 2621440 | tf_op jit(solution)/shard_map/all_to_all | solution.py:193
  28.2 4.8 %collective-permute-start = (bf16[320,1280]{1,0:T(8,128)(2,1)S(1)}, bf16[320,1280]{1,0:T(8,128)(2,1)S(1)}, u32[]{:S(2)}, u32[]{:S(2)}) collective-permute-start(bf16[320,1280]{1,0:T(8,128)(2,1)S(1)} %bitcast.26), channel_id=1, source_target_pairs={{0,64},{64,0},{1,65},{65,1},{2,66},{66,2},{3,67},{67,3},{4,68},{68... | collective-permute-start | bytes 2457608 | tf_op jit(solution)/shard_map/ppermute | solution.py:197
  31.1 4.4 %collective-permute-start.1 = (bf16[320,1280]{1,0:T(8,128)(2,1)}, bf16[320,1280]{1,0:T(8,128)(2,1)S(1)}, u32[]{:S(2)}, u32[]{:S(2)}) collective-permute-start(bf16[320,1280]{1,0:T(8,128)(2,1)} %bitcast.5), channel_id=1, source_target_pairs={{0,64},{64,0},{1,65},{65,1},{2,66},{66,2},{3,67},{67,3},{4,68},{68... | collective-permute-start | bytes 2457608 | tf_op jit(solution)/shard_map/ppermute | solution.py:197
  68.5 0.7 copy-start.3
  69.3 44.4 %all-to-all-start.1 = ((bf16[256,2,1280]{2,1,0:T(2,128)(2,1)}), bf16[256,2,1280]{2,1,0:T(2,128)(2,1)S(1)}, u32[]{:S(2)}, u32[]{:S(2)}) async-start(bf16[256,2,1280]{2,1,0:T(2,128)(2,1)} %get-tuple-element.23), calls=%async_computation.1 | async-start | bytes 2621440 | tf_op jit(solution)/shard_map/all_to_all | solution.py:193
  79.1 1.8 %copy-start.4 = (bf16[256,640]{1,0:T(8,128)(2,1)S(1)}, bf16[256,640]{1,0:T(8,128)(2,1)}, u32[]{:S(2)}) copy-start(bf16[256,640]{1,0:T(8,128)(2,1)} %copy-done.3) | copy-start | bytes 983044
  81.6 6.8 %collective-permute-start.3 = (bf16[320,1280]{1,0:T(8,128)(2,1)S(1)}, bf16[320,1280]{1,0:T(8,128)(2,1)S(1)}, u32[]{:S(2)}, u32[]{:S(2)}) collective-permute-start(bf16[320,1280]{1,0:T(8,128)(2,1)S(1)} %slice.40), channel_id=1, source_target_pairs={{0,64},{64,0},{1,65},{65,1},{2,66},{66,2},{3,67},{67,3},{4,68},{68... | collective-permute-start | bytes 2457608 | tf_op jit(solution)/shard_map/ppermute | solution.py:197
  86.5 4.2 %collective-permute-start.2 = (bf16[320,1280]{1,0:T(8,128)(2,1)S(1)}, bf16[320,1280]{1,0:T(8,128)(2,1)S(1)}, u32[]{:S(2)}, u32[]{:S(2)}) collective-permute-start(bf16[320,1280]{1,0:T(8,128)(2,1)S(1)} %slice.41), channel_id=1, source_target_pairs={{0,64},{64,0},{1,65},{65,1},{2,66},{66,2},{3,67},{67,3},{4,68},{68... | collective-permute-start | bytes 2457608 | tf_op jit(solution)/shard_map/ppermute | solution.py:197
  89.5 24.2 %copy-start = (bf16[1,192,1280]{2,1,0:T(8,128)(2,1)S(1)}, bf16[1,192,1280]{2,1,0:T(8,128)(2,1)}, u32[]{:S(2)}) copy-start(bf16[1,192,1280]{2,1,0:T(8,128)(2,1)} %param.5) | copy-start | bytes 1474564
  89.5 24.2 %copy-start.1 = (bf16[1,192,1280]{2,1,0:T(8,128)(2,1)S(1)}, bf16[1,192,1280]{2,1,0:T(8,128)(2,1)}, u32[]{:S(2)}) copy-start(bf16[1,192,1280]{2,1,0:T(8,128)(2,1)} %param.6) | copy-start | bytes 1474564
  89.5 24.2 %copy-start.2 = (f32[192,64]{1,0:T(8,128)S(1)}, f32[192,64]{1,0:T(8,128)}, u32[]{:S(2)}) copy-start(f32[192,64]{1,0:T(8,128)} %get-tuple-element.19.dispatch_ref) | copy-start | bytes 147460
  89.5 24.2 %copy-start.5 = (bf16[64,1280]{1,0:T(8,128)(2,1)S(1)}, bf16[64,1280]{1,0:T(8,128)(2,1)}, u32[]{:S(2)}) copy-start(bf16[64,1280]{1,0:T(8,128)(2,1)} %get-tuple-element.21.own_ref) | copy-start | bytes 491524
  89.5 24.2 %copy-start.6 = (f32[192,64]{1,0:T(8,128)S(1)}, f32[192,64]{1,0:T(8,128)}, u32[]{:S(2)}) copy-start(f32[192,64]{1,0:T(8,128)} %get-tuple-element.20.combine_ref) | copy-start | bytes 147460
  91.8 28.4 %copy-start.8 = (bf16[1280,64]{0,1:T(8,128)(2,1)S(1)}, bf16[1280,64]{0,1:T(8,128)(2,1)}, u32[]{:S(2)}) copy-start(bf16[1280,64]{0,1:T(8,128)(2,1)} %param.7) | copy-start | bytes 491524
  116.3 13.1 %all-to-all-start.2 = ((bf16[32,2,1280]{2,1,0:T(2,128)(2,1)}), bf16[32,2,1280]{2,1,0:T(2,128)(2,1)S(1)}, u32[]{:S(2)}, u32[]{:S(2)}) async-start(bf16[32,2,1280]{2,1,0:T(2,128)(2,1)} %get-tuple-element.27), calls=%async_computation.2 | async-start | bytes 327680 | tf_op jit(solution)/shard_map/all_to_all | solution.py:193

commit v9 on v8

--- a/solution.py
+++ b/solution.py
@@ -19,7 +19,6 @@
 
 VMEM = pl.BlockSpec(memory_space=pltpu.VMEM)
 HBM = pl.BlockSpec(memory_space=pltpu.HBM)
-STEP = 256
 GELU_A = math.sqrt(2.0 / math.pi)
 GELU_B = 0.044715
 
@@ -56,7 +55,8 @@
 
 
 def image_kernel(
-    tokens_ref, router_ref, grad_hbm, dispatch_ref, combine_ref, own_ref, out_ref, grad, pair, sems
+    tokens_ref, router_ref, grad_hbm, dispatch_hbm, combine_hbm, own_hbm, out_ref,
+    grad, dispatch_ref, combine_ref, own_ref, pair, sems,
 ):
     copy = pltpu.make_async_copy(grad_hbm, grad, sems.at[4])
     copy.start()
@@ -67,57 +67,57 @@
     dispatch_ref[...] = dispatch
     own_in = dot_first(dispatch.astype(BF), tokens).astype(BF)
     own_ref[...] = own_in
+    copies = [
+        pltpu.make_async_copy(dispatch_ref, dispatch_hbm, sems.at[5]),
+        pltpu.make_async_copy(own_ref, own_hbm, sems.at[6]),
+    ]
+    for early in copies:
+        early.start()
     pair[:, 0, :] = own_in
     combine = jnp.exp(logits - jnp.max(logits, axis=1, keepdims=True))
     combine = combine / jnp.sum(combine, axis=1, keepdims=True)
     combine_ref[...] = combine
+    copies.append(pltpu.make_async_copy(combine_ref, combine_hbm, sems.at[7]))
+    copies[-1].start()
     copy.wait()
     pair[:, 1, :] = dot_first(combine.astype(BF), grad[...]).astype(BF)
-    copies = [pltpu.make_async_copy(pair, out_ref.at[i], sems.at[i]) for i in range(4)]
-    for copy in copies:
-        copy.start()
-    for copy in copies:
-        copy.wait()
+    late = [pltpu.make_async_copy(pair, out_ref.at[i], sems.at[i]) for i in range(4)]
+    for each in late:
+        each.start()
+    for each in copies + late:
+        each.wait()
 
 
 def expert_kernel(
     blocks_ref, w_in_ref, w_out_hbm, spent_ref, hid_ref, grad_ref, out_ref, buffer, w_out_ref, sems
 ):
     del spent_ref
-    load = pltpu.make_async_copy(w_out_hbm, w_out_ref, sems.at[256 // STEP])
+    load = pltpu.make_async_copy(w_out_hbm, w_out_ref, sems.at[0])
     load.start()
-    row = lax.broadcasted_iota(jnp.int32, (STEP, 2 * STEP), 0)
-    col = lax.broadcasted_iota(jnp.int32, (STEP, 2 * STEP), 1)
-    copies = []
-    for i in range(256 // STEP):
-        part = pl.ds(i * STEP, STEP)
-        both = blocks_ref.reshape(512, 1280)[pl.ds(2 * i * STEP, 2 * STEP)]
-        slot_in, slot_grad = (
-            jnp.dot((col == 2 * row + kind).astype(BF), both, preferred_element_type=F32).astype(BF)
-            for kind in (0, 1)
-        )
-        v = dot_last(slot_in, w_in_ref[...])
-        if i == 0:
-            load.wait()
-        upstream = dot_last(slot_grad, w_out_ref[...])
-        square = v * v
-        t = jnp.tanh(GELU_A * v * (1.0 + GELU_B * square))
-        half = 0.5 * (1.0 + t)
-        slope = half + (0.5 * GELU_A) * v * (1.0 - t * t) * (1.0 + (3.0 * GELU_B) * square)
-        hid = (v * half).astype(BF)
-        grad = (slope * upstream).astype(BF)
-        hid_ref[part] = hid
-        grad_ref[part] = grad
-        buffer[part, 0, :] = jnp.dot(
-            hid, w_out_ref[...], preferred_element_type=F32
-        ).astype(BF)
-        buffer[part, 1, :] = jnp.dot(
-            grad, w_in_ref[...], preferred_element_type=F32
-        ).astype(BF)
-        copies.append(pltpu.make_async_copy(buffer.at[part], out_ref.at[part], sems.at[i]))
-        copies[-1].start()
-    for copy in copies:
-        copy.wait()
+    row = lax.broadcasted_iota(jnp.int32, (128, 128), 0)
+    col = lax.broadcasted_iota(jnp.int32, (128, 128), 1)
+    sort = (col == 2 * (row & 63) + (row >> 6)).astype(BF)
+    rows = blocks_ref.reshape(512, 1280)
+    sorted_rows = [
+        jnp.dot(sort, rows[pl.ds(at, 128)], preferred_element_type=F32).astype(BF)
+        for at in range(0, 512, 128)
+    ]
+    v = dot_last(w_in_ref[...], jnp.concatenate([part[:64] for part in sorted_rows]))
+    load.wait()
+    upstream = dot_last(w_out_ref[...], jnp.concatenate([part[64:] for part in sorted_rows]))
+    square = v * v
+    half = 0.5 * jnp.tanh(v * (GELU_A + (GELU_A * GELU_B) * square)) + 0.5
+    value = v * half
+    slope = half + (value - value * half) * ((2.0 * GELU_A) + (6.0 * GELU_A * GELU_B) * square)
+    hid = value.astype(BF)
+    grad = (slope * upstream).astype(BF)
+    hid_ref[...] = hid
+    grad_ref[...] = grad
+    buffer[:, 0, :] = dot_first(hid, w_out_ref[...]).astype(BF)
+    buffer[:, 1, :] = dot_first(grad, w_in_ref[...]).astype(BF)
+    copy = pltpu.make_async_copy(buffer, out_ref, sems.at[1])
+    copy.start()
+    copy.wait()
 
 
 def logit_kernel(
@@ -127,13 +127,13 @@
     copy = pltpu.make_async_copy(grad_hbm, grad, sem)
     copy.start()
     tokens = tokens_ref[...]
-    row = lax.broadcasted_iota(jnp.int32, (64, 512), 0)
-    col = lax.broadcasted_iota(jnp.int32, (64, 512), 1) & 127
-    parts = parts_ref.reshape(512, 1280)[...]
-    slot_out, slot_in_grad = (
-        jnp.dot((col == 2 * row + kind).astype(BF), parts, preferred_element_type=F32).astype(BF)
-        for kind in (0, 1)
-    )
+    row = lax.broadcasted_iota(jnp.int32, (128, 512), 0)
+    col = lax.broadcasted_iota(jnp.int32, (128, 512), 1) & 127
+    adder = (col == 2 * (row & 63) + (row >> 6)).astype(BF)
+    slots = jnp.dot(
+        adder, parts_ref.reshape(512, 1280)[...], preferred_element_type=F32
+    ).astype(BF)
+    slot_out, slot_in_grad = slots[:64], slots[64:]
     slot_ref[...] = slot_in_grad
     row = lax.broadcasted_iota(jnp.int32, (64, 64), 0)
     col = lax.broadcasted_iota(jnp.int32, (64, 64), 1)
@@ -158,23 +158,26 @@
         shape(64, 1280),
         shape(4, 64, 2, 1280),
     ),
-    (VMEM, VMEM, VMEM, HBM),
+    (HBM,) * 4,
     (
         pltpu.VMEM((192, 1280), BF),
+        pltpu.VMEM((192, 64), F32),
+        pltpu.VMEM((192, 64), F32),
+        pltpu.VMEM((64, 1280), BF),
         pltpu.VMEM((64, 2, 1280), BF),
-        pltpu.SemaphoreType.DMA((5,)),
+        pltpu.SemaphoreType.DMA((8,)),
     ),
     {2: HBM},
     grant=63_000_000,
 )
 experts = on_core(
     expert_kernel,
-    (shape(256, 640), shape(256, 640), shape(256, 2, 1280)),
+    (shape(640, 256), shape(640, 256), shape(256, 2, 1280)),
     (VMEM, VMEM, HBM),
     (
         pltpu.VMEM((256, 2, 1280), BF),
         pltpu.VMEM((640, 1280), BF),
-        pltpu.SemaphoreType.DMA((256 // STEP + 1,)),
+        pltpu.SemaphoreType.DMA((2,)),
     ),
     {2: HBM, 3: HBM},
     {3: 2},
@@ -210,8 +213,8 @@
     blocks = exchange(spent, CHIPS)
     hid, preact_grad, partial = experts(blocks, all_in, all_out, spent)
     parts = exchange(partial, CHIPS)
-    d_in = dot("ih,id->hd", preact_grad, blocks[:, 0])
-    d_out = dot("ih,id->hd", hid, blocks[:, 1])
+    d_in = dot("hi,id->hd", preact_grad, blocks[:, 0])
+    d_out = dot("hi,id->hd", hid, blocks[:, 1])
     d_w_in = (d_in[:320] + swap(d_in[320:].astype(BF)).astype(F32)).astype(BF)
     d_w_out = (d_out[:320] + swap(d_out[320:].astype(BF)).astype(F32)).astype(BF)
     parts, d_w_in, d_w_out = lax.optimization_barrier((parts, d_w_in, d_w_out))

time: 160 us -> 159 us (level)
  no operation moved by 1% of the time
where the time goes in v9:
time: 159 us; the launch traced here: 158 us
  waiting for transfers between devices  58.3 us (37%)
  starting transfers between devices  47.7 us (30%)
  blocking collectives  28.4 us (18%)
  Pallas kernels  10.8 us (7%)
  other arithmetic  6.06 us (4%)
  local copies, waits for them, and re-layouts  3.6 us (2%)
  matrix products  2.5 us (2%)
    all_to_all x3, waiting for transfers between devices, exchange(): return lax.all_to_all(blocks, axes, split_axis=0, concat_axis=0, tiled=True)  55.8 us
    all_to_all x3, starting transfers between devices, exchange(): return lax.all_to_all(blocks, axes, split_axis=0, concat_axis=0, tiled=True)  37.1 us
    all_to_all x2, blocking collectives, exchange(): return lax.all_to_all(blocks, axes, split_axis=0, concat_axis=0, tiled=True)  28.4 us
    pallas_call x3, Pallas kernels, call(): pl.pallas_call(kernel, out_shape=outs, in_specs=[(in_specs or {}).get(i,...  10.8 us
    ppermute x4, starting transfers between devices, swap(): return lax.ppermute(value, 'core', SWAP)  10.6 us
  transfers between devices with their start and end apart: 7, of which 5 were waited for; matrix products, arithmetic and copies ran while one was open for 7% of the time, Pallas kernels for 0%

profile of v9, /device:TPU:1, one launch (start us, length us, event | category | flops | bytes accessed | tf_op | source)
XLA Modules:
  0.0 158.2 jit_solution(2154742425259899727)
XLA Ops:
  0.6 3.6 %shard_map.84 = (f32[192,64]{1,0:T(8,128)}, f32[192,64]{1,0:T(8,128)}, bf16[64,1280]{1,0:T(8,128)(2,1)}, bf16[4,64,2,1280]{3,2,1,0:T(2,128)(2,1)}) custom-call(bf16[192,1280]{1,0:T(8,128)(2,1)} %bitcast.21, bf16[64,1280]{1,0:T(8,128)(2,1)} %bitcast.29, bf16[192,1280]{1,0:T(8,128)(2,1)} %bitcast.23), custom_call_target="tpu_custom_call" | custom-call | tf_op jit(solution)/shard_map/pallas_call | solution.py:40
  4.3 23.2 %all-to-all-start = ((bf16[256,2,1280]{2,1,0:T(2,128)(2,1)}), bf16[256,2,1280]{2,1,0:T(2,128)(2,1)S(1)}, u32[]{:S(2)}, u32[]{:S(2)}) async-start(bf16[256,2,1280]{2,1,0:T(2,128)(2,1)} %bitcast.3.spent_ref), calls=%async_computation | async-start | bytes 2621440 | tf_op jit(solution)/shard_map/all_to_all | solution.py:196
  27.5 2.9 %collective-permute-start = (bf16[320,1280]{1,0:T(8,128)(2,1)S(1)}, bf16[320,1280]{1,0:T(8,128)(2,1)S(1)}, u32[]{:S(2)}, u32[]{:S(2)}) collective-permute-start(bf16[320,1280]{1,0:T(8,128)(2,1)S(1)} %bitcast.26), channel_id=1, source_target_pairs={{0,64},{64,0},{1,65},{65,1},{2,66},{66,2},{3,67},{67,3},{4,68},{68... | collective-permute-start | bytes 2457608 | tf_op jit(solution)/shard_map/ppermute | solution.py:200
  30.4 1.9 %collective-permute-start.1 = (bf16[320,1280]{1,0:T(8,128)(2,1)}, bf16[320,1280]{1,0:T(8,128)(2,1)S(1)}, u32[]{:S(2)}, u32[]{:S(2)}) collective-permute-start(bf16[320,1280]{1,0:T(8,128)(2,1)} %bitcast.5), channel_id=1, source_target_pairs={{0,64},{64,0},{1,65},{65,1},{2,66},{66,2},{3,67},{67,3},{4,68},{68... | collective-permute-start | bytes 2457608 | tf_op jit(solution)/shard_map/ppermute | solution.py:200
  32.3 1.3 pad_maximum_fusion.w_in_ref
  33.6 1.2 collective-permute-done.1
  34.8 2.4 %pad_maximum_fusion.1.w_out_hbm = bf16[640,1280]{1,0:T(8,128)(2,1)} fusion(bf16[320,1280]{1,0:T(8,128)(2,1)S(1)} %collective-permute-done.1, bf16[320,1280]{1,0:T(8,128)(2,1)} %bitcast.5), kind=kLoop, calls=%fused_computation.9 | loop fusion | flops 3276800 | bytes 3276800 | tf_op jit(solution)/shard_map/concatenate | solution.py:210
  37.3 25.7 %all-to-all-done.blocks_ref = bf16[256,2,1280]{2,1,0:T(2,128)(2,1)S(1)} async-done(((bf16[256,2,1280]{2,1,0:T(2,128)(2,1)}), bf16[256,2,1280]{2,1,0:T(2,128)(2,1)S(1)}, u32[]{:S(2)}, u32[]{:S(2)}) %all-to-all-start) | async-done | bytes 1310752 | tf_op jit(solution)/shard_map/all_to_all | solution.py:196
  62.9 4.7 %shard_map.85 = (bf16[640,256]{1,0:T(8,128)(2,1)S(1)}, bf16[640,256]{1,0:T(8,128)(2,1)S(1)}, bf16[256,2,1280]{2,1,0:T(2,128)(2,1)}) custom-call(bf16[256,2,1280]{2,1,0:T(2,128)(2,1)S(1)} %all-to-all-done.blocks_ref, bf16[640,1280]{1,0:T(8,128)(2,1)S(1)} %pad_maximum_fusion.w_in_ref, ...), custom_call_target="tpu_custom_call", output_to_operand_aliasing={{2}: (3, {})} | custom-call | tf_op jit(solution)/shard_map/pallas_call | solution.py:40
  67.7 0.7 copy-done.3
  68.4 10.0 %all-to-all-start.1 = ((bf16[256,2,1280]{2,1,0:T(2,128)(2,1)}), bf16[256,2,1280]{2,1,0:T(2,128)(2,1)S(1)}, u32[]{:S(2)}, u32[]{:S(2)}) async-start(bf16[256,2,1280]{2,1,0:T(2,128)(2,1)} %get-tuple-element.23), calls=%async_computation.1 | async-start | bytes 2621440 | tf_op jit(solution)/shard_map/all_to_all | solution.py:196
  78.4 1.8 %fusion.10 = (bf16[256,1,1280]{2,1,0:T(2,128)(2,1)S(1)}, bf16[256,1,1280]{2,1,0:T(2,128)(2,1)S(1)}) fusion(bf16[256,2,1280]{2,1,0:T(2,128)(2,1)S(1)} %all-to-all-done.blocks_ref), kind=kLoop, calls=%fused_computation.17 | loop fusion | bytes 2621440 | tf_op jit(solution)/shard_map/slice | solution.py:217
  80.2 0.6 fusion.3
  80.8 0.1 slice.40
  80.9 3.9 %collective-permute-start.3 = (bf16[320,1280]{1,0:T(8,128)(2,1)S(1)}, bf16[320,1280]{1,0:T(8,128)(2,1)S(1)}, u32[]{:S(2)}, u32[]{:S(2)}) collective-permute-start(bf16[320,1280]{1,0:T(8,128)(2,1)S(1)} %slice.40), channel_id=1, source_target_pairs={{0,64},{64,0},{1,65},{65,1},{2,66},{66,2},{3,67},{67,3},{4,68},{68... | collective-permute-start | bytes 2457608 | tf_op jit(solution)/shard_map/ppermute | solution.py:200
  84.9 0.6 fusion.6
  85.5 0.1 slice.41
  85.6 1.9 %collective-permute-start.2 = (bf16[320,1280]{1,0:T(8,128)(2,1)S(1)}, bf16[320,1280]{1,0:T(8,128)(2,1)S(1)}, u32[]{:S(2)}, u32[]{:S(2)}) collective-permute-start(bf16[320,1280]{1,0:T(8,128)(2,1)S(1)} %slice.41), channel_id=1, source_target_pairs={{0,64},{64,0},{1,65},{65,1},{2,66},{66,2},{3,67},{67,3},{4,68},{68... | collective-permute-start | bytes 2457608 | tf_op jit(solution)/shard_map/ppermute | solution.py:200
  87.5 1.1 fusion.1
  88.6 1.2 collective-permute-done.2
  89.8 1.1 fusion.2
  90.8 22.2 %all-to-all-done.1.parts_ref = bf16[256,2,1280]{2,1,0:T(2,128)(2,1)S(1)} async-done(((bf16[256,2,1280]{2,1,0:T(2,128)(2,1)}), bf16[256,2,1280]{2,1,0:T(2,128)(2,1)S(1)}, u32[]{:S(2)}, u32[]{:S(2)}) %all-to-all-start.1) | async-done | bytes 1310752 | tf_op jit(solution)/shard_map/all_to_all | solution.py:196
  113.1 2.4 %shard_map.86 = (bf16[64,1280]{1,0:T(8,128)(2,1)S(1)}, bf16[192,64]{1,0:T(8,128)(2,1)S(1)}, bf16[32,2,1280]{2,1,0:T(2,128)(2,1)}) custom-call(bf16[192,1280]{1,0:T(8,128)(2,1)S(1)} %bitcast.22, bf16[192,1280]{1,0:T(8,128)(2,1)S(1)} %bitcast.24, f32[192,64]{1,0:T(8,128)S(1)} %copy-done.2, f32[192,64]{1,0:T(8,128)S(1)} %copy-done.6, ...), custom_call_target="tpu_custom_call" | custom-call | tf_op jit(solution)/shard_map/pallas_call | solution.py:40
  115.5 3.9 %all-to-all-start.2 = ((bf16[32,2,1280]{2,1,0:T(2,128)(2,1)}), bf16[32,2,1280]{2,1,0:T(2,128)(2,1)S(1)}, u32[]{:S(2)}, u32[]{:S(2)}) async-start(bf16[32,2,1280]{2,1,0:T(2,128)(2,1)} %get-tuple-element.27), calls=%async_computation.2 | async-start | bytes 327680 | tf_op jit(solution)/shard_map/all_to_all | solution.py:196
  119.4 0.3 fusion.11
  119.7 1.0 fusion
  120.7 7.9 %all-to-all-done.2 = bf16[32,2,1280]{2,1,0:T(2,128)(2,1)S(1)} async-done(((bf16[32,2,1280]{2,1,0:T(2,128)(2,1)}), bf16[32,2,1280]{2,1,0:T(2,128)(2,1)S(1)}, u32[]{:S(2)}, u32[]{:S(2)}) %all-to-all-start.2) | async-done | bytes 163872 | tf_op jit(solution)/shard_map/all_to_all | solution.py:196
  128.6 0.2 reduce_sum.24
  128.9 15.8 %all_to_all.25 = bf16[16,2,1280]{2,1,0:T(2,128)(2,1)S(1)} all-to-all(bf16[16,2,1280]{2,1,0:T(2,128)(2,1)S(1)} %broadcast_in_dim.22), channel_id=1, replica_groups=mesh['y_lo'=4,'core'=2,'y_hi'=2,'x'=4,'z'=8] {'y_lo','core','y_hi'}, dimensions={0} | all-to-all | bytes 163840 | tf_op jit(solution)/shard_map/all_to_all | solution.py:196
  144.7 0.1 broadcast_in_dim.23
  144.8 12.6 %all_to_all.26 = bf16[32,2,1280]{2,1,0:T(2,128)(2,1)S(1)} all-to-all(bf16[32,2,1280]{2,1,0:T(2,128)(2,1)S(1)} %broadcast_in_dim.23), channel_id=1, replica_groups=mesh['y_lo'=4,'core'=2,'y_hi'=2,'x'=4,'z'=8] {'x','z'}, dimensions={0} | all-to-all | bytes 327680 | tf_op jit(solution)/shard_map/all_to_all | solution.py:196
  157.4 0.7 reshape.17
  (21 shorter events, 0.2 us)
Async XLA Ops:
  0.6 26.9 %copy-start.7 = (bf16[1,320,1280]{2,1,0:T(8,128)(2,1)S(1)}, bf16[1,320,1280]{2,1,0:T(8,128)(2,1)}, u32[]{:S(2)}) copy-start(bf16[1,320,1280]{2,1,0:T(8,128)(2,1)} %param.8) | copy-start | bytes 2457604
  4.3 58.7 %all-to-all-start = ((bf16[256,2,1280]{2,1,0:T(2,128)(2,1)}), bf16[256,2,1280]{2,1,0:T(2,128)(2,1)S(1)}, u32[]{:S(2)}, u32[]{:S(2)}) async-start(bf16[256,2,1280]{2,1,0:T(2,128)(2,1)} %bitcast.3.spent_ref), calls=%async_computation | async-start | bytes 2621440 | tf_op jit(solution)/shard_map/all_to_all | solution.py:196
  27.5 4.8 %collective-permute-start = (bf16[320,1280]{1,0:T(8,128)(2,1)S(1)}, bf16[320,1280]{1,0:T(8,128)(2,1)S(1)}, u32[]{:S(2)}, u32[]{:S(2)}) collective-permute-start(bf16[320,1280]{1,0:T(8,128)(2,1)S(1)} %bitcast.26), channel_id=1, source_target_pairs={{0,64},{64,0},{1,65},{65,1},{2,66},{66,2},{3,67},{67,3},{4,68},{68... | collective-permute-start | bytes 2457608 | tf_op jit(solution)/shard_map/ppermute | solution.py:200
  30.4 4.4 %collective-permute-start.1 = (bf16[320,1280]{1,0:T(8,128)(2,1)}, bf16[320,1280]{1,0:T(8,128)(2,1)S(1)}, u32[]{:S(2)}, u32[]{:S(2)}) collective-permute-start(bf16[320,1280]{1,0:T(8,128)(2,1)} %bitcast.5), channel_id=1, source_target_pairs={{0,64},{64,0},{1,65},{65,1},{2,66},{66,2},{3,67},{67,3},{4,68},{68... | collective-permute-start | bytes 2457608 | tf_op jit(solution)/shard_map/ppermute | solution.py:200
  67.7 0.7 copy-start.3
  68.4 44.7 %all-to-all-start.1 = ((bf16[256,2,1280]{2,1,0:T(2,128)(2,1)}), bf16[256,2,1280]{2,1,0:T(2,128)(2,1)S(1)}, u32[]{:S(2)}, u32[]{:S(2)}) async-start(bf16[256,2,1280]{2,1,0:T(2,128)(2,1)} %get-tuple-element.23), calls=%async_computation.1 | async-start | bytes 2621440 | tf_op jit(solution)/shard_map/all_to_all | solution.py:196
  78.4 1.8 %copy-start.4 = (bf16[640,256]{1,0:T(8,128)(2,1)S(1)}, bf16[640,256]{1,0:T(8,128)(2,1)}, u32[]{:S(2)}) copy-start(bf16[640,256]{1,0:T(8,128)(2,1)} %copy-done.3) | copy-start | bytes 983044
  80.9 6.6 %collective-permute-start.3 = (bf16[320,1280]{1,0:T(8,128)(2,1)S(1)}, bf16[320,1280]{1,0:T(8,128)(2,1)S(1)}, u32[]{:S(2)}, u32[]{:S(2)}) collective-permute-start(bf16[320,1280]{1,0:T(8,128)(2,1)S(1)} %slice.40), channel_id=1, source_target_pairs={{0,64},{64,0},{1,65},{65,1},{2,66},{66,2},{3,67},{67,3},{4,68},{68... | collective-permute-start | bytes 2457608 | tf_op jit(solution)/shard_map/ppermute | solution.py:200
  85.6 4.2 %collective-permute-start.2 = (bf16[320,1280]{1,0:T(8,128)(2,1)S(1)}, bf16[320,1280]{1,0:T(8,128)(2,1)S(1)}, u32[]{:S(2)}, u32[]{:S(2)}) collective-permute-start(bf16[320,1280]{1,0:T(8,128)(2,1)S(1)} %slice.41), channel_id=1, source_target_pairs={{0,64},{64,0},{1,65},{65,1},{2,66},{66,2},{3,67},{67,3},{4,68},{68... | collective-permute-start | bytes 2457608 | tf_op jit(solution)/shard_map/ppermute | solution.py:200
  88.6 24.5 %copy-start = (bf16[1,192,1280]{2,1,0:T(8,128)(2,1)S(1)}, bf16[1,192,1280]{2,1,0:T(8,128)(2,1)}, u32[]{:S(2)}) copy-start(bf16[1,192,1280]{2,1,0:T(8,128)(2,1)} %param.5) | copy-start | bytes 1474564
  88.6 24.5 %copy-start.1 = (bf16[1,192,1280]{2,1,0:T(8,128)(2,1)S(1)}, bf16[1,192,1280]{2,1,0:T(8,128)(2,1)}, u32[]{:S(2)}) copy-start(bf16[1,192,1280]{2,1,0:T(8,128)(2,1)} %param.6) | copy-start | bytes 1474564
  88.6 24.5 %copy-start.2 = (f32[192,64]{1,0:T(8,128)S(1)}, f32[192,64]{1,0:T(8,128)}, u32[]{:S(2)}) copy-start(f32[192,64]{1,0:T(8,128)} %get-tuple-element.19.dispatch_ref) | copy-start | bytes 147460
  88.6 24.5 %copy-start.5 = (bf16[64,1280]{1,0:T(8,128)(2,1)S(1)}, bf16[64,1280]{1,0:T(8,128)(2,1)}, u32[]{:S(2)}) copy-start(bf16[64,1280]{1,0:T(8,128)(2,1)} %get-tuple-element.21.own_ref) | copy-start | bytes 491524
  88.6 24.5 %copy-start.6 = (f32[192,64]{1,0:T(8,128)S(1)}, f32[192,64]{1,0:T(8,128)}, u32[]{:S(2)}) copy-start(f32[192,64]{1,0:T(8,128)} %get-tuple-element.20.combine_ref) | copy-start | bytes 147460
  90.8 28.6 %copy-start.8 = (bf16[1280,64]{0,1:T(8,128)(2,1)S(1)}, bf16[1280,64]{0,1:T(8,128)(2,1)}, u32[]{:S(2)}) copy-start(bf16[1280,64]{0,1:T(8,128)(2,1)} %param.7) | copy-start | bytes 491524
  115.5 13.1 %all-to-all-start.2 = ((bf16[32,2,1280]{2,1,0:T(2,128)(2,1)}), bf16[32,2,1280]{2,1,0:T(2,128)(2,1)S(1)}, u32[]{:S(2)}, u32[]{:S(2)}) async-start(bf16[32,2,1280]{2,1,0:T(2,128)(2,1)} %get-tuple-element.27), calls=%async_computation.2 | async-start | bytes 327680 | tf_op jit(solution)/shard_map/all_to_all | solution.py:196

commit v10 on v9

--- a/solution.py
+++ b/solution.py
@@ -8,11 +8,11 @@
 from jax.sharding import Mesh, PartitionSpec as P
 
 SWAP = [(0, 1), (1, 0)]
-DP = ("y_lo", "core")
+DP = ("y_pair", "y_side", "core")
 EXPERT = ("y_hi", "x", "z")
-CHIPS = ("y_lo",) + EXPERT
+CHIPS = ("y_pair",) + EXPERT
 PLANE = ("x", "z")
-LINE = ("y_lo", "core", "y_hi")
+LINE = ("y_pair", "y_side", "core", "y_hi")
 BF = jnp.bfloat16
 F32 = jnp.float32
 
@@ -81,29 +81,27 @@
     copies[-1].start()
     copy.wait()
     pair[:, 1, :] = dot_first(combine.astype(BF), grad[...]).astype(BF)
-    late = [pltpu.make_async_copy(pair, out_ref.at[i], sems.at[i]) for i in range(4)]
+    late = [pltpu.make_async_copy(pair, out_ref.at[i], sems.at[i]) for i in range(2)]
     for each in late:
         each.start()
     for each in copies + late:
         each.wait()
 
 
-def expert_kernel(
-    blocks_ref, w_in_ref, w_out_hbm, spent_ref, hid_ref, grad_ref, out_ref, buffer, w_out_ref, sems
-):
-    del spent_ref
-    load = pltpu.make_async_copy(w_out_hbm, w_out_ref, sems.at[0])
-    load.start()
+def expert_kernel(*refs):
+    *blocks, w_in_ref, w_out_ref, hid_ref, grad_ref = refs[: len(refs) // 2 + 2]
+    outs = refs[len(refs) // 2 + 2 :]
     row = lax.broadcasted_iota(jnp.int32, (128, 128), 0)
     col = lax.broadcasted_iota(jnp.int32, (128, 128), 1)
     sort = (col == 2 * (row & 63) + (row >> 6)).astype(BF)
-    rows = blocks_ref.reshape(512, 1280)
     sorted_rows = [
-        jnp.dot(sort, rows[pl.ds(at, 128)], preferred_element_type=F32).astype(BF)
-        for at in range(0, 512, 128)
+        jnp.dot(
+            sort, ref.reshape(2 * ref.shape[0], 1280)[pl.ds(at, 128)], preferred_element_type=F32
+        ).astype(BF)
+        for ref in blocks
+        for at in range(0, 2 * ref.shape[0], 128)
     ]
     v = dot_last(w_in_ref[...], jnp.concatenate([part[:64] for part in sorted_rows]))
-    load.wait()
     upstream = dot_last(w_out_ref[...], jnp.concatenate([part[64:] for part in sorted_rows]))
     square = v * v
     half = 0.5 * jnp.tanh(v * (GELU_A + (GELU_A * GELU_B) * square)) + 0.5
@@ -113,11 +111,12 @@
     grad = (slope * upstream).astype(BF)
     hid_ref[...] = hid
     grad_ref[...] = grad
-    buffer[:, 0, :] = dot_first(hid, w_out_ref[...]).astype(BF)
-    buffer[:, 1, :] = dot_first(grad, w_in_ref[...]).astype(BF)
-    copy = pltpu.make_async_copy(buffer, out_ref, sems.at[1])
-    copy.start()
-    copy.wait()
+    for kind, rows in enumerate((dot_first(hid, w_out_ref[...]), dot_first(grad, w_in_ref[...]))):
+        rows = rows.astype(BF)
+        at = 0
+        for ref in outs:
+            ref[:, kind, :] = rows[at : at + ref.shape[0]]
+            at += ref.shape[0]
 
 
 def logit_kernel(
@@ -127,11 +126,11 @@
     copy = pltpu.make_async_copy(grad_hbm, grad, sem)
     copy.start()
     tokens = tokens_ref[...]
-    row = lax.broadcasted_iota(jnp.int32, (128, 512), 0)
-    col = lax.broadcasted_iota(jnp.int32, (128, 512), 1) & 127
+    row = lax.broadcasted_iota(jnp.int32, (128, 256), 0)
+    col = lax.broadcasted_iota(jnp.int32, (128, 256), 1) & 127
     adder = (col == 2 * (row & 63) + (row >> 6)).astype(BF)
     slots = jnp.dot(
-        adder, parts_ref.reshape(512, 1280)[...], preferred_element_type=F32
+        adder, parts_ref.reshape(256, 1280)[...], preferred_element_type=F32
     ).astype(BF)
     slot_out, slot_in_grad = slots[:64], slots[64:]
     slot_ref[...] = slot_in_grad
@@ -156,7 +155,7 @@
         shape(192, 64, dtype=F32),
         shape(192, 64, dtype=F32),
         shape(64, 1280),
-        shape(4, 64, 2, 1280),
+        shape(2, 64, 2, 1280),
     ),
     (HBM,) * 4,
     (
@@ -170,19 +169,9 @@
     {2: HBM},
     grant=63_000_000,
 )
-experts = on_core(
-    expert_kernel,
-    (shape(640, 256), shape(640, 256), shape(256, 2, 1280)),
-    (VMEM, VMEM, HBM),
-    (
-        pltpu.VMEM((256, 2, 1280), BF),
-        pltpu.VMEM((640, 1280), BF),
-        pltpu.SemaphoreType.DMA((2,)),
-    ),
-    {2: HBM, 3: HBM},
-    {3: 2},
-    grant=48 * 2**20,
-)
+ACTS = (shape(640, 128), shape(640, 128))
+experts_near = on_core(expert_kernel, ACTS + (shape(128, 2, 1280),), (VMEM,) * 3)
+experts_far = on_core(expert_kernel, ACTS + (shape(64, 2, 1280),) * 2, (VMEM,) * 4)
 logits_back = on_core(
     logit_kernel,
     (shape(64, 1280), shape(192, 64), shape(32, 2, 1280)),
@@ -196,6 +185,10 @@
     return lax.all_to_all(blocks, axes, split_axis=0, concat_axis=0, tiled=True)
 
 
+def across(value):
+    return lax.ppermute(value, "y_side", SWAP)
+
+
 def swap(value):
     return lax.ppermute(value, "core", SWAP)
 
@@ -209,12 +202,16 @@
     all_in = jnp.concatenate([w_in, swap(w_in)])
     all_out = jnp.concatenate([w_out, swap(w_out)])
     dispatch, combine, own_in, spent = image_slots(tokens, router.T, grad_out)
-    spent = spent.reshape(256, 2, 1280)
-    blocks = exchange(spent, CHIPS)
-    hid, preact_grad, partial = experts(blocks, all_in, all_out, spent)
+    near = exchange(spent.reshape(128, 2, 1280), CHIPS)
+    far = (across(near[:64]), across(near[64:]))
+    hid_near, grad_near, part_near = experts_near(near, all_in, all_out)
+    hid_far, grad_far, *part_far = experts_far(*far, all_in, all_out)
+    part_got = jnp.concatenate([across(part) for part in part_far])
+    partial = (part_near.astype(F32) + part_got.astype(F32)).astype(BF)
     parts = exchange(partial, CHIPS)
-    d_in = dot("hi,id->hd", preact_grad, blocks[:, 0])
-    d_out = dot("hi,id->hd", hid, blocks[:, 1])
+    blocks = jnp.concatenate((near,) + far)
+    d_in = dot("hi,id->hd", jnp.concatenate([grad_near, grad_far], axis=1), blocks[:, 0])
+    d_out = dot("hi,id->hd", jnp.concatenate([hid_near, hid_far], axis=1), blocks[:, 1])
     d_w_in = (d_in[:320] + swap(d_in[320:].astype(BF)).astype(F32)).astype(BF)
     d_w_out = (d_out[:320] + swap(d_out[320:].astype(BF)).astype(F32)).astype(BF)
     parts, d_w_in, d_w_out = lax.optimization_barrier((parts, d_w_in, d_w_out))
@@ -236,7 +233,7 @@
 
 def solution(mesh):
     fine = Mesh(
-        mesh.devices.reshape(4, 2, 2, 4, 8), ("y_lo", "core", "y_hi", "x", "z")
+        mesh.devices.reshape(2, 2, 2, 2, 4, 8), ("y_pair", "y_side", "core", "y_hi", "x", "z")
     )
     image = P(DP + EXPERT, None, None)
     unit = P(EXPERT, DP, None)

time: 159 us -> 162 us (1.019)
  starting transfers between devices: 47.7 us -> 54.3 us
  waiting for transfers between devices: 58.3 us -> 53.8 us
  local copies, waits for them, and re-layouts: 3.6 us -> 5.3 us
    ppermute x0 -> x4, starting transfers between devices: none -> 10.6 us  [across(): return lax.ppermute(value, 'y_side', SWAP)]
    all_to_all x3, waiting for transfers between devices: 55.8 us -> 46.4 us  [exchange(): return lax.all_to_all(blocks, axes, split_axis=0, concat_axis=0, tiled=True)]
    ppermute x0 -> x4, waiting for transfers between devices: none -> 7.43 us  [across(): return lax.ppermute(value, 'y_side', SWAP)]
    all_to_all x3, starting transfers between devices: 37.1 us -> 32.1 us  [exchange(): return lax.all_to_all(blocks, axes, split_axis=0, concat_axis=0, tiled=True)]
    ppermute x4, waiting for transfers between devices: 2.45 us -> 0.01 us  [swap(): return lax.ppermute(value, 'core', SWAP)]
    convert_element_type x0 -> x1, other arithmetic: none -> 1.68 us  [local(): partial = (part_near.astype(F32) + part_got.astype(F32)).astype(BF)]
    pallas_call x3 -> x4, Pallas kernels: 10.8 us -> 9.8 us  [call(): pl.pallas_call(kernel, out_shape=outs, in_specs=[(in_specs or {}).get(i,...]
  transfers between devices with their start and end apart: 7 -> 11, of which waited for: 5 -> 5; matrix products, arithmetic and copies ran while one was open for 7% -> 9% of each run, Pallas kernels for 0% -> 1%
where the time goes in v10:
time: 162 us
  starting transfers between devices  54.3 us (34%)
  waiting for transfers between devices  53.8 us (33%)
  blocking collectives  27.9 us (17%)
  Pallas kernels  9.8 us (6%)
  other arithmetic  7.25 us (4%)
  local copies, waits for them, and re-layouts  5.3 us (3%)
  matrix products  2.5 us (2%)
    all_to_all x3, waiting for transfers between devices, exchange(): return lax.all_to_all(blocks, axes, split_axis=0, concat_axis=0, tiled=True)  46.4 us
    all_to_all x3, starting transfers between devices, exchange(): return lax.all_to_all(blocks, axes, split_axis=0, concat_axis=0, tiled=True)  32.1 us
    all_to_all x2, blocking collectives, exchange(): return lax.all_to_all(blocks, axes, split_axis=0, concat_axis=0, tiled=True)  27.9 us
    ppermute x4, starting transfers between devices, swap(): return lax.ppermute(value, 'core', SWAP)  11.6 us
    ppermute x4, starting transfers between devices, across(): return lax.ppermute(value, 'y_side', SWAP)  10.6 us
    pallas_call x4, Pallas kernels, call(): pl.pallas_call(kernel, out_shape=outs, in_specs=[(in_specs or {}).get(i,...  9.8 us
    ppermute x4, waiting for transfers between devices, across(): return lax.ppermute(value, 'y_side', SWAP)  7.43 us
  transfers between devices with their start and end apart: 11, of which 5 were waited for; matrix products, arithmetic and copies ran while one was open for 9% of the time, Pallas kernels for 1%

profile of v10, /device:TPU:1, one launch (start us, length us, event | category | flops | bytes accessed | tf_op | source)
XLA Modules:
  0.0 161.8 jit_solution(13682229888380680067)
XLA Ops:
  0.6 3.4 %shard_map.84 = (f32[192,64]{1,0:T(8,128)}, f32[192,64]{1,0:T(8,128)}, bf16[64,1280]{1,0:T(8,128)(2,1)}, bf16[2,64,2,1280]{3,2,1,0:T(2,128)(2,1)}) custom-call(bf16[192,1280]{1,0:T(8,128)(2,1)} %bitcast.19, bf16[64,1280]{1,0:T(8,128)(2,1)} %bitcast.27, bf16[192,1280]{1,0:T(8,128)(2,1)} %bitcast.21), custom_call_target="tpu_custom_call" | custom-call | tf_op jit(solution)/shard_map/pallas_call | solution.py:40
  4.1 20.8 %all-to-all-start = ((bf16[128,2,1280]{2,1,0:T(2,128)(2,1)}), bf16[128,2,1280]{2,1,0:T(2,128)(2,1)S(1)}, u32[]{:S(2)}, u32[]{:S(2)}) async-start(bf16[128,2,1280]{2,1,0:T(2,128)(2,1)} %bitcast.28), calls=%async_computation | async-start | bytes 1310720 | tf_op jit(solution)/shard_map/all_to_all | solution.py:185
  24.9 2.9 %collective-permute-start = (bf16[320,1280]{1,0:T(8,128)(2,1)S(1)}, bf16[320,1280]{1,0:T(8,128)(2,1)S(1)}, u32[]{:S(2)}, u32[]{:S(2)}) collective-permute-start(bf16[320,1280]{1,0:T(8,128)(2,1)S(1)} %bitcast.23), channel_id=1, source_target_pairs={{0,64},{64,0},{1,65},{65,1},{2,66},{66,2},{3,67},{67,3},{4,68},{68... | collective-permute-start | bytes 2457608 | tf_op jit(solution)/shard_map/ppermute | solution.py:193
  27.8 1.9 %collective-permute-start.1 = (bf16[320,1280]{1,0:T(8,128)(2,1)}, bf16[320,1280]{1,0:T(8,128)(2,1)}, u32[]{:S(2)}, u32[]{:S(2)}) collective-permute-start(bf16[320,1280]{1,0:T(8,128)(2,1)} %bitcast.5), channel_id=1, source_target_pairs={{0,64},{64,0},{1,65},{65,1},{2,66},{66,2},{3,67},{67,3},{4,68},{68... | collective-permute-start | bytes 2457608 | tf_op jit(solution)/shard_map/ppermute | solution.py:193
  29.8 19.4 %all-to-all-done.refs_0_ = bf16[128,2,1280]{2,1,0:T(2,128)(2,1)S(1)} async-done(((bf16[128,2,1280]{2,1,0:T(2,128)(2,1)}), bf16[128,2,1280]{2,1,0:T(2,128)(2,1)S(1)}, u32[]{:S(2)}, u32[]{:S(2)}) %all-to-all-start) | async-done | bytes 655392 | tf_op jit(solution)/shard_map/all_to_all | solution.py:185
  49.7 1.9 %collective-permute-start.3 = (bf16[64,2,1280]{2,1,0:T(2,128)(2,1)S(1)}, bf16[64,2,1280]{2,1,0:T(2,128)(2,1)S(1)}, u32[]{:S(2)}, u32[]{:S(2)}) collective-permute-start(bf16[64,2,1280]{2,1,0:T(2,128)(2,1)S(1)} %get-tuple-element.44), channel_id=1, source_target_pairs={{0,128},{128,0},{1,129},{129,1},{2,130},{130,2},{3,131},{131,3},{4... | collective-permute-start | bytes 983048 | tf_op jit(solution)/shard_map/ppermute | solution.py:189
  51.6 3.4 %collective-permute-start.2 = (bf16[64,2,1280]{2,1,0:T(2,128)(2,1)S(1)}, bf16[64,2,1280]{2,1,0:T(2,128)(2,1)S(1)}, u32[]{:S(2)}, u32[]{:S(2)}) collective-permute-start(bf16[64,2,1280]{2,1,0:T(2,128)(2,1)S(1)} %get-tuple-element.45), channel_id=1, source_target_pairs={{0,128},{128,0},{1,129},{129,1},{2,130},{130,2},{3,131},{131,3},{4... | collective-permute-start | bytes 983048 | tf_op jit(solution)/shard_map/ppermute | solution.py:189
  55.0 1.5 pad_maximum_fusion.1.refs_2_.refs_3_
  56.5 2.0 %shard_map.85 = (bf16[640,128]{1,0:T(8,128)(2,1)S(1)}, bf16[640,128]{1,0:T(8,128)(2,1)S(1)}, bf16[128,2,1280]{2,1,0:T(2,128)(2,1)S(1)}) custom-call(bf16[128,2,1280]{2,1,0:T(2,128)(2,1)S(1)} %all-to-all-done.refs_0_, bf16[640,1280]{1,0:T(8,128)(2,1)S(1)} %pad_maximum_fusion.refs_1_.refs_2_, bf16[640,1280]{1,0:T(8,128)(2,1)S(1)} %pad_maximum_fusion.1.refs_2_.refs_3_), custom_call_target="tpu_custom_call" | custom-call | tf_op jit(solution)/shard_map/pallas_call | solution.py:40
  58.5 0.5 constant_dynamic-update-slice_fusion.2
  59.4 7.0 %collective-permute-done.2.refs_0_ = bf16[64,2,1280]{2,1,0:T(2,128)(2,1)S(1)} collective-permute-done((bf16[64,2,1280]{2,1,0:T(2,128)(2,1)S(1)}, bf16[64,2,1280]{2,1,0:T(2,128)(2,1)S(1)}, u32[]{:S(2)}, u32[]{:S(2)}) %collective-permute-start.2) | collective-permute-done | bytes 327712 | tf_op jit(solution)/shard_map/ppermute | solution.py:189
  66.4 2.0 %shard_map.86 = (bf16[640,128]{1,0:T(8,128)(2,1)S(1)}, bf16[640,128]{1,0:T(8,128)(2,1)S(1)}, bf16[64,2,1280]{2,1,0:T(2,128)(2,1)S(1)}, bf16[64,2,1280]{2,1,0:T(2,128)(2,1)S(1)}) custom-call(bf16[64,2,1280]{2,1,0:T(2,128)(2,1)S(1)} %collective-permute-done.2.refs_0_, bf16[64,2,1280]{2,1,0:T(2,128)(2,1)S(1)} %collective-permute-done.3.refs_1_, ...), custom_call_target="tpu_custom_call" | custom-call | tf_op jit(solution)/shard_map/pallas_call | solution.py:40
  68.4 2.2 %collective-permute-start.4 = (bf16[64,2,1280]{2,1,0:T(2,128)(2,1)S(1)}, bf16[64,2,1280]{2,1,0:T(2,128)(2,1)S(1)}, u32[]{:S(2)}, u32[]{:S(2)}) collective-permute-start(bf16[64,2,1280]{2,1,0:T(2,128)(2,1)S(1)} %get-tuple-element.28), channel_id=1, source_target_pairs={{0,128},{128,0},{1,129},{129,1},{2,130},{130,2},{3,131},{131,3},{4... | collective-permute-start | bytes 983048 | tf_op jit(solution)/shard_map/ppermute | solution.py:189
  70.6 3.1 %collective-permute-start.5 = (bf16[64,2,1280]{2,1,0:T(2,128)(2,1)S(1)}, bf16[64,2,1280]{2,1,0:T(2,128)(2,1)S(1)}, u32[]{:S(2)}, u32[]{:S(2)}) collective-permute-start(bf16[64,2,1280]{2,1,0:T(2,128)(2,1)S(1)} %get-tuple-element.29), channel_id=1, source_target_pairs={{0,128},{128,0},{1,129},{129,1},{2,130},{130,2},{3,131},{131,3},{4... | collective-permute-start | bytes 983048 | tf_op jit(solution)/shard_map/ppermute | solution.py:189
  74.3 1.8 %fusion.18 = (bf16[256,1,1280]{2,1,0:T(2,128)(2,1)S(1)}, bf16[256,1,1280]{2,1,0:T(2,128)(2,1)S(1)}) fusion(bf16[256,2,1280]{2,1,0:T(2,128)(2,1)S(1)} %constant_dynamic-update-slice_fusion), kind=kLoop, calls=%fused_computation.29 | loop fusion | bytes 2621440 | tf_op jit(solution)/shard_map/slice | solution.py:214
  76.1 0.6 fusion.3
  76.8 4.8 %collective-permute-start.7 = (bf16[320,1280]{1,0:T(8,128)(2,1)S(1)}, bf16[320,1280]{1,0:T(8,128)(2,1)S(1)}, u32[]{:S(2)}, u32[]{:S(2)}) collective-permute-start(bf16[320,1280]{1,0:T(8,128)(2,1)S(1)} %slice.50), channel_id=1, source_target_pairs={{0,64},{64,0},{1,65},{65,1},{2,66},{66,2},{3,67},{67,3},{4,68},{68... | collective-permute-start | bytes 2457608 | tf_op jit(solution)/shard_map/ppermute | solution.py:193
  81.6 0.6 fusion.6
  82.2 1.1 slice.51
  83.3 2.1 %collective-permute-start.6 = (bf16[320,1280]{1,0:T(8,128)(2,1)}, bf16[320,1280]{1,0:T(8,128)(2,1)S(1)}, u32[]{:S(2)}, u32[]{:S(2)}) collective-permute-start(bf16[320,1280]{1,0:T(8,128)(2,1)} %slice.51), channel_id=1, source_target_pairs={{0,64},{64,0},{1,65},{65,1},{2,66},{66,2},{3,67},{67,3},{4,68},{68... | collective-permute-start | bytes 2457608 | tf_op jit(solution)/shard_map/ppermute | solution.py:193
  85.4 1.7 %add_convert_fusion = bf16[128,2,1280]{2,1,0:T(2,128)(2,1)} fusion(bf16[128,2,1280]{2,1,0:T(2,128)(2,1)S(1)} %get-tuple-element.27, bf16[64,2,1280]{2,1,0:T(2,128)(2,1)S(1)} %collective-permute-done.5, bf16[64,2,1280]{2,1,0:T(2,128)(2,1)S(1)} %collective-permute-done.4), kind=kLoop, calls=%fused_computation.10 | loop fusion | flops 1638400 | bytes 1966080 | tf_op jit(solution)/shard_map/convert_element_type | solution.py:210
  87.1 7.4 %all-to-all-start.1 = ((bf16[128,2,1280]{2,1,0:T(2,128)(2,1)}), bf16[128,2,1280]{2,1,0:T(2,128)(2,1)S(1)}, u32[]{:S(2)}, u32[]{:S(2)}) async-start(bf16[128,2,1280]{2,1,0:T(2,128)(2,1)} %add_convert_fusion), calls=%async_computation.1 | async-start | bytes 1310720 | tf_op jit(solution)/shard_map/all_to_all | solution.py:185
  94.4 2.6 %fusion.1 = bf16[320,1280]{1,0:T(8,128)(2,1)} fusion(f32[640,1280]{1,0:T(8,128)} %copy-done.5, bf16[320,1280]{1,0:T(8,128)(2,1)S(1)} %collective-permute-done.7), kind=kLoop, calls=%fused_computation.4 | loop fusion | flops 1228800 | bytes 3276800 | tf_op jit(solution)/shard_map/convert_element_type | solution.py:216
  97.1 1.1 fusion.2
  98.2 19.1 %all-to-all-done.1.parts_ref = bf16[128,2,1280]{2,1,0:T(2,128)(2,1)S(1)} async-done(((bf16[128,2,1280]{2,1,0:T(2,128)(2,1)}), bf16[128,2,1280]{2,1,0:T(2,128)(2,1)S(1)}, u32[]{:S(2)}, u32[]{:S(2)}) %all-to-all-start.1) | async-done | bytes 655392 | tf_op jit(solution)/shard_map/all_to_all | solution.py:185
  117.3 2.3 %shard_map.87 = (bf16[64,1280]{1,0:T(8,128)(2,1)S(1)}, bf16[192,64]{1,0:T(8,128)(2,1)S(1)}, bf16[32,2,1280]{2,1,0:T(2,128)(2,1)}) custom-call(bf16[192,1280]{1,0:T(8,128)(2,1)S(1)} %bitcast.20, bf16[192,1280]{1,0:T(8,128)(2,1)S(1)} %bitcast.22, f32[192,64]{1,0:T(8,128)S(1)} %copy-done.2, f32[192,64]{1,0:T(8,128)S(1)} %copy-done.4, ...), custom_call_target="tpu_custom_call" | custom-call | tf_op jit(solution)/shard_map/pallas_call | solution.py:40
  119.7 3.9 %all-to-all-start.2 = ((bf16[32,2,1280]{2,1,0:T(2,128)(2,1)}), bf16[32,2,1280]{2,1,0:T(2,128)(2,1)S(1)}, u32[]{:S(2)}, u32[]{:S(2)}) async-start(bf16[32,2,1280]{2,1,0:T(2,128)(2,1)} %get-tuple-element.35), calls=%async_computation.2 | async-start | bytes 327680 | tf_op jit(solution)/shard_map/all_to_all | solution.py:185
  123.8 1.1 fusion
  124.9 7.9 %all-to-all-done.2 = bf16[32,2,1280]{2,1,0:T(2,128)(2,1)S(1)} async-done(((bf16[32,2,1280]{2,1,0:T(2,128)(2,1)}), bf16[32,2,1280]{2,1,0:T(2,128)(2,1)S(1)}, u32[]{:S(2)}, u32[]{:S(2)}) %all-to-all-start.2) | async-done | bytes 163872 | tf_op jit(solution)/shard_map/all_to_all | solution.py:185
  133.0 15.3 %all_to_all.25 = bf16[16,2,1280]{2,1,0:T(2,128)(2,1)S(1)} all-to-all(bf16[16,2,1280]{2,1,0:T(2,128)(2,1)S(1)} %broadcast_in_dim.22), channel_id=1, replica_groups=mesh['y_pair'=2,'y_side'=2,'core'=2,'y_hi'=2,'x'=4,'z'=8] {'y_pair','y_s..., dimensions={0} | all-to-all | bytes 163840 | tf_op jit(solution)/shard_map/all_to_all | solution.py:185
  148.5 12.6 %all_to_all.26 = bf16[32,2,1280]{2,1,0:T(2,128)(2,1)S(1)} all-to-all(bf16[32,2,1280]{2,1,0:T(2,128)(2,1)S(1)} %broadcast_in_dim.23), channel_id=1, replica_groups=mesh['y_pair'=2,'y_side'=2,'core'=2,'y_hi'=2,'x'=4,'z'=8] {'x','z'}, dimensions={0} | all-to-all | bytes 327680 | tf_op jit(solution)/shard_map/all_to_all | solution.py:185
  161.1 0.7 reshape.17
  (37 shorter events, 2.3 us)
Async XLA Ops:
  0.6 24.3 %copy-start.8 = (bf16[1,320,1280]{2,1,0:T(8,128)(2,1)S(1)}, bf16[1,320,1280]{2,1,0:T(8,128)(2,1)}, u32[]{:S(2)}) copy-start(bf16[1,320,1280]{2,1,0:T(8,128)(2,1)} %param.8) | copy-start | bytes 2457604
  4.1 45.1 %all-to-all-start = ((bf16[128,2,1280]{2,1,0:T(2,128)(2,1)}), bf16[128,2,1280]{2,1,0:T(2,128)(2,1)S(1)}, u32[]{:S(2)}, u32[]{:S(2)}) async-start(bf16[128,2,1280]{2,1,0:T(2,128)(2,1)} %bitcast.28), calls=%async_computation | async-start | bytes 1310720 | tf_op jit(solution)/shard_map/all_to_all | solution.py:185
  24.9 4.8 %collective-permute-start = (bf16[320,1280]{1,0:T(8,128)(2,1)S(1)}, bf16[320,1280]{1,0:T(8,128)(2,1)S(1)}, u32[]{:S(2)}, u32[]{:S(2)}) collective-permute-start(bf16[320,1280]{1,0:T(8,128)(2,1)S(1)} %bitcast.23), channel_id=1, source_target_pairs={{0,64},{64,0},{1,65},{65,1},{2,66},{66,2},{3,67},{67,3},{4,68},{68... | collective-permute-start | bytes 2457608 | tf_op jit(solution)/shard_map/ppermute | solution.py:193
  27.8 27.2 %collective-permute-start.1 = (bf16[320,1280]{1,0:T(8,128)(2,1)}, bf16[320,1280]{1,0:T(8,128)(2,1)}, u32[]{:S(2)}, u32[]{:S(2)}) collective-permute-start(bf16[320,1280]{1,0:T(8,128)(2,1)} %bitcast.5), channel_id=1, source_target_pairs={{0,64},{64,0},{1,65},{65,1},{2,66},{66,2},{3,67},{67,3},{4,68},{68... | collective-permute-start | bytes 2457608 | tf_op jit(solution)/shard_map/ppermute | solution.py:193
  49.7 9.7 %collective-permute-start.3 = (bf16[64,2,1280]{2,1,0:T(2,128)(2,1)S(1)}, bf16[64,2,1280]{2,1,0:T(2,128)(2,1)S(1)}, u32[]{:S(2)}, u32[]{:S(2)}) collective-permute-start(bf16[64,2,1280]{2,1,0:T(2,128)(2,1)S(1)} %get-tuple-element.44), channel_id=1, source_target_pairs={{0,128},{128,0},{1,129},{129,1},{2,130},{130,2},{3,131},{131,3},{4... | collective-permute-start | bytes 983048 | tf_op jit(solution)/shard_map/ppermute | solution.py:189
  51.6 14.8 %collective-permute-start.2 = (bf16[64,2,1280]{2,1,0:T(2,128)(2,1)S(1)}, bf16[64,2,1280]{2,1,0:T(2,128)(2,1)S(1)}, u32[]{:S(2)}, u32[]{:S(2)}) collective-permute-start(bf16[64,2,1280]{2,1,0:T(2,128)(2,1)S(1)} %get-tuple-element.45), channel_id=1, source_target_pairs={{0,128},{128,0},{1,129},{129,1},{2,130},{130,2},{3,131},{131,3},{4... | collective-permute-start | bytes 983048 | tf_op jit(solution)/shard_map/ppermute | solution.py:189
  68.4 16.9 %collective-permute-start.4 = (bf16[64,2,1280]{2,1,0:T(2,128)(2,1)S(1)}, bf16[64,2,1280]{2,1,0:T(2,128)(2,1)S(1)}, u32[]{:S(2)}, u32[]{:S(2)}) collective-permute-start(bf16[64,2,1280]{2,1,0:T(2,128)(2,1)S(1)} %get-tuple-element.28), channel_id=1, source_target_pairs={{0,128},{128,0},{1,129},{129,1},{2,130},{130,2},{3,131},{131,3},{4... | collective-permute-start | bytes 983048 | tf_op jit(solution)/shard_map/ppermute | solution.py:189
  70.6 14.7 %collective-permute-start.5 = (bf16[64,2,1280]{2,1,0:T(2,128)(2,1)S(1)}, bf16[64,2,1280]{2,1,0:T(2,128)(2,1)S(1)}, u32[]{:S(2)}, u32[]{:S(2)}) collective-permute-start(bf16[64,2,1280]{2,1,0:T(2,128)(2,1)S(1)} %get-tuple-element.29), channel_id=1, source_target_pairs={{0,128},{128,0},{1,129},{129,1},{2,130},{130,2},{3,131},{131,3},{4... | collective-permute-start | bytes 983048 | tf_op jit(solution)/shard_map/ppermute | solution.py:189
  76.7 5.5 %copy-start.5 = (f32[640,1280]{1,0:T(8,128)}, f32[640,1280]{1,0:T(8,128)S(1)}, u32[]{:S(2)}) copy-start(f32[640,1280]{1,0:T(8,128)S(1)} %fusion.3) | copy-start | bytes 9830404
  76.8 17.6 %collective-permute-start.7 = (bf16[320,1280]{1,0:T(8,128)(2,1)S(1)}, bf16[320,1280]{1,0:T(8,128)(2,1)S(1)}, u32[]{:S(2)}, u32[]{:S(2)}) collective-permute-start(bf16[320,1280]{1,0:T(8,128)(2,1)S(1)} %slice.50), channel_id=1, source_target_pairs={{0,64},{64,0},{1,65},{65,1},{2,66},{66,2},{3,67},{67,3},{4,68},{68... | collective-permute-start | bytes 2457608 | tf_op jit(solution)/shard_map/ppermute | solution.py:193
  82.2 3.2 %copy-start.6 = (f32[640,1280]{1,0:T(8,128)}, f32[640,1280]{1,0:T(8,128)S(1)}, u32[]{:S(2)}) copy-start(f32[640,1280]{1,0:T(8,128)S(1)} %fusion.6) | copy-start | bytes 9830404
  83.3 13.8 %collective-permute-start.6 = (bf16[320,1280]{1,0:T(8,128)(2,1)}, bf16[320,1280]{1,0:T(8,128)(2,1)S(1)}, u32[]{:S(2)}, u32[]{:S(2)}) collective-permute-start(bf16[320,1280]{1,0:T(8,128)(2,1)} %slice.51), channel_id=1, source_target_pairs={{0,64},{64,0},{1,65},{65,1},{2,66},{66,2},{3,67},{67,3},{4,68},{68... | collective-permute-start | bytes 2457608 | tf_op jit(solution)/shard_map/ppermute | solution.py:193
  87.1 30.2 %all-to-all-start.1 = ((bf16[128,2,1280]{2,1,0:T(2,128)(2,1)}), bf16[128,2,1280]{2,1,0:T(2,128)(2,1)S(1)}, u32[]{:S(2)}, u32[]{:S(2)}) async-start(bf16[128,2,1280]{2,1,0:T(2,128)(2,1)} %add_convert_fusion), calls=%async_computation.1 | async-start | bytes 1310720 | tf_op jit(solution)/shard_map/all_to_all | solution.py:185
  94.4 2.7 %copy-start.7 = (f32[640,1280]{1,0:T(8,128)S(1)}, f32[640,1280]{1,0:T(8,128)}, u32[]{:S(2)}) copy-start(f32[640,1280]{1,0:T(8,128)} %copy-done.6) | copy-start | bytes 9830404
  97.1 20.2 %copy-start = (bf16[1,192,1280]{2,1,0:T(8,128)(2,1)S(1)}, bf16[1,192,1280]{2,1,0:T(8,128)(2,1)}, u32[]{:S(2)}) copy-start(bf16[1,192,1280]{2,1,0:T(8,128)(2,1)} %param.5) | copy-start | bytes 1474564
  97.1 20.2 %copy-start.1 = (bf16[1,192,1280]{2,1,0:T(8,128)(2,1)S(1)}, bf16[1,192,1280]{2,1,0:T(8,128)(2,1)}, u32[]{:S(2)}) copy-start(bf16[1,192,1280]{2,1,0:T(8,128)(2,1)} %param.6) | copy-start | bytes 1474564
  97.1 20.2 %copy-start.2 = (f32[192,64]{1,0:T(8,128)S(1)}, f32[192,64]{1,0:T(8,128)}, u32[]{:S(2)}) copy-start(f32[192,64]{1,0:T(8,128)} %get-tuple-element.23.dispatch_ref) | copy-start | bytes 147460
  97.1 20.2 %copy-start.3 = (bf16[64,1280]{1,0:T(8,128)(2,1)S(1)}, bf16[64,1280]{1,0:T(8,128)(2,1)}, u32[]{:S(2)}) copy-start(bf16[64,1280]{1,0:T(8,128)(2,1)} %get-tuple-element.25.own_ref) | copy-start | bytes 491524
  97.1 20.2 %copy-start.4 = (f32[192,64]{1,0:T(8,128)S(1)}, f32[192,64]{1,0:T(8,128)}, u32[]{:S(2)}) copy-start(f32[192,64]{1,0:T(8,128)} %get-tuple-element.24.combine_ref) | copy-start | bytes 147460
  98.2 25.3 %copy-start.9 = (bf16[1280,64]{0,1:T(8,128)(2,1)S(1)}, bf16[1280,64]{0,1:T(8,128)(2,1)}, u32[]{:S(2)}) copy-start(bf16[1280,64]{0,1:T(8,128)(2,1)} %param.7) | copy-start | bytes 491524
  119.7 13.1 %all-to-all-start.2 = ((bf16[32,2,1280]{2,1,0:T(2,128)(2,1)}), bf16[32,2,1280]{2,1,0:T(2,128)(2,1)S(1)}, u32[]{:S(2)}, u32[]{:S(2)}) async-start(bf16[32,2,1280]{2,1,0:T(2,128)(2,1)} %get-tuple-element.35), calls=%async_computation.2 | async-start | bytes 327680 | tf_op jit(solution)/shard_map/all_to_all | solution.py:185

commit v11 on v9

--- a/solution.py
+++ b/solution.py
@@ -113,11 +113,15 @@
     grad = (slope * upstream).astype(BF)
     hid_ref[...] = hid
     grad_ref[...] = grad
-    buffer[:, 0, :] = dot_first(hid, w_out_ref[...]).astype(BF)
-    buffer[:, 1, :] = dot_first(grad, w_in_ref[...]).astype(BF)
-    copy = pltpu.make_async_copy(buffer, out_ref, sems.at[1])
-    copy.start()
-    copy.wait()
+    copies = []
+    for i in range(2):
+        part = pl.ds(i * 128, 128)
+        buffer[part, 0, :] = dot_first(hid[:, i * 128 : i * 128 + 128], w_out_ref[...]).astype(BF)
+        buffer[part, 1, :] = dot_first(grad[:, i * 128 : i * 128 + 128], w_in_ref[...]).astype(BF)
+        copies.append(pltpu.make_async_copy(buffer.at[part], out_ref.at[part], sems.at[1 + i]))
+        copies[-1].start()
+    for copy in copies:
+        copy.wait()
 
 
 def logit_kernel(
@@ -177,7 +181,7 @@
     (
         pltpu.VMEM((256, 2, 1280), BF),
         pltpu.VMEM((640, 1280), BF),
-        pltpu.SemaphoreType.DMA((2,)),
+        pltpu.SemaphoreType.DMA((3,)),
     ),
     {2: HBM, 3: HBM},
     {3: 2},

time: 159 us -> 159 us (level)
  no operation moved by 1% of the time
where the time goes in v11:
time: 159 us; the launch traced here: 158 us
  waiting for transfers between devices  58.3 us (37%)
  starting transfers between devices  47.7 us (30%)
  blocking collectives  28.4 us (18%)
  Pallas kernels  10.6 us (7%)
  other arithmetic  6.06 us (4%)
  local copies, waits for them, and re-layouts  3.6 us (2%)
  matrix products  2.5 us (2%)
    all_to_all x3, waiting for transfers between devices, exchange(): return lax.all_to_all(blocks, axes, split_axis=0, concat_axis=0, tiled=True)  55.8 us
    all_to_all x3, starting transfers between devices, exchange(): return lax.all_to_all(blocks, axes, split_axis=0, concat_axis=0, tiled=True)  37.1 us
    all_to_all x2, blocking collectives, exchange(): return lax.all_to_all(blocks, axes, split_axis=0, concat_axis=0, tiled=True)  28.4 us
    ppermute x4, starting transfers between devices, swap(): return lax.ppermute(value, 'core', SWAP)  10.6 us
    pallas_call x3, Pallas kernels, call(): pl.pallas_call(kernel, out_shape=outs, in_specs=[(in_specs or {}).get(i,...  10.6 us
  transfers between devices with their start and end apart: 7, of which 5 were waited for; matrix products, arithmetic and copies ran while one was open for 7% of the time, Pallas kernels for 0%

profile of v11, /device:TPU:1, one launch (start us, length us, event | category | flops | bytes accessed | tf_op | source)
XLA Modules:
  0.0 158.0 jit_solution(13594861565664140160)
XLA Ops:
  0.6 3.6 %shard_map.84 = (f32[192,64]{1,0:T(8,128)}, f32[192,64]{1,0:T(8,128)}, bf16[64,1280]{1,0:T(8,128)(2,1)}, bf16[4,64,2,1280]{3,2,1,0:T(2,128)(2,1)}) custom-call(bf16[192,1280]{1,0:T(8,128)(2,1)} %bitcast.21, bf16[64,1280]{1,0:T(8,128)(2,1)} %bitcast.29, bf16[192,1280]{1,0:T(8,128)(2,1)} %bitcast.23), custom_call_target="tpu_custom_call" | custom-call | tf_op jit(solution)/shard_map/pallas_call | solution.py:40
  4.3 23.2 %all-to-all-start = ((bf16[256,2,1280]{2,1,0:T(2,128)(2,1)}), bf16[256,2,1280]{2,1,0:T(2,128)(2,1)S(1)}, u32[]{:S(2)}, u32[]{:S(2)}) async-start(bf16[256,2,1280]{2,1,0:T(2,128)(2,1)} %bitcast.3.spent_ref), calls=%async_computation | async-start | bytes 2621440 | tf_op jit(solution)/shard_map/all_to_all | solution.py:200
  27.5 2.9 %collective-permute-start = (bf16[320,1280]{1,0:T(8,128)(2,1)S(1)}, bf16[320,1280]{1,0:T(8,128)(2,1)S(1)}, u32[]{:S(2)}, u32[]{:S(2)}) collective-permute-start(bf16[320,1280]{1,0:T(8,128)(2,1)S(1)} %bitcast.26), channel_id=1, source_target_pairs={{0,64},{64,0},{1,65},{65,1},{2,66},{66,2},{3,67},{67,3},{4,68},{68... | collective-permute-start | bytes 2457608 | tf_op jit(solution)/shard_map/ppermute | solution.py:204
  30.4 1.9 %collective-permute-start.1 = (bf16[320,1280]{1,0:T(8,128)(2,1)}, bf16[320,1280]{1,0:T(8,128)(2,1)S(1)}, u32[]{:S(2)}, u32[]{:S(2)}) collective-permute-start(bf16[320,1280]{1,0:T(8,128)(2,1)} %bitcast.5), channel_id=1, source_target_pairs={{0,64},{64,0},{1,65},{65,1},{2,66},{66,2},{3,67},{67,3},{4,68},{68... | collective-permute-start | bytes 2457608 | tf_op jit(solution)/shard_map/ppermute | solution.py:204
  32.3 1.3 pad_maximum_fusion.w_in_ref
  33.6 1.2 collective-permute-done.1
  34.8 2.4 %pad_maximum_fusion.1.w_out_hbm = bf16[640,1280]{1,0:T(8,128)(2,1)} fusion(bf16[320,1280]{1,0:T(8,128)(2,1)S(1)} %collective-permute-done.1, bf16[320,1280]{1,0:T(8,128)(2,1)} %bitcast.5), kind=kLoop, calls=%fused_computation.9 | loop fusion | flops 3276800 | bytes 3276800 | tf_op jit(solution)/shard_map/concatenate | solution.py:214
  37.3 25.7 %all-to-all-done.blocks_ref = bf16[256,2,1280]{2,1,0:T(2,128)(2,1)S(1)} async-done(((bf16[256,2,1280]{2,1,0:T(2,128)(2,1)}), bf16[256,2,1280]{2,1,0:T(2,128)(2,1)S(1)}, u32[]{:S(2)}, u32[]{:S(2)}) %all-to-all-start) | async-done | bytes 1310752 | tf_op jit(solution)/shard_map/all_to_all | solution.py:200
  62.9 4.6 %shard_map.85 = (bf16[640,256]{1,0:T(8,128)(2,1)S(1)}, bf16[640,256]{1,0:T(8,128)(2,1)S(1)}, bf16[256,2,1280]{2,1,0:T(2,128)(2,1)}) custom-call(bf16[256,2,1280]{2,1,0:T(2,128)(2,1)S(1)} %all-to-all-done.blocks_ref, bf16[640,1280]{1,0:T(8,128)(2,1)S(1)} %pad_maximum_fusion.w_in_ref, ...), custom_call_target="tpu_custom_call", output_to_operand_aliasing={{2}: (3, {})} | custom-call | tf_op jit(solution)/shard_map/pallas_call | solution.py:40
  67.5 0.7 copy-done.3
  68.2 10.0 %all-to-all-start.1 = ((bf16[256,2,1280]{2,1,0:T(2,128)(2,1)}), bf16[256,2,1280]{2,1,0:T(2,128)(2,1)S(1)}, u32[]{:S(2)}, u32[]{:S(2)}) async-start(bf16[256,2,1280]{2,1,0:T(2,128)(2,1)} %get-tuple-element.23), calls=%async_computation.1 | async-start | bytes 2621440 | tf_op jit(solution)/shard_map/all_to_all | solution.py:200
  78.2 1.8 %fusion.10 = (bf16[256,1,1280]{2,1,0:T(2,128)(2,1)S(1)}, bf16[256,1,1280]{2,1,0:T(2,128)(2,1)S(1)}) fusion(bf16[256,2,1280]{2,1,0:T(2,128)(2,1)S(1)} %all-to-all-done.blocks_ref), kind=kLoop, calls=%fused_computation.17 | loop fusion | bytes 2621440 | tf_op jit(solution)/shard_map/slice | solution.py:221
  80.1 0.6 fusion.3
  80.7 0.1 slice.40
  80.7 3.9 %collective-permute-start.3 = (bf16[320,1280]{1,0:T(8,128)(2,1)S(1)}, bf16[320,1280]{1,0:T(8,128)(2,1)S(1)}, u32[]{:S(2)}, u32[]{:S(2)}) collective-permute-start(bf16[320,1280]{1,0:T(8,128)(2,1)S(1)} %slice.40), channel_id=1, source_target_pairs={{0,64},{64,0},{1,65},{65,1},{2,66},{66,2},{3,67},{67,3},{4,68},{68... | collective-permute-start | bytes 2457608 | tf_op jit(solution)/shard_map/ppermute | solution.py:204
  84.7 0.6 fusion.6
  85.3 0.1 slice.41
  85.4 1.9 %collective-permute-start.2 = (bf16[320,1280]{1,0:T(8,128)(2,1)S(1)}, bf16[320,1280]{1,0:T(8,128)(2,1)S(1)}, u32[]{:S(2)}, u32[]{:S(2)}) collective-permute-start(bf16[320,1280]{1,0:T(8,128)(2,1)S(1)} %slice.41), channel_id=1, source_target_pairs={{0,64},{64,0},{1,65},{65,1},{2,66},{66,2},{3,67},{67,3},{4,68},{68... | collective-permute-start | bytes 2457608 | tf_op jit(solution)/shard_map/ppermute | solution.py:204
  87.3 1.1 fusion.1
  88.4 1.2 collective-permute-done.2
  89.6 1.1 fusion.2
  90.7 22.2 %all-to-all-done.1.parts_ref = bf16[256,2,1280]{2,1,0:T(2,128)(2,1)S(1)} async-done(((bf16[256,2,1280]{2,1,0:T(2,128)(2,1)}), bf16[256,2,1280]{2,1,0:T(2,128)(2,1)S(1)}, u32[]{:S(2)}, u32[]{:S(2)}) %all-to-all-start.1) | async-done | bytes 1310752 | tf_op jit(solution)/shard_map/all_to_all | solution.py:200
  112.9 2.4 %shard_map.86 = (bf16[64,1280]{1,0:T(8,128)(2,1)S(1)}, bf16[192,64]{1,0:T(8,128)(2,1)S(1)}, bf16[32,2,1280]{2,1,0:T(2,128)(2,1)}) custom-call(bf16[192,1280]{1,0:T(8,128)(2,1)S(1)} %bitcast.22, bf16[192,1280]{1,0:T(8,128)(2,1)S(1)} %bitcast.24, f32[192,64]{1,0:T(8,128)S(1)} %copy-done.2, f32[192,64]{1,0:T(8,128)S(1)} %copy-done.6, ...), custom_call_target="tpu_custom_call" | custom-call | tf_op jit(solution)/shard_map/pallas_call | solution.py:40
  115.3 3.9 %all-to-all-start.2 = ((bf16[32,2,1280]{2,1,0:T(2,128)(2,1)}), bf16[32,2,1280]{2,1,0:T(2,128)(2,1)S(1)}, u32[]{:S(2)}, u32[]{:S(2)}) async-start(bf16[32,2,1280]{2,1,0:T(2,128)(2,1)} %get-tuple-element.27), calls=%async_computation.2 | async-start | bytes 327680 | tf_op jit(solution)/shard_map/all_to_all | solution.py:200
  119.2 0.3 fusion.11
  119.5 1.0 fusion
  120.5 7.9 %all-to-all-done.2 = bf16[32,2,1280]{2,1,0:T(2,128)(2,1)S(1)} async-done(((bf16[32,2,1280]{2,1,0:T(2,128)(2,1)}), bf16[32,2,1280]{2,1,0:T(2,128)(2,1)S(1)}, u32[]{:S(2)}, u32[]{:S(2)}) %all-to-all-start.2) | async-done | bytes 163872 | tf_op jit(solution)/shard_map/all_to_all | solution.py:200
  128.5 0.2 reduce_sum.24
  128.7 15.8 %all_to_all.25 = bf16[16,2,1280]{2,1,0:T(2,128)(2,1)S(1)} all-to-all(bf16[16,2,1280]{2,1,0:T(2,128)(2,1)S(1)} %broadcast_in_dim.22), channel_id=1, replica_groups=mesh['y_lo'=4,'core'=2,'y_hi'=2,'x'=4,'z'=8] {'y_lo','core','y_hi'}, dimensions={0} | all-to-all | bytes 163840 | tf_op jit(solution)/shard_map/all_to_all | solution.py:200
  144.5 0.1 broadcast_in_dim.23
  144.6 12.6 %all_to_all.26 = bf16[32,2,1280]{2,1,0:T(2,128)(2,1)S(1)} all-to-all(bf16[32,2,1280]{2,1,0:T(2,128)(2,1)S(1)} %broadcast_in_dim.23), channel_id=1, replica_groups=mesh['y_lo'=4,'core'=2,'y_hi'=2,'x'=4,'z'=8] {'x','z'}, dimensions={0} | all-to-all | bytes 327680 | tf_op jit(solution)/shard_map/all_to_all | solution.py:200
  157.2 0.7 reshape.17
  (21 shorter events, 0.2 us)
Async XLA Ops:
  0.6 26.9 %copy-start.7 = (bf16[1,320,1280]{2,1,0:T(8,128)(2,1)S(1)}, bf16[1,320,1280]{2,1,0:T(8,128)(2,1)}, u32[]{:S(2)}) copy-start(bf16[1,320,1280]{2,1,0:T(8,128)(2,1)} %param.8) | copy-start | bytes 2457604
  4.3 58.7 %all-to-all-start = ((bf16[256,2,1280]{2,1,0:T(2,128)(2,1)}), bf16[256,2,1280]{2,1,0:T(2,128)(2,1)S(1)}, u32[]{:S(2)}, u32[]{:S(2)}) async-start(bf16[256,2,1280]{2,1,0:T(2,128)(2,1)} %bitcast.3.spent_ref), calls=%async_computation | async-start | bytes 2621440 | tf_op jit(solution)/shard_map/all_to_all | solution.py:200
  27.5 4.8 %collective-permute-start = (bf16[320,1280]{1,0:T(8,128)(2,1)S(1)}, bf16[320,1280]{1,0:T(8,128)(2,1)S(1)}, u32[]{:S(2)}, u32[]{:S(2)}) collective-permute-start(bf16[320,1280]{1,0:T(8,128)(2,1)S(1)} %bitcast.26), channel_id=1, source_target_pairs={{0,64},{64,0},{1,65},{65,1},{2,66},{66,2},{3,67},{67,3},{4,68},{68... | collective-permute-start | bytes 2457608 | tf_op jit(solution)/shard_map/ppermute | solution.py:204
  30.4 4.4 %collective-permute-start.1 = (bf16[320,1280]{1,0:T(8,128)(2,1)}, bf16[320,1280]{1,0:T(8,128)(2,1)S(1)}, u32[]{:S(2)}, u32[]{:S(2)}) collective-permute-start(bf16[320,1280]{1,0:T(8,128)(2,1)} %bitcast.5), channel_id=1, source_target_pairs={{0,64},{64,0},{1,65},{65,1},{2,66},{66,2},{3,67},{67,3},{4,68},{68... | collective-permute-start | bytes 2457608 | tf_op jit(solution)/shard_map/ppermute | solution.py:204
  67.5 0.7 copy-start.3
  68.2 44.7 %all-to-all-start.1 = ((bf16[256,2,1280]{2,1,0:T(2,128)(2,1)}), bf16[256,2,1280]{2,1,0:T(2,128)(2,1)S(1)}, u32[]{:S(2)}, u32[]{:S(2)}) async-start(bf16[256,2,1280]{2,1,0:T(2,128)(2,1)} %get-tuple-element.23), calls=%async_computation.1 | async-start | bytes 2621440 | tf_op jit(solution)/shard_map/all_to_all | solution.py:200
  78.2 1.8 %copy-start.4 = (bf16[640,256]{1,0:T(8,128)(2,1)S(1)}, bf16[640,256]{1,0:T(8,128)(2,1)}, u32[]{:S(2)}) copy-start(bf16[640,256]{1,0:T(8,128)(2,1)} %copy-done.3) | copy-start | bytes 983044
  80.7 6.6 %collective-permute-start.3 = (bf16[320,1280]{1,0:T(8,128)(2,1)S(1)}, bf16[320,1280]{1,0:T(8,128)(2,1)S(1)}, u32[]{:S(2)}, u32[]{:S(2)}) collective-permute-start(bf16[320,1280]{1,0:T(8,128)(2,1)S(1)} %slice.40), channel_id=1, source_target_pairs={{0,64},{64,0},{1,65},{65,1},{2,66},{66,2},{3,67},{67,3},{4,68},{68... | collective-permute-start | bytes 2457608 | tf_op jit(solution)/shard_map/ppermute | solution.py:204
  85.4 4.2 %collective-permute-start.2 = (bf16[320,1280]{1,0:T(8,128)(2,1)S(1)}, bf16[320,1280]{1,0:T(8,128)(2,1)S(1)}, u32[]{:S(2)}, u32[]{:S(2)}) collective-permute-start(bf16[320,1280]{1,0:T(8,128)(2,1)S(1)} %slice.41), channel_id=1, source_target_pairs={{0,64},{64,0},{1,65},{65,1},{2,66},{66,2},{3,67},{67,3},{4,68},{68... | collective-permute-start | bytes 2457608 | tf_op jit(solution)/shard_map/ppermute | solution.py:204
  88.4 24.5 %copy-start = (bf16[1,192,1280]{2,1,0:T(8,128)(2,1)S(1)}, bf16[1,192,1280]{2,1,0:T(8,128)(2,1)}, u32[]{:S(2)}) copy-start(bf16[1,192,1280]{2,1,0:T(8,128)(2,1)} %param.5) | copy-start | bytes 1474564
  88.4 24.5 %copy-start.1 = (bf16[1,192,1280]{2,1,0:T(8,128)(2,1)S(1)}, bf16[1,192,1280]{2,1,0:T(8,128)(2,1)}, u32[]{:S(2)}) copy-start(bf16[1,192,1280]{2,1,0:T(8,128)(2,1)} %param.6) | copy-start | bytes 1474564
  88.4 24.5 %copy-start.2 = (f32[192,64]{1,0:T(8,128)S(1)}, f32[192,64]{1,0:T(8,128)}, u32[]{:S(2)}) copy-start(f32[192,64]{1,0:T(8,128)} %get-tuple-element.19.dispatch_ref) | copy-start | bytes 147460
  88.4 24.5 %copy-start.5 = (bf16[64,1280]{1,0:T(8,128)(2,1)S(1)}, bf16[64,1280]{1,0:T(8,128)(2,1)}, u32[]{:S(2)}) copy-start(bf16[64,1280]{1,0:T(8,128)(2,1)} %get-tuple-element.21.own_ref) | copy-start | bytes 491524
  88.4 24.5 %copy-start.6 = (f32[192,64]{1,0:T(8,128)S(1)}, f32[192,64]{1,0:T(8,128)}, u32[]{:S(2)}) copy-start(f32[192,64]{1,0:T(8,128)} %get-tuple-element.20.combine_ref) | copy-start | bytes 147460
  90.7 28.6 %copy-start.8 = (bf16[1280,64]{0,1:T(8,128)(2,1)S(1)}, bf16[1280,64]{0,1:T(8,128)(2,1)}, u32[]{:S(2)}) copy-start(bf16[1280,64]{0,1:T(8,128)(2,1)} %param.7) | copy-start | bytes 491524
  115.3 13.1 %all-to-all-start.2 = ((bf16[32,2,1280]{2,1,0:T(2,128)(2,1)}), bf16[32,2,1280]{2,1,0:T(2,128)(2,1)S(1)}, u32[]{:S(2)}, u32[]{:S(2)}) async-start(bf16[32,2,1280]{2,1,0:T(2,128)(2,1)} %get-tuple-element.27), calls=%async_computation.2 | async-start | bytes 327680 | tf_op jit(solution)/shard_map/all_to_all | solution.py:200

commit v12 on v11

--- a/solution.py
+++ b/solution.py
@@ -196,6 +196,13 @@
 )
 
 
+def rows_kernel(blocks_ref, out_ref):
+    out_ref[...] = blocks_ref.reshape(64, 1280)[...]
+
+
+plain_rows = on_core(rows_kernel, shape(64, 1280), VMEM)
+
+
 def exchange(blocks, axes):
     return lax.all_to_all(blocks, axes, split_axis=0, concat_axis=0, tiled=True)
 
@@ -234,7 +241,7 @@
     term = exchange(jnp.broadcast_to(term[None], (16, 2, 1280)), LINE)
     term = jnp.sum(term.astype(F32), axis=0).astype(BF)
     term = exchange(jnp.broadcast_to(term[None], (32, 2, 1280)), PLANE)
-    d_router = term.reshape(64, 1280).T
+    d_router = plain_rows(term).T
     return (d_tokens[None], d_router, d_w_in[None], d_w_out[None])
 
 

time: 159 us -> 159 us (level)
    pallas_call x3 -> x4, Pallas kernels: 10.6 us -> 11.3 us  [call(): pl.pallas_call(kernel, out_shape=outs, in_specs=[(in_specs or {}).get(i,...]
where the time goes in v12:
time: 159 us; the launch traced here: 158 us
  waiting for transfers between devices  58.3 us (37%)
  starting transfers between devices  47.7 us (30%)
  blocking collectives  28.4 us (18%)
  Pallas kernels  11.3 us (7%)
  other arithmetic  6.06 us (4%)
  local copies, waits for them, and re-layouts  2.87 us (2%)
  matrix products  2.5 us (2%)
    all_to_all x3, waiting for transfers between devices, exchange(): return lax.all_to_all(blocks, axes, split_axis=0, concat_axis=0, tiled=True)  55.8 us
    all_to_all x3, starting transfers between devices, exchange(): return lax.all_to_all(blocks, axes, split_axis=0, concat_axis=0, tiled=True)  37.1 us
    all_to_all x2, blocking collectives, exchange(): return lax.all_to_all(blocks, axes, split_axis=0, concat_axis=0, tiled=True)  28.4 us
    pallas_call x4, Pallas kernels, call(): pl.pallas_call(kernel, out_shape=outs, in_specs=[(in_specs or {}).get(i,...  11.3 us
    ppermute x4, starting transfers between devices, swap(): return lax.ppermute(value, 'core', SWAP)  10.6 us
  transfers between devices with their start and end apart: 7, of which 5 were waited for; matrix products, arithmetic and copies ran while one was open for 7% of the time, Pallas kernels for 0%

profile of v12, /device:TPU:1, one launch (start us, length us, event | category | flops | bytes accessed | tf_op | source)
XLA Modules:
  0.0 157.9 jit_solution(12794287248733443874)
XLA Ops:
  0.6 3.6 %shard_map.84 = (f32[192,64]{1,0:T(8,128)}, f32[192,64]{1,0:T(8,128)}, bf16[64,1280]{1,0:T(8,128)(2,1)}, bf16[4,64,2,1280]{3,2,1,0:T(2,128)(2,1)}) custom-call(bf16[192,1280]{1,0:T(8,128)(2,1)} %bitcast.21, bf16[64,1280]{1,0:T(8,128)(2,1)} %bitcast.29, bf16[192,1280]{1,0:T(8,128)(2,1)} %bitcast.23), custom_call_target="tpu_custom_call" | custom-call | tf_op jit(solution)/shard_map/pallas_call | solution.py:40
  4.3 23.2 %all-to-all-start = ((bf16[256,2,1280]{2,1,0:T(2,128)(2,1)}), bf16[256,2,1280]{2,1,0:T(2,128)(2,1)S(1)}, u32[]{:S(2)}, u32[]{:S(2)}) async-start(bf16[256,2,1280]{2,1,0:T(2,128)(2,1)} %bitcast.3.spent_ref), calls=%async_computation | async-start | bytes 2621440 | tf_op jit(solution)/shard_map/all_to_all | solution.py:207
  27.5 2.9 %collective-permute-start = (bf16[320,1280]{1,0:T(8,128)(2,1)S(1)}, bf16[320,1280]{1,0:T(8,128)(2,1)S(1)}, u32[]{:S(2)}, u32[]{:S(2)}) collective-permute-start(bf16[320,1280]{1,0:T(8,128)(2,1)S(1)} %bitcast.26), channel_id=1, source_target_pairs={{0,64},{64,0},{1,65},{65,1},{2,66},{66,2},{3,67},{67,3},{4,68},{68... | collective-permute-start | bytes 2457608 | tf_op jit(solution)/shard_map/ppermute | solution.py:211
  30.4 1.9 %collective-permute-start.1 = (bf16[320,1280]{1,0:T(8,128)(2,1)}, bf16[320,1280]{1,0:T(8,128)(2,1)S(1)}, u32[]{:S(2)}, u32[]{:S(2)}) collective-permute-start(bf16[320,1280]{1,0:T(8,128)(2,1)} %bitcast.5), channel_id=1, source_target_pairs={{0,64},{64,0},{1,65},{65,1},{2,66},{66,2},{3,67},{67,3},{4,68},{68... | collective-permute-start | bytes 2457608 | tf_op jit(solution)/shard_map/ppermute | solution.py:211
  32.3 1.3 pad_maximum_fusion.w_in_ref
  33.6 1.2 collective-permute-done.1
  34.8 2.4 %pad_maximum_fusion.1.w_out_hbm = bf16[640,1280]{1,0:T(8,128)(2,1)} fusion(bf16[320,1280]{1,0:T(8,128)(2,1)S(1)} %collective-permute-done.1, bf16[320,1280]{1,0:T(8,128)(2,1)} %bitcast.5), kind=kLoop, calls=%fused_computation.9 | loop fusion | flops 3276800 | bytes 3276800 | tf_op jit(solution)/shard_map/concatenate | solution.py:221
  37.3 25.7 %all-to-all-done.blocks_ref = bf16[256,2,1280]{2,1,0:T(2,128)(2,1)S(1)} async-done(((bf16[256,2,1280]{2,1,0:T(2,128)(2,1)}), bf16[256,2,1280]{2,1,0:T(2,128)(2,1)S(1)}, u32[]{:S(2)}, u32[]{:S(2)}) %all-to-all-start) | async-done | bytes 1310752 | tf_op jit(solution)/shard_map/all_to_all | solution.py:207
  62.9 4.6 %shard_map.85 = (bf16[640,256]{1,0:T(8,128)(2,1)S(1)}, bf16[640,256]{1,0:T(8,128)(2,1)S(1)}, bf16[256,2,1280]{2,1,0:T(2,128)(2,1)}) custom-call(bf16[256,2,1280]{2,1,0:T(2,128)(2,1)S(1)} %all-to-all-done.blocks_ref, bf16[640,1280]{1,0:T(8,128)(2,1)S(1)} %pad_maximum_fusion.w_in_ref, ...), custom_call_target="tpu_custom_call", output_to_operand_aliasing={{2}: (3, {})} | custom-call | tf_op jit(solution)/shard_map/pallas_call | solution.py:40
  67.5 0.7 copy-done.3
  68.2 10.0 %all-to-all-start.1 = ((bf16[256,2,1280]{2,1,0:T(2,128)(2,1)}), bf16[256,2,1280]{2,1,0:T(2,128)(2,1)S(1)}, u32[]{:S(2)}, u32[]{:S(2)}) async-start(bf16[256,2,1280]{2,1,0:T(2,128)(2,1)} %get-tuple-element.23), calls=%async_computation.1 | async-start | bytes 2621440 | tf_op jit(solution)/shard_map/all_to_all | solution.py:207
  78.2 1.8 %fusion.10 = (bf16[256,1,1280]{2,1,0:T(2,128)(2,1)S(1)}, bf16[256,1,1280]{2,1,0:T(2,128)(2,1)S(1)}) fusion(bf16[256,2,1280]{2,1,0:T(2,128)(2,1)S(1)} %all-to-all-done.blocks_ref), kind=kLoop, calls=%fused_computation.17 | loop fusion | bytes 2621440 | tf_op jit(solution)/shard_map/slice | solution.py:228
  80.1 0.6 fusion.3
  80.7 0.1 slice.40
  80.7 3.9 %collective-permute-start.3 = (bf16[320,1280]{1,0:T(8,128)(2,1)S(1)}, bf16[320,1280]{1,0:T(8,128)(2,1)S(1)}, u32[]{:S(2)}, u32[]{:S(2)}) collective-permute-start(bf16[320,1280]{1,0:T(8,128)(2,1)S(1)} %slice.40), channel_id=1, source_target_pairs={{0,64},{64,0},{1,65},{65,1},{2,66},{66,2},{3,67},{67,3},{4,68},{68... | collective-permute-start | bytes 2457608 | tf_op jit(solution)/shard_map/ppermute | solution.py:211
  84.7 0.6 fusion.6
  85.3 0.1 slice.41
  85.4 1.9 %collective-permute-start.2 = (bf16[320,1280]{1,0:T(8,128)(2,1)S(1)}, bf16[320,1280]{1,0:T(8,128)(2,1)S(1)}, u32[]{:S(2)}, u32[]{:S(2)}) collective-permute-start(bf16[320,1280]{1,0:T(8,128)(2,1)S(1)} %slice.41), channel_id=1, source_target_pairs={{0,64},{64,0},{1,65},{65,1},{2,66},{66,2},{3,67},{67,3},{4,68},{68... | collective-permute-start | bytes 2457608 | tf_op jit(solution)/shard_map/ppermute | solution.py:211
  87.3 1.1 fusion.1
  88.4 1.2 collective-permute-done.2
  89.6 1.1 fusion.2
  90.7 22.2 %all-to-all-done.1.parts_ref = bf16[256,2,1280]{2,1,0:T(2,128)(2,1)S(1)} async-done(((bf16[256,2,1280]{2,1,0:T(2,128)(2,1)}), bf16[256,2,1280]{2,1,0:T(2,128)(2,1)S(1)}, u32[]{:S(2)}, u32[]{:S(2)}) %all-to-all-start.1) | async-done | bytes 1310752 | tf_op jit(solution)/shard_map/all_to_all | solution.py:207
  112.9 2.4 %shard_map.86 = (bf16[64,1280]{1,0:T(8,128)(2,1)S(1)}, bf16[192,64]{1,0:T(8,128)(2,1)S(1)}, bf16[32,2,1280]{2,1,0:T(2,128)(2,1)}) custom-call(bf16[192,1280]{1,0:T(8,128)(2,1)S(1)} %bitcast.22, bf16[192,1280]{1,0:T(8,128)(2,1)S(1)} %bitcast.24, f32[192,64]{1,0:T(8,128)S(1)} %copy-done.2, f32[192,64]{1,0:T(8,128)S(1)} %copy-done.6, ...), custom_call_target="tpu_custom_call" | custom-call | tf_op jit(solution)/shard_map/pallas_call | solution.py:40
  115.3 3.9 %all-to-all-start.2 = ((bf16[32,2,1280]{2,1,0:T(2,128)(2,1)}), bf16[32,2,1280]{2,1,0:T(2,128)(2,1)S(1)}, u32[]{:S(2)}, u32[]{:S(2)}) async-start(bf16[32,2,1280]{2,1,0:T(2,128)(2,1)} %get-tuple-element.27), calls=%async_computation.2 | async-start | bytes 327680 | tf_op jit(solution)/shard_map/all_to_all | solution.py:207
  119.2 0.3 fusion.11
  119.5 1.0 fusion
  120.5 7.9 %all-to-all-done.2 = bf16[32,2,1280]{2,1,0:T(2,128)(2,1)S(1)} async-done(((bf16[32,2,1280]{2,1,0:T(2,128)(2,1)}), bf16[32,2,1280]{2,1,0:T(2,128)(2,1)S(1)}, u32[]{:S(2)}, u32[]{:S(2)}) %all-to-all-start.2) | async-done | bytes 163872 | tf_op jit(solution)/shard_map/all_to_all | solution.py:207
  128.5 0.2 reduce_sum.24
  128.7 15.8 %all_to_all.25 = bf16[16,2,1280]{2,1,0:T(2,128)(2,1)S(1)} all-to-all(bf16[16,2,1280]{2,1,0:T(2,128)(2,1)S(1)} %broadcast_in_dim.22), channel_id=1, replica_groups=mesh['y_lo'=4,'core'=2,'y_hi'=2,'x'=4,'z'=8] {'y_lo','core','y_hi'}, dimensions={0} | all-to-all | bytes 163840 | tf_op jit(solution)/shard_map/all_to_all | solution.py:207
  144.5 0.1 broadcast_in_dim.23
  144.6 12.6 %all_to_all.26.blocks_ref = bf16[32,2,1280]{2,1,0:T(2,128)(2,1)S(1)} all-to-all(bf16[32,2,1280]{2,1,0:T(2,128)(2,1)S(1)} %broadcast_in_dim.23), channel_id=1, replica_groups=mesh['y_lo'=4,'core'=2,'y_hi'=2,'x'=4,'z'=8] {'x','z'}, dimensions={0} | all-to-all | bytes 327680 | tf_op jit(solution)/shard_map/all_to_all | solution.py:207
  157.2 0.7 shard_map.87
  (21 shorter events, 0.2 us)
Async XLA Ops:
  0.6 26.9 %copy-start.7 = (bf16[1,320,1280]{2,1,0:T(8,128)(2,1)S(1)}, bf16[1,320,1280]{2,1,0:T(8,128)(2,1)}, u32[]{:S(2)}) copy-start(bf16[1,320,1280]{2,1,0:T(8,128)(2,1)} %param.8) | copy-start | bytes 2457604
  4.3 58.7 %all-to-all-start = ((bf16[256,2,1280]{2,1,0:T(2,128)(2,1)}), bf16[256,2,1280]{2,1,0:T(2,128)(2,1)S(1)}, u32[]{:S(2)}, u32[]{:S(2)}) async-start(bf16[256,2,1280]{2,1,0:T(2,128)(2,1)} %bitcast.3.spent_ref), calls=%async_computation | async-start | bytes 2621440 | tf_op jit(solution)/shard_map/all_to_all | solution.py:207
  27.5 4.8 %collective-permute-start = (bf16[320,1280]{1,0:T(8,128)(2,1)S(1)}, bf16[320,1280]{1,0:T(8,128)(2,1)S(1)}, u32[]{:S(2)}, u32[]{:S(2)}) collective-permute-start(bf16[320,1280]{1,0:T(8,128)(2,1)S(1)} %bitcast.26), channel_id=1, source_target_pairs={{0,64},{64,0},{1,65},{65,1},{2,66},{66,2},{3,67},{67,3},{4,68},{68... | collective-permute-start | bytes 2457608 | tf_op jit(solution)/shard_map/ppermute | solution.py:211
  30.4 4.4 %collective-permute-start.1 = (bf16[320,1280]{1,0:T(8,128)(2,1)}, bf16[320,1280]{1,0:T(8,128)(2,1)S(1)}, u32[]{:S(2)}, u32[]{:S(2)}) collective-permute-start(bf16[320,1280]{1,0:T(8,128)(2,1)} %bitcast.5), channel_id=1, source_target_pairs={{0,64},{64,0},{1,65},{65,1},{2,66},{66,2},{3,67},{67,3},{4,68},{68... | collective-permute-start | bytes 2457608 | tf_op jit(solution)/shard_map/ppermute | solution.py:211
  67.5 0.7 copy-start.3
  68.2 44.7 %all-to-all-start.1 = ((bf16[256,2,1280]{2,1,0:T(2,128)(2,1)}), bf16[256,2,1280]{2,1,0:T(2,128)(2,1)S(1)}, u32[]{:S(2)}, u32[]{:S(2)}) async-start(bf16[256,2,1280]{2,1,0:T(2,128)(2,1)} %get-tuple-element.23), calls=%async_computation.1 | async-start | bytes 2621440 | tf_op jit(solution)/shard_map/all_to_all | solution.py:207
  78.2 1.8 %copy-start.4 = (bf16[640,256]{1,0:T(8,128)(2,1)S(1)}, bf16[640,256]{1,0:T(8,128)(2,1)}, u32[]{:S(2)}) copy-start(bf16[640,256]{1,0:T(8,128)(2,1)} %copy-done.3) | copy-start | bytes 983044
  80.7 6.6 %collective-permute-start.3 = (bf16[320,1280]{1,0:T(8,128)(2,1)S(1)}, bf16[320,1280]{1,0:T(8,128)(2,1)S(1)}, u32[]{:S(2)}, u32[]{:S(2)}) collective-permute-start(bf16[320,1280]{1,0:T(8,128)(2,1)S(1)} %slice.40), channel_id=1, source_target_pairs={{0,64},{64,0},{1,65},{65,1},{2,66},{66,2},{3,67},{67,3},{4,68},{68... | collective-permute-start | bytes 2457608 | tf_op jit(solution)/shard_map/ppermute | solution.py:211
  85.4 4.2 %collective-permute-start.2 = (bf16[320,1280]{1,0:T(8,128)(2,1)S(1)}, bf16[320,1280]{1,0:T(8,128)(2,1)S(1)}, u32[]{:S(2)}, u32[]{:S(2)}) collective-permute-start(bf16[320,1280]{1,0:T(8,128)(2,1)S(1)} %slice.41), channel_id=1, source_target_pairs={{0,64},{64,0},{1,65},{65,1},{2,66},{66,2},{3,67},{67,3},{4,68},{68... | collective-permute-start | bytes 2457608 | tf_op jit(solution)/shard_map/ppermute | solution.py:211
  88.4 24.5 %copy-start = (bf16[1,192,1280]{2,1,0:T(8,128)(2,1)S(1)}, bf16[1,192,1280]{2,1,0:T(8,128)(2,1)}, u32[]{:S(2)}) copy-start(bf16[1,192,1280]{2,1,0:T(8,128)(2,1)} %param.5) | copy-start | bytes 1474564
  88.4 24.5 %copy-start.1 = (bf16[1,192,1280]{2,1,0:T(8,128)(2,1)S(1)}, bf16[1,192,1280]{2,1,0:T(8,128)(2,1)}, u32[]{:S(2)}) copy-start(bf16[1,192,1280]{2,1,0:T(8,128)(2,1)} %param.6) | copy-start | bytes 1474564
  88.4 24.5 %copy-start.2 = (f32[192,64]{1,0:T(8,128)S(1)}, f32[192,64]{1,0:T(8,128)}, u32[]{:S(2)}) copy-start(f32[192,64]{1,0:T(8,128)} %get-tuple-element.19.dispatch_ref) | copy-start | bytes 147460
  88.4 24.5 %copy-start.5 = (bf16[64,1280]{1,0:T(8,128)(2,1)S(1)}, bf16[64,1280]{1,0:T(8,128)(2,1)}, u32[]{:S(2)}) copy-start(bf16[64,1280]{1,0:T(8,128)(2,1)} %get-tuple-element.21.own_ref) | copy-start | bytes 491524
  88.4 24.5 %copy-start.6 = (f32[192,64]{1,0:T(8,128)S(1)}, f32[192,64]{1,0:T(8,128)}, u32[]{:S(2)}) copy-start(f32[192,64]{1,0:T(8,128)} %get-tuple-element.20.combine_ref) | copy-start | bytes 147460
  90.7 28.6 %copy-start.8 = (bf16[1280,64]{0,1:T(8,128)(2,1)S(1)}, bf16[1280,64]{0,1:T(8,128)(2,1)}, u32[]{:S(2)}) copy-start(bf16[1280,64]{0,1:T(8,128)(2,1)} %param.7) | copy-start | bytes 491524
  115.3 13.1 %all-to-all-start.2 = ((bf16[32,2,1280]{2,1,0:T(2,128)(2,1)}), bf16[32,2,1280]{2,1,0:T(2,128)(2,1)S(1)}, u32[]{:S(2)}, u32[]{:S(2)}) async-start(bf16[32,2,1280]{2,1,0:T(2,128)(2,1)} %get-tuple-element.27), calls=%async_computation.2 | async-start | bytes 327680 | tf_op jit(solution)/shard_map/all_to_all | solution.py:207
